TPU v7x, 32 devices: a whole 2x2x4 slice. The times are simulated.
32 devices in a mesh: groups: 2 (over x), example: 8 (over z, y), cls: 2 (over core).
Axes of the slice: x: 2, y: 2, z: 4, core: 2. Of those that a mesh axis runs over, the one named last changes fastest.
Arguments:
- features: bfloat16 [2048, 4096], P(('groups', 'example'), 'cls'), parts along dimension 0
- weights: float32 [8192, 8192], P(('groups', 'cls'), 'example'), parts along dimension 0
- labels: int32 [2048], P(('groups', 'example')), parts along dimension 0, may hold values from 0 to 8191
- counts: int32 [16], P(('groups', 'example')), parts along dimension 0, may hold values from 16 to 128, as said below
- active: int32 [2], P('groups'), parts along dimension 0, may hold values from 4096 to 8192
Outputs:
- moved: float32 [8192, 8192], P(('groups', 'cls'), 'example'), parts along dimension 0
- losses: float32 [2048], P(('groups', 'example')), parts along dimension 0
There are 2 independent parts, one for each index of `groups`. A program takes and returns all parts, laid end to end along the dimension named above; each array names one. Nothing has to cross between parts.
Inputs may be any that keep to these rules, and one draw needn't show every extreme that they name: `counts`: each block has at least 16 valid slots; some block is full in every draw.
All inputs are finite; a program needn't handle non-finite values.
Results may differ from a plain program's by a relative error of at most 0.006.
Values may be sent and summed in bfloat16 or wider, within the bound.
No kernel may reach another device: no remote copies, remote signals or barrier semaphores. Data moves between devices by JAX's collectives and lax.ppermute only.
A program may use at most 128 MiB of HBM per device.

v0:
```python
import functools

import jax
import jax.numpy as jnp
from jax import lax
from jax.experimental import pallas as pl
from jax.experimental.pallas import tpu as pltpu
from jax.sharding import PartitionSpec as P

ITERS = 2
NEGATIVE = -1e30
LEARNING_RATE = 2e-05
DAMPING_SHARE = 0.1
EPSILON = 1e-06

F32 = jnp.float32
BF16 = jnp.bfloat16
VMEM = pl.BlockSpec(memory_space=pltpu.VMEM)
SMEM = pl.BlockSpec(memory_space=pltpu.SMEM)
HBM = pl.BlockSpec(memory_space=pltpu.HBM)
ANY = pl.BlockSpec(memory_space=pl.ANY)
STEP = 64
LANES = 128


def params(mib=10):
    return pltpu.CompilerParams(vmem_limit_bytes=mib << 20)


def cost(flops=0, nbytes=0):
    return pl.CostEstimate(flops=int(flops), bytes_accessed=int(nbytes), transcendentals=0)


def swap(x, axis, n, offset):
    return lax.ppermute(x, axis, [(i, i ^ offset) for i in range(n)])


def gray(v):
    return v ^ (v >> 1)


def block_of(place, slot, n):
    if n != 8:
        return lax.rem(place + n - slot, n)
    z, y = place // 2, place % 2
    return gray((gray(z) + 4 - slot // 2) & 3) * 2 + (y ^ (slot % 2))


def token_kernel(*refs):
    refs[-1][...] = jnp.zeros_like(refs[-1])


def token(values):
    return pl.pallas_call(
        token_kernel,
        out_shape=jax.ShapeDtypeStruct((8, LANES), F32),
        in_specs=[ANY] * len(values),
        out_specs=VMEM,
        compiler_params=params(),
        cost_estimate=cost(1, 1),
        name="token",
    )(*values)


def relay_kernel(*refs):
    refs[-1][...] = refs[0][...]


def relay(block, tokens):
    return pl.pallas_call(
        relay_kernel,
        out_shape=pltpu.VMEM(block.shape, block.dtype),
        in_specs=[VMEM] + [ANY] * len(tokens),
        out_specs=VMEM,
        compiler_params=params(),
        cost_estimate=cost(1, 1),
        name="relay",
    )(block, *tokens)


def gather_blocks(x, n, early):
    if n != 8:
        ring = [(i, (i + 1) % n) for i in range(n)]
        slots = [x]
        for _ in range(n - 1):
            slots.append(lax.ppermute(slots[-1], "example", ring))
        return [[slot] for slot in slots], [()] * (n // 2), early, [slot for slot in slots[3::2]]
    hops = ((0, 1), (1, 3), (3, 2), (2, 0))
    ring = [(a * 2 + y, b * 2 + y) for a, b in hops for y in range(2)]
    tie = lax.optimization_barrier
    rows = x.shape[0] // 2
    held, ready = [x[:rows], x[rows:]], [x[:rows], x[rows:]]
    slots = []
    for step in range(3):
        across, later = [], []
        for k in range(2):
            later.append(lax.ppermute(held[k], "example", ring))
            across.append(swap(ready[k], "example", n, 1))
        slots += [held, list(across)]
        if step == 0:
            later = [tie((up, early))[0] for up in later]
        if step < 2:
            ready = [tie((up, over))[0] for up, over in zip(later, across)]
        held = later
    seen = token((held[0],))
    seen = token((across[0], seen))
    seen = token((held[1], seen))
    seen = token((across[1], seen))
    lower = relay(across[1], (seen,))
    upper = relay(held[0], (seen,))
    last = [swap(upper, "example", n, 1), lax.ppermute(lower, "example", ring)]
    slots += [held, last]
    return slots, [tuple(slots[2 * k + 2]) for k in range(3)] + [()], early, [slots[3][1], upper]


def prepare_kernel(tile, chunks, w_ref, x_ref, labels_ref, counts_ref, active_ref, *refs):
    kept = refs[:chunks]
    low_ref, target_ref, norm_ref, block_ref, label_ref, sems = refs[chunks:]
    first = [
        pltpu.make_async_copy(x_ref, block_ref, sems.at[0]),
        pltpu.make_async_copy(labels_ref, label_ref, sems.at[1]),
    ]
    copies = []
    for k in range(w_ref.shape[0] // tile):
        at = slice(k * tile, (k + 1) * tile)
        for c, keep in enumerate(kept):
            own = slice(c * keep.shape[1], (c + 1) * keep.shape[1])
            copy = pltpu.make_async_copy(
                w_ref.at[at, own], keep.at[at, :], sems.at[2 + len(copies)]
            )
            copies.append((copy, keep, at, own))
    for copy in first + [c[0] for c in copies]:
        copy.start()
    for copy in first:
        copy.wait()
    rows = x_ref.shape[0]
    slot = lax.broadcasted_iota(jnp.int32, (1, rows), 1)
    target = jnp.where(slot < counts_ref[0], label_ref[...] % active_ref[0], -1)
    target_ref[...] = target.astype(F32)
    squares = (block_ref[...] * block_ref[...]).astype(F32)
    norm = jnp.sum(squares, axis=1, keepdims=True)
    norm_ref[...] = jnp.broadcast_to(norm, (rows, LANES)).T[0:1, :]
    for copy, keep, at, own in copies:
        copy.wait()
        low_ref[at, own] = keep[at, :].astype(BF16)


def prepare(weights, features, labels, counts, active, columns):
    rows = features.shape[0]
    feature_count, classes = weights.shape
    tile, chunks = 256, classes // columns
    line = jax.ShapeDtypeStruct((1, rows), F32)
    *kept, low, target, norm = pl.pallas_call(
        functools.partial(prepare_kernel, tile, chunks),
        out_shape=(pltpu.VMEM((feature_count, columns), F32),) * chunks
        + (pltpu.VMEM((feature_count, classes), BF16), line, line),
        in_specs=[HBM, HBM, HBM, SMEM, SMEM],
        out_specs=(VMEM,) * (chunks + 3),
        scratch_shapes=[
            pltpu.VMEM(features.shape, BF16),
            pltpu.VMEM((1, rows), jnp.int32),
            pltpu.SemaphoreType.DMA((2 + chunks * (feature_count // tile),)),
        ],
        compiler_params=params(),
        cost_estimate=cost(1, 1),
        name="prepare",
    )(
        weights,
        pltpu.with_memory_space_constraint(features, pltpu.HBM),
        pltpu.with_memory_space_constraint(labels.reshape(1, rows), pltpu.HBM),
        counts,
        active,
    )
    return kept, low, target, norm


def arriving_kernel(count, pieces, start, *refs):
    parts, w_ref = refs[:count], refs[count]
    plain_ref, outs = refs[-pieces - 1], refs[-pieces:]
    done = start
    for part in parts:
        plain_ref[done : done + part.shape[0], :] = part[...]
        done += part.shape[0]
    columns = 256
    for first in range(0, w_ref.shape[1], columns):
        own = slice(first, first + columns)
        found = jnp.dot(plain_ref[start:done, :], w_ref[:, own], preferred_element_type=F32)
        for k, out in enumerate(outs):
            out[:, own] = found[k * out.shape[0] : (k + 1) * out.shape[0], :]


def arriving_logits(parts, w_low, plain, start, all_rows, piece, tokens):
    rows = sum(p.shape[0] for p in parts)
    pieces, count = rows // piece, len(parts)
    plain, *logits = pl.pallas_call(
        functools.partial(arriving_kernel, count, pieces, start),
        out_shape=(pltpu.VMEM((all_rows, w_low.shape[0]), BF16),)
        + (jax.ShapeDtypeStruct((piece, w_low.shape[1]), F32),) * pieces,
        in_specs=[VMEM] * (count + 1 + len(plain)) + [ANY] * len(tokens),
        out_specs=(VMEM,) * (pieces + 1),
        input_output_aliases={count + 1: 0} if plain else {},
        compiler_params=params(),
        cost_estimate=cost(1, 1),
        name="arriving_logits",
    )(*parts, w_low, *plain, *tokens)
    return plain, logits


def turn_kernel(start, rows, plain_ref, *refs):
    turned_ref, squares_ref = refs[-2:]
    at = slice(start, start + rows)
    block = plain_ref[at, :].T
    turned_ref[:, at] = block
    squares_ref[:, at] = block * block


def turn(plain, start, rows, buffers):
    buffer = pltpu.VMEM(plain.shape[::-1], BF16)
    return pl.pallas_call(
        functools.partial(turn_kernel, start, rows),
        out_shape=(buffer, buffer),
        in_specs=[VMEM] * (1 + len(buffers)),
        out_specs=(VMEM, VMEM),
        input_output_aliases={1: 0, 2: 1} if buffers else {},
        compiler_params=params(),
        cost_estimate=cost(1, 1),
        name="turn",
    )(plain, *buffers)


def lane_pack(columns, rows):
    lane = lax.broadcasted_iota(jnp.int32, (rows, LANES), 1)
    packed = jnp.zeros((rows, LANES), F32)
    for k, column in enumerate(columns):
        packed = jnp.where(lane == k, column, packed)
    return packed


def put_stats(packed, place, shape):
    lines = packed.T
    line = jnp.concatenate([lines[k : k + 1, :] for k in range(3)], axis=1)
    here = lax.broadcasted_iota(jnp.int32, shape, 0) == place
    return jnp.where(here, line, 0.0)


def first_stats_kernel(slot, pieces, earlier, last, tokens, *refs):
    own, other = refs[:pieces], refs[pieces : 2 * pieces]
    active_ref, refs = refs[2 * pieces], refs[2 * pieces + 1 :]
    lines = refs[: 3 * last]
    older = refs[3 * last : 3 * last + earlier]
    outs = refs[3 * last + earlier + tokens :]
    e_ref, stats_ref, pack_ref = outs[0], outs[1], outs[-1]
    rows, classes = e_ref.shape
    active, place = active_ref[0], lax.axis_index("example")
    class_start = place * classes
    index = class_start + lax.broadcasted_iota(jnp.int32, (1, classes), 1)
    live = index < active
    for k in range(rows // STEP):
        at = slice(k * STEP, (k + 1) * STEP)
        piece, first = k * STEP // own[0].shape[0], k * STEP % own[0].shape[0]
        here = slice(first, first + STEP)
        logits = jnp.where(live, own[piece][here, :] + other[piece][here, :], NEGATIVE)
        peak = jnp.max(logits, axis=1, keepdims=True)
        e = jnp.exp(logits - peak)
        e_ref[at, :] = e
        total = jnp.sum(e, axis=1, keepdims=True)
        square = jnp.sum(e * e, axis=1, keepdims=True)
        pack_ref[at, :] = lane_pack((peak, total, square), STEP)
    shape = stats_ref.shape
    n = shape[0]
    stats = older[0][...] if earlier else jnp.zeros(shape, F32)
    for k in range(rows // LANES):
        stats += put_stats(pack_ref[k * LANES : (k + 1) * LANES, :], block_of(place, slot + k, n), shape)
    stats_ref[...] = stats
    if last:
        copies_ref = outs[2]
        target, norm = lines[0][...], lines[1][...] + lines[2][...]
        wide = [jnp.broadcast_to(line, (shape[0], LANES)) for line in (target, norm)]
        full = jnp.concatenate([stats] + wide, axis=1)
        copies_ref[...] = jnp.broadcast_to(full[None], copies_ref.shape)


def first_stats(own, other, active, slot, n, earlier, side, tokens):
    pieces, classes = len(own), own[0].shape[1]
    rows = pieces * own[0].shape[0]
    last = len(side) > 0
    shapes = [jax.ShapeDtypeStruct((rows, classes), F32), jax.ShapeDtypeStruct((n, 3 * LANES), F32)]
    if last:
        shapes.append(jax.ShapeDtypeStruct((n, n, 5 * LANES), F32))
    extra = list(side) + list(earlier)
    return pl.pallas_call(
        functools.partial(
            first_stats_kernel, slot, pieces, len(earlier), last, len(tokens)
        ),
        out_shape=tuple(shapes),
        in_specs=[VMEM] * (2 * pieces) + [SMEM] + [VMEM] * len(extra) + [ANY] * len(tokens),
        out_specs=(VMEM,) * len(shapes),
        scratch_shapes=[pltpu.VMEM((rows, LANES), F32)],
        compiler_params=params(),
        cost_estimate=cost(1, 1),
        name="first_stats",
    )(*own, *other, active, *extra, *tokens)


def combine(own_ref, all_ref):
    n = all_ref.shape[0]
    part = lambda d, k: all_ref[d, :, k * LANES : (k + 1) * LANES]
    peaks = [part(d, 0) for d in range(n)]
    peak = functools.reduce(jnp.maximum, peaks)
    scales = [jnp.exp(p - peak) for p in peaks]
    total = sum(part(d, 1) * scales[d] for d in range(n))
    own_scale = jnp.exp(own_ref[:, 0:LANES] - peak)
    return part, peak, scales, total, own_scale


def to_slots(value, line_ref, place):
    n = value.shape[0]
    line_ref[...] = value
    return jnp.concatenate([line_ref[pl.ds(block_of(place, j, n), 1), :] for j in range(n)], axis=0)


def to_columns(lines):
    stacked = jnp.concatenate(lines, axis=0)
    rest = jnp.zeros((LANES - stacked.shape[0], LANES), F32)
    return jnp.concatenate([stacked, rest], axis=0).T


def first_weights_kernel(entries, parts, own_ref, all_ref, *refs):
    e_refs = refs[:parts]
    residual_ref, fisher_ref, damping_ref, target_ref, column_ref, line_ref = refs[parts:]
    n = all_ref.shape[0]
    classes = residual_ref.shape[1]
    place = lax.axis_index("example")
    class_start = place * classes
    part, peak, scales, total, own_scale = combine(own_ref, all_ref)
    square = sum(part(d, 2) * (scales[d] * scales[d]) for d in range(n))
    inverse = 1.0 / total
    spread = 1.0 - square * inverse * inverse
    target = jnp.concatenate([all_ref[d, 0:1, 3 * LANES : 4 * LANES] for d in range(n)], axis=0)
    norm = jnp.concatenate([all_ref[d, 0:1, 4 * LANES : 5 * LANES] for d in range(n)], axis=0)
    valid = (target >= 0.0).astype(F32)
    share = valid / jnp.sum(valid)
    fisher_sum = jnp.sum(norm * share * spread)
    damping_ref[...] = jnp.full(
        damping_ref.shape, DAMPING_SHARE * fisher_sum / entries + EPSILON, F32
    )
    factor = to_slots(own_scale * inverse, line_ref, place)
    share = to_slots(share, line_ref, place)
    target = to_slots(target, line_ref, place)
    target_ref[...] = target
    column_ref[...] = to_columns([factor, share, target])
    index = class_start + lax.broadcasted_iota(jnp.int32, (1, classes), 1)
    done = 0
    for e_ref in e_refs:
        for k in range(e_ref.shape[0] // LANES):
            j = done + k

            def step(i, _, j=j, k=k, e_ref=e_ref):
                start = i * STEP
                at = pl.ds(j * LANES + start, STEP)
                column = column_ref[pl.ds(start, STEP), :]
                e = e_ref[pl.ds(k * LANES + start, STEP), :]
                probability = e * column[:, j : j + 1]
                hit = index == column[:, 2 * n + j : 2 * n + j + 1].astype(jnp.int32)
                part = column[:, n + j : n + j + 1]
                residual_ref[at, :] = (part * (probability - hit.astype(F32))).astype(BF16)
                fisher_ref[at, :] = (part * probability * (1.0 - probability)).astype(BF16)
                return 0

            for i in range(LANES // STEP):
                step(i, 0)
        done += e_ref.shape[0] // LANES


def first_weights(own, every, e_parts, entries):
    n = own.shape[0]
    classes = e_parts[0].shape[1]
    weight = pltpu.VMEM((n * LANES, classes), BF16)
    return pl.pallas_call(
        functools.partial(first_weights_kernel, float(entries), len(e_parts)),
        out_shape=(
            weight,
            weight,
            jax.ShapeDtypeStruct((8, LANES), F32),
            jax.ShapeDtypeStruct((n, LANES), F32),
        ),
        in_specs=[VMEM] * (2 + len(e_parts)),
        out_specs=(VMEM,) * 4,
        scratch_shapes=[pltpu.VMEM((LANES, LANES), F32), pltpu.VMEM((n, LANES), F32)],
        compiler_params=params(),
        cost_estimate=cost(0, 8 * n * LANES * classes),
        name="first_weights",
    )(own, every, *e_parts)


def update_kernel(start, tile, turned_ref, squares_ref, w_ref, residual_ref, fisher_ref,
                  damping_ref, moved_ref, inverse_ref, low_ref):
    features, columns = moved_ref.shape
    damping = damping_ref[0:1, 0:1]
    own = slice(start, start + columns)
    for k in range(features // tile):
        at = slice(k * tile, (k + 1) * tile)
        fisher = jnp.dot(squares_ref[at, :], fisher_ref[:, own], preferred_element_type=F32)
        gradient = jnp.dot(turned_ref[at, :], residual_ref[:, own], preferred_element_type=F32)
        inverse = 1.0 / (fisher + damping)
        change = gradient * inverse
        inverse_ref[at, :] = inverse
        low_ref[at, :] = (w_ref[at, :] - LEARNING_RATE * change).astype(BF16)
        moved_ref[at, :] = -change


def update(turned, squares, weights, residual, fisher_weight, damping, start):
    features, rows = turned.shape
    columns = weights.shape[1]
    return pl.pallas_call(
        functools.partial(update_kernel, start, 512),
        out_shape=(
            pltpu.VMEM((features, columns), F32),
            pltpu.VMEM((features, columns), F32),
            pltpu.VMEM((features, columns), BF16),
        ),
        in_specs=[VMEM] * 6,
        out_specs=(VMEM, VMEM, VMEM),
        input_output_aliases={2: 0},
        compiler_params=params(),
        cost_estimate=cost(4 * rows * features * columns),
        name="update",
    )(turned, squares, weights, residual, fisher_weight, damping)


def next_logits_kernel(start, tile, plain_ref, low_ref, out_ref):
    for first in range(0, out_ref.shape[0], tile):
        out_ref[first : first + tile, :] = jnp.dot(
            plain_ref[start + first : start + first + tile, :],
            low_ref[...],
            preferred_element_type=F32,
        )


def next_logits(plain, low, start, rows):
    features, columns = low.shape
    return pl.pallas_call(
        functools.partial(next_logits_kernel, start, min(512, rows)),
        out_shape=jax.ShapeDtypeStruct((rows, columns), F32),
        in_specs=[VMEM, VMEM],
        out_specs=VMEM,
        compiler_params=params(),
        cost_estimate=cost(2 * rows * features * columns),
        name="next_logits",
    )(plain, low)


def last_stats_kernel(slot, last, pieces, offsets, earlier, *refs):
    own, other = refs[:pieces], refs[pieces : 2 * pieces]
    target_ref, active_ref = refs[2 * pieces : 2 * pieces + 2]
    older = refs[2 * pieces + 2 : 2 * pieces + 2 + earlier]
    outs = refs[2 * pieces + 2 + earlier :]
    e_ref, stats_ref, pack_ref, column_ref = outs[0], outs[1], outs[-2], outs[-1]
    rows, classes = e_ref.shape
    active, place = active_ref[0], lax.axis_index("example")
    class_start = place * classes
    n = stats_ref.shape[0]
    column_ref[...] = to_columns([target_ref[...]])
    index = class_start + lax.broadcasted_iota(jnp.int32, (1, classes), 1)
    live = index < active
    for k in range(rows // LANES):
        def step(i, _, k=k):
            start = i * STEP

            def rows_of(base):
                return pl.ds(base + k * LANES + start, STEP)

            logits = jnp.concatenate(
                [a[rows_of(o), :] + b[rows_of(o), :] for a, b, o in zip(own, other, offsets)],
                axis=1,
            )
            column = column_ref[pl.ds(start, STEP), slot + k : slot + k + 1]
            hit = index == column.astype(jnp.int32)
            label = jnp.sum(jnp.where(hit, logits, 0.0), axis=1, keepdims=True)
            logits = jnp.where(live, logits, NEGATIVE)
            peak = jnp.max(logits, axis=1, keepdims=True)
            e = jnp.exp(logits - peak)
            e_ref[rows_of(0), :] = e
            total = jnp.sum(e, axis=1, keepdims=True)
            pack_ref[rows_of(0), :] = lane_pack((peak, total, label), STEP)
            return 0

        for i in range(LANES // STEP):
            step(i, 0)
    shape = stats_ref.shape
    n = shape[0]
    stats = older[0][...] if earlier else jnp.zeros(shape, F32)
    for k in range(rows // LANES):
        stats += put_stats(pack_ref[k * LANES : (k + 1) * LANES, :], block_of(place, slot + k, n), shape)
    stats_ref[...] = stats
    if last:
        outs[2][...] = jnp.broadcast_to(stats[None], outs[2].shape)


def last_stats(own, other, offsets, target, active, slot, rows, n, earlier):
    classes = sum(c.shape[1] for c in own)
    last = slot + rows // LANES == n
    shapes = [
        jax.ShapeDtypeStruct((rows, classes), F32),
        jax.ShapeDtypeStruct((n, 3 * LANES), F32),
    ]
    if last:
        shapes.append(jax.ShapeDtypeStruct((n, n, 3 * LANES), F32))
    return pl.pallas_call(
        functools.partial(
            last_stats_kernel, slot, last, len(own), tuple(offsets), len(earlier)
        ),
        out_shape=tuple(shapes),
        in_specs=[VMEM] * (2 * len(own) + 1) + [SMEM] + [VMEM] * len(earlier),
        out_specs=(VMEM,) * len(shapes),
        scratch_shapes=[pltpu.VMEM((rows, LANES), F32), pltpu.VMEM((LANES, LANES), F32)],
        compiler_params=params(),
        cost_estimate=cost(0, 24 * rows * classes),
        name="last_stats",
    )(*own, *other, target, active, *earlier)


def finish_kernel(chunks, e_parts, tile, own_ref, all_ref, target_ref, turned_ref, *refs):
    e_refs = refs[:e_parts]
    refs = refs[e_parts:]
    moved_refs, inverse_refs = refs[:chunks], refs[chunks : 2 * chunks]
    out_ref, loss_ref, residual_ref, column_ref, line_ref, held_ref, sems = refs[2 * chunks :]
    n = all_ref.shape[0]
    classes = residual_ref.shape[1]
    place = lax.axis_index("example")
    class_start = place * classes
    part, peak, scales, total, own_scale = combine(own_ref, all_ref)
    label = sum(part(d, 2) for d in range(n))
    target = target_ref[...]
    valid = (target >= 0.0).astype(F32)
    share = valid / jnp.sum(valid)
    losses = to_slots(peak + jnp.log(total) - label, line_ref, place)
    loss_ref[...] = (valid * losses)[0:1, :]
    factor = to_slots(own_scale / total, line_ref, place)
    column_ref[...] = to_columns([factor, share, target])
    index = class_start + lax.broadcasted_iota(jnp.int32, (1, classes), 1)
    done = 0
    for e_ref in e_refs:
        for k in range(e_ref.shape[0] // LANES):
            j = done + k

            def step(i, _, j=j, k=k, e_ref=e_ref):
                start = i * STEP
                at = pl.ds(j * LANES + start, STEP)
                column = column_ref[pl.ds(start, STEP), :]
                e = e_ref[pl.ds(k * LANES + start, STEP), :]
                probability = e * column[:, j : j + 1]
                hit = index == column[:, 2 * n + j : 2 * n + j + 1].astype(jnp.int32)
                part = column[:, n + j : n + j + 1]
                residual_ref[at, :] = (part * (probability - hit.astype(F32))).astype(BF16)
                return 0

            for i in range(LANES // STEP):
                step(i, 0)
        done += e_ref.shape[0] // LANES

    copies = []
    for k in range(out_ref.shape[0] // tile):
        at = slice(k * tile, (k + 1) * tile)
        done = 0
        for moved_ref, inverse_ref in zip(moved_refs, inverse_refs):
            own = slice(done, done + moved_ref.shape[1])
            gradient = jnp.dot(
                turned_ref[at, :], residual_ref[:, own], preferred_element_type=F32
            )
            held_ref[k, :, own] = moved_ref[at, :] - gradient * inverse_ref[at, :]
            done += moved_ref.shape[1]
        copies.append(pltpu.make_async_copy(held_ref.at[k], out_ref.at[at, :], sems.at[k]))
        copies[-1].start()
    for copy in copies:
        copy.wait()


def finish(own, every, target, e_parts, turned, moved, inverse):
    n = own.shape[0]
    features, all_rows = turned.shape
    classes = e_parts[0].shape[1]
    tile = 512
    return pl.pallas_call(
        functools.partial(finish_kernel, len(moved), len(e_parts), tile),
        out_shape=(
            jax.ShapeDtypeStruct((features, classes), F32),
            jax.ShapeDtypeStruct((1, LANES), F32),
        ),
        in_specs=[VMEM] * (4 + len(e_parts) + 2 * len(moved)),
        out_specs=(ANY, VMEM),
        scratch_shapes=[
            pltpu.VMEM((all_rows, classes), BF16),
            pltpu.VMEM((LANES, LANES), F32),
            pltpu.VMEM((n, LANES), F32),
            pltpu.VMEM((features // tile, tile, classes), F32),
            pltpu.SemaphoreType.DMA((features // tile,)),
        ],
        compiler_params=params(16),
        cost_estimate=cost(2 * all_rows * features * classes),
        name="finish",
    )(own, every, target, turned, *e_parts, *moved, *inverse)


def exchange(copies):
    return lax.all_to_all(copies, "example", 0, 0)


def body(n, n_cls, features, weights, labels, counts, active):
    rows = features.shape[0]
    all_rows = rows * n
    feature_count, classes = weights.shape
    entries = feature_count * n_cls * classes * n
    weights = pltpu.with_memory_space_constraint(weights, pltpu.HBM)
    columns = min(512, classes)
    kept, w_low, target, norm = prepare(weights, features, labels, counts, active, columns)
    slots, waits, w_low, gates = gather_blocks(features, n, w_low)
    side = (target, norm, swap(norm, "cls", n_cls, 1))

    groups = [[k, k + 1] for k in range(0, n - 2, 2)] + [[n - 2], [n - 1]]
    count = len(groups)
    behind = max(count - 3, 0)
    plain, buffers, logits, e_parts, stats = (), (), [], [], []

    def statistics(g, tokens):
        last = g == count - 1
        other = [swap(piece, "cls", n_cls, 1) for piece in logits[g]]
        e, found, *copies = first_stats(
            logits[g], other, active, groups[g][0], n, tuple(stats[-1:]),
            side if last else (), tokens,
        )
        e_parts.append(e)
        stats.append(found)
        return copies

    for g in range(count):
        if g == count - 1 and behind:
            logits[behind:], slots[-1] = lax.optimization_barrier((logits[behind:], slots[-1]))
        parts = [part for slot in groups[g] for part in slots[slot]]
        tokens = tuple(stats[-1:]) + tuple(buffers[:1]) + tuple(waits[g] if g < n // 2 else ())
        start = groups[g][0] * rows
        piece = STEP if g < behind else LANES
        block, found = arriving_logits(parts, w_low, plain, start, all_rows, piece, tokens)
        plain = (block,)
        logits.append(found)
        if g < n // 2 - 1:
            buffers = turn(block, start, 2 * rows, buffers)
        if g < behind:
            logits[g], _ = lax.optimization_barrier((logits[g], gates[g]))
        if g < behind - 1:
            statistics(g, ())
    plain = plain[0]
    turned, squares = turn(plain, (n - 2) * rows, 2 * rows, buffers)
    for g in range(max(behind - 1, 0), count):
        copies = statistics(g, (logits[-1][0], turned))
    own_stats = stats[-1]
    every = exchange(copies[0])
    residual, fisher_weight, damping, target = first_weights(own_stats, every, e_parts, entries)

    moved, inverse, own, other = [], [], [], []
    for start in range(0, classes, columns):
        a, b, low = update(
            turned, squares, kept[start // columns], residual, fisher_weight, damping, start
        )
        moved.append(a)
        inverse.append(b)
        if start + columns < classes:
            own.append(next_logits(plain, low, 0, all_rows))
            other.append(swap(own[-1], "cls", n_cls, 1))
    half = n // 2
    late = [next_logits(plain, low, first * rows, half * rows) for first in (0, half)]
    late_other = [swap(c, "cls", n_cls, 1) for c in late]
    e_parts, earlier = [], ()
    for first, c, d in zip((0, half), late, late_other):
        offsets = [first * rows] * len(own) + [0]
        e, own_stats, *copies = last_stats(
            own + [c], other + [d], offsets, target, active, first, half * rows, n, earlier
        )
        e_parts.append(e)
        earlier = (own_stats,)
    every = exchange(copies[0])
    out, losses = finish(own_stats, every, target, e_parts, turned, moved, inverse)
    return out, losses.reshape(rows)


def solution(mesh):
    return jax.shard_map(
        functools.partial(body, mesh.shape["example"], mesh.shape["cls"]),
        mesh=mesh,
        in_specs=(
            P(("groups", "example"), "cls"),
            P(("groups", "cls"), "example"),
            P(("groups", "example")),
            P(("groups", "example")),
            P("groups"),
        ),
        out_specs=(P(("groups", "cls"), "example"), P(("groups", "example"))),
        check_vma=False,
    )
```

profile of v0, /device:TPU:0, one launch (start us, length us, event | category | flops | bytes accessed | tf_op | source)
XLA Modules:
  0.0 112.1 jit_solution(173732120134741694)
XLA Ops:
  0.6 1.1 fusion
  1.7 3.1 %collective-permute-start = (bf16[64,2048]{1,0:T(8,128)(2,1)S(1)}, bf16[64,2048]{1,0:T(8,128)(2,1)S(1)}, u32[]{:S(2)}, u32[]{:S(2)}) collective-permute-start(bf16[64,2048]{1,0:T(8,128)(2,1)S(1)} %get-tuple-element.157.refs_0_), channel_id=1, source_target_pairs={{0,4},{2,6},{4,12},{6,14},{12,8},{14,10},{8,0},{10,2},{1,5},{3,7},... | collective-permute-start | bytes 786440 | tf_op jit(solution)/shard_map/ppermute | solution.py:97
  4.8 1.5 %collective-permute-start.4 = (bf16[64,2048]{1,0:T(8,128)(2,1)S(1)}, bf16[64,2048]{1,0:T(8,128)(2,1)S(1)}, u32[]{:S(2)}, u32[]{:S(2)}) collective-permute-start(bf16[64,2048]{1,0:T(8,128)(2,1)S(1)} %get-tuple-element.157.refs_0_), channel_id=1, source_target_pairs={{0,2},{2,0},{4,6},{6,4},{8,10},{10,8},{12,14},{14,12},{1,3},{3,1},... | collective-permute-start | bytes 786440 | tf_op jit(solution)/shard_map/ppermute | solution.py:35
  6.3 2.6 %collective-permute-start.2 = (bf16[64,2048]{1,0:T(8,128)(2,1)S(1)}, bf16[64,2048]{1,0:T(8,128)(2,1)S(1)}, u32[]{:S(2)}, u32[]{:S(2)}) collective-permute-start(bf16[64,2048]{1,0:T(8,128)(2,1)S(1)} %get-tuple-element.156.refs_1_), channel_id=1, source_target_pairs={{0,4},{2,6},{4,12},{6,14},{12,8},{14,10},{8,0},{10,2},{1,5},{3,7},... | collective-permute-start | bytes 786440 | tf_op jit(solution)/shard_map/ppermute | solution.py:97
  8.9 0.5 collective-permute-start.7
  10.7 3.7 %prepare.1 = (f32[2048,512]{1,0:T(8,128)S(1)}, f32[2048,512]{1,0:T(8,128)S(1)}, bf16[2048,1024]{1,0:T(8,128)(2,1)S(1)}, f32[1,128]{1,0:T(1,128)S(1)}, f32[1,128]{1,0:T(1,128)S(1)}) custom-call(f32[2048,1024]{1,0:T(8,128)} %w_ref.1, bf16[128,2048]{1,0:T(8,128)(2,1)} %x_ref.1, s32[1,128]{1,0:T(1,128)} %bitcast.2, s32[1]{0:T(128)S(6)} %copy.31.counts_ref, ...), custom_call_target="tpu_custom_call" | custom-call | flops 1 | bytes 1 | tf_op jit(solution)/shard_map/prepare/pallas_call | solution.py:153
  14.5 1.6 %collective-permute-start.5 = (bf16[64,2048]{1,0:T(8,128)(2,1)S(1)}, bf16[64,2048]{1,0:T(8,128)(2,1)S(1)}, u32[]{:S(2)}, u32[]{:S(2)}) collective-permute-start(bf16[64,2048]{1,0:T(8,128)(2,1)S(1)} %collective-permute-done.refs_5_.refs_0_), channel_id=1, source_target_pairs={{0,2},{2,0},{4,6},{6,4},{8,10},{10,8},{12,14},{14,12},{1,3},{3,1},... | collective-permute-start | bytes 786440 | tf_op jit(solution)/shard_map/ppermute | solution.py:35
  16.0 2.1 %collective-permute-start.1 = (bf16[64,2048]{1,0:T(8,128)(2,1)S(1)}, bf16[64,2048]{1,0:T(8,128)(2,1)S(1)}, u32[]{:S(2)}, u32[]{:S(2)}) collective-permute-start(bf16[64,2048]{1,0:T(8,128)(2,1)S(1)} %collective-permute-done.refs_5_.refs_0_), channel_id=1, source_target_pairs={{0,4},{2,6},{4,12},{6,14},{12,8},{14,10},{8,0},{10,2},{1,5},{3,7},... | collective-permute-start | bytes 786440 | tf_op jit(solution)/shard_map/ppermute | solution.py:97
  18.1 1.6 %collective-permute-start.3 = (bf16[64,2048]{1,0:T(8,128)(2,1)S(1)}, bf16[64,2048]{1,0:T(8,128)(2,1)S(1)}, u32[]{:S(2)}, u32[]{:S(2)}) collective-permute-start(bf16[64,2048]{1,0:T(8,128)(2,1)S(1)} %collective-permute-done.2.refs_6_.refs_1_), channel_id=1, source_target_pairs={{0,4},{2,6},{4,12},{6,14},{12,8},{14,10},{8,0},{10,2},{1,5},{3,7},... | collective-permute-start | bytes 786440 | tf_op jit(solution)/shard_map/ppermute | solution.py:97
  19.7 1.5 %collective-permute-start.8 = (bf16[64,2048]{1,0:T(8,128)(2,1)S(1)}, bf16[64,2048]{1,0:T(8,128)(2,1)S(1)}, u32[]{:S(2)}, u32[]{:S(2)}) collective-permute-start(bf16[64,2048]{1,0:T(8,128)(2,1)S(1)} %collective-permute-done.2.refs_6_.refs_1_), channel_id=1, source_target_pairs={{0,2},{2,0},{4,6},{6,4},{8,10},{10,8},{12,14},{14,12},{1,3},{3,1},... | collective-permute-start | bytes 786440 | tf_op jit(solution)/shard_map/ppermute | solution.py:35
  21.2 4.0 %collective-permute-done.5.refs_2_ = bf16[64,2048]{1,0:T(8,128)(2,1)S(1)} collective-permute-done((bf16[64,2048]{1,0:T(8,128)(2,1)S(1)}, bf16[64,2048]{1,0:T(8,128)(2,1)S(1)}, u32[]{:S(2)}, u32[]{:S(2)}) %collective-permute-start.5) | collective-permute-done | bytes 262176 | tf_op jit(solution)/shard_map/ppermute | solution.py:35
  25.2 0.9 collective-permute-done.1.refs_8_.refs_0_
  26.2 0.6 collective-permute-start.6
  26.8 2.6 %collective-permute-start.14 = (bf16[64,2048]{1,0:T(8,128)(2,1)S(1)}, bf16[64,2048]{1,0:T(8,128)(2,1)S(1)}, u32[]{:S(2)}, u32[]{:S(2)}) collective-permute-start(bf16[64,2048]{1,0:T(8,128)(2,1)S(1)} %collective-permute-done.1.refs_8_.refs_0_), channel_id=1, source_target_pairs={{0,4},{2,6},{4,12},{6,14},{12,8},{14,10},{8,0},{10,2},{1,5},{3,7},... | collective-permute-start | bytes 786440 | tf_op jit(solution)/shard_map/ppermute | solution.py:97
  29.4 1.8 %collective-permute-done.3.refs_9_.refs_1_ = bf16[64,2048]{1,0:T(8,128)(2,1)S(1)} collective-permute-done((bf16[64,2048]{1,0:T(8,128)(2,1)S(1)}, bf16[64,2048]{1,0:T(8,128)(2,1)S(1)}, u32[]{:S(2)}, u32[]{:S(2)}) %collective-permute-start.3) | collective-permute-done | bytes 262176 | tf_op jit(solution)/shard_map/ppermute | solution.py:97
  31.4 1.3 %arriving_logits.5 = (bf16[1024,2048]{1,0:T(8,128)(2,1)S(1)}, f32[64,1024]{1,0:T(8,128)S(1)}, f32[64,1024]{1,0:T(8,128)S(1)}, f32[64,1024]{1,0:T(8,128)S(1)}, f32[64,1024]{1,0:T(8,128)S(1)}) custom-call(bf16[64,2048]{1,0:T(8,128)(2,1)S(1)} %get-tuple-element.157.refs_0_, bf16[64,2048]{1,0:T(8,128)(2,1)S(1)} %get-tuple-element.156.refs_1_, ...), custom_call_target="tpu_custom_call" | custom-call | flops 1 | bytes 1 | tf_op jit(solution)/shard_map/arriving_logits/pallas_call | solution.py:195
  32.7 1.7 %collective-permute-start.9 = (bf16[64,2048]{1,0:T(8,128)(2,1)S(1)}, bf16[64,2048]{1,0:T(8,128)(2,1)S(1)}, u32[]{:S(2)}, u32[]{:S(2)}) collective-permute-start(bf16[64,2048]{1,0:T(8,128)(2,1)S(1)} %collective-permute-done.3.refs_9_.refs_1_), channel_id=1, source_target_pairs={{0,2},{2,0},{4,6},{6,4},{8,10},{10,8},{12,14},{14,12},{1,3},{3,1},... | collective-permute-start | bytes 786440 | tf_op jit(solution)/shard_map/ppermute | solution.py:35
  34.3 2.1 %collective-permute-done.6.refs_2_.refs_0_ = bf16[64,2048]{1,0:T(8,128)(2,1)S(1)} collective-permute-done((bf16[64,2048]{1,0:T(8,128)(2,1)S(1)}, bf16[64,2048]{1,0:T(8,128)(2,1)S(1)}, u32[]{:S(2)}, u32[]{:S(2)}) %collective-permute-start.6) | collective-permute-done | bytes 262176 | tf_op jit(solution)/shard_map/ppermute | solution.py:35
  36.5 0.4 collective-permute-done.14.refs_8_.refs_0_
  37.0 3.4 %collective-permute-done.15.refs_9_.refs_1_.refs_0_ = bf16[64,2048]{1,0:T(8,128)(2,1)S(1)} collective-permute-done((bf16[64,2048]{1,0:T(8,128)(2,1)S(1)}, bf16[64,2048]{1,0:T(8,128)(2,1)S(1)}, u32[]{:S(2)}, u32[]{:S(2)}) %collective-permute-start.15) | collective-permute-done | bytes 262176 | tf_op jit(solution)/shard_map/ppermute | solution.py:97
  41.0 2.6 %collective-permute-start.17 = (bf16[64,2048]{1,0:T(8,128)(2,1)S(1)}, bf16[64,2048]{1,0:T(8,128)(2,1)S(1)}, u32[]{:S(2)}, u32[]{:S(2)}) collective-permute-start(bf16[64,2048]{1,0:T(8,128)(2,1)S(1)} %relay.3), channel_id=1, source_target_pairs={{0,4},{2,6},{4,12},{6,14},{12,8},{14,10},{8,0},{10,2},{1,5},{3,7},... | collective-permute-start | bytes 786440 | tf_op jit(solution)/shard_map/ppermute | solution.py:111
  43.7 1.6 %collective-permute-start.16 = (bf16[64,2048]{1,0:T(8,128)(2,1)S(1)}, bf16[64,2048]{1,0:T(8,128)(2,1)S(1)}, u32[]{:S(2)}, u32[]{:S(2)}) collective-permute-start(bf16[64,2048]{1,0:T(8,128)(2,1)S(1)} %relay.2), channel_id=1, source_target_pairs={{0,2},{2,0},{4,6},{6,4},{8,10},{10,8},{12,14},{14,12},{1,3},{3,1},... | collective-permute-start | bytes 786440 | tf_op jit(solution)/shard_map/ppermute | solution.py:35
  45.3 0.5 first_stats.5
  45.8 1.3 %arriving_logits.6 = (bf16[1024,2048]{1,0:T(8,128)(2,1)S(1)}, f32[64,1024]{1,0:T(8,128)S(1)}, f32[64,1024]{1,0:T(8,128)S(1)}, f32[64,1024]{1,0:T(8,128)S(1)}, f32[64,1024]{1,0:T(8,128)S(1)}) custom-call(bf16[64,2048]{1,0:T(8,128)(2,1)S(1)} %collective-permute-done.refs_5_.refs_0_, ...), custom_call_target="tpu_custom_call", output_to_operand_aliasing={{0}: (5, {})} | custom-call | flops 1 | bytes 1 | tf_op jit(solution)/shard_map/arriving_logits/pallas_call | solution.py:195
  47.2 0.5 collective-permute-start.24
  48.1 1.3 %arriving_logits.7 = (bf16[1024,2048]{1,0:T(8,128)(2,1)S(1)}, f32[128,1024]{1,0:T(8,128)S(1)}, f32[128,1024]{1,0:T(8,128)S(1)}) custom-call(bf16[64,2048]{1,0:T(8,128)(2,1)S(1)} %collective-permute-done.1.refs_8_.refs_0_, bf16[64,2048]{1,0:T(8,128)(2,1)S(1)} %collective-permute-done.3.refs_9_.refs_1_, ...), custom_call_target="tpu_custom_call", output_to_operand_aliasing={{0}: (5, {})} | custom-call | flops 1 | bytes 1 | tf_op jit(solution)/shard_map/arriving_logits/pallas_call | solution.py:195
  49.8 0.7 arriving_logits.8
  50.5 0.5 collective-permute-start.20
  51.1 0.4 collective-permute-start.22
  51.5 0.8 arriving_logits.9
  52.4 0.4 collective-permute-start.26
  52.9 2.3 %collective-permute-done.26.refs_7_ = f32[64,1024]{1,0:T(8,128)S(1)} collective-permute-done((f32[64,1024]{1,0:T(8,128)S(1)}, f32[64,1024]{1,0:T(8,128)S(1)}, u32[]{:S(2)}, u32[]{:S(2)}) %collective-permute-start.26) | collective-permute-done | bytes 262176 | tf_op jit(solution)/shard_map/ppermute | solution.py:35
  55.2 0.4 collective-permute-start.19
  55.9 0.5 first_stats.6
  56.4 0.5 first_stats.7
  57.6 13.1 %all_to_all.10.all_ref = f32[8,8,640]{2,1,0:T(8,128)S(1)} all-to-all(f32[8,8,640]{2,1,0:T(8,128)S(1)} %get-tuple-element.132), channel_id=1, replica_groups=mesh['groups'=2,'example'=8,'cls'=2] {'example'}, dimensions={0} | all-to-all | bytes 327680 | tf_op jit(solution)/shard_map/all_to_all | solution.py:606
  70.7 1.6 %first_weights.1 = (bf16[1024,1024]{1,0:T(8,128)(2,1)S(1)}, bf16[1024,1024]{1,0:T(8,128)(2,1)S(1)}, f32[8,128]{1,0:T(8,128)S(1)}, f32[8,128]{1,0:T(8,128)S(1)}) custom-call(f32[8,384]{1,0:T(8,128)S(1)} %get-tuple-element.131.own_ref, f32[8,8,640]{2,1,0:T(8,128)S(1)} %all_to_all.10.all_ref, f32[256,1024]{1,0:T(8,128)S(1)} %get-tuple-element.133.refs_0_, ...), custom_call_target="tpu_custom_call" | custom-call | bytes 8388608 | tf_op jit(solution)/shard_map/first_weights/pallas_call | solution.py:379
  72.3 6.2 %update.2 = (f32[2048,512]{1,0:T(8,128)S(1)}, f32[2048,512]{1,0:T(8,128)S(1)}, bf16[2048,512]{1,0:T(8,128)(2,1)S(1)}) custom-call(bf16[2048,1024]{1,0:T(8,128)(2,1)S(1)} %get-tuple-element.111.refs_11_.refs_7_.refs_5_.refs_8_.turned_ref, bf16[2048,1024]{1,0:T(8,128)(2,1)S(1)} %get-tuple-element.112.squares_ref, ...), custom_call_target="tpu_custom_call", output_to_operand_aliasing={{0}: (2, {})} | custom-call | flops 4294967296 | tf_op jit(solution)/shard_map/update/pallas_call | solution.py:415
  78.5 2.3 %next_logits.3.refs_0_ = f32[1024,512]{1,0:T(8,128)S(1)} custom-call(bf16[1024,2048]{1,0:T(8,128)(2,1)S(1)} %get-tuple-element.109.plain_ref, bf16[2048,512]{1,0:T(8,128)(2,1)S(1)} %get-tuple-element.141.low_ref), custom_call_target="tpu_custom_call" | custom-call | flops 2147483648 | tf_op jit(solution)/shard_map/next_logits/pallas_call | solution.py:442
  80.9 6.4 %update.3 = (f32[2048,512]{1,0:T(8,128)S(1)}, f32[2048,512]{1,0:T(8,128)S(1)}, bf16[2048,512]{1,0:T(8,128)(2,1)S(1)}) custom-call(bf16[2048,1024]{1,0:T(8,128)(2,1)S(1)} %get-tuple-element.111.refs_11_.refs_7_.refs_5_.refs_8_.turned_ref, bf16[2048,1024]{1,0:T(8,128)(2,1)S(1)} %get-tuple-element.112.squares_ref, ...), custom_call_target="tpu_custom_call", output_to_operand_aliasing={{0}: (2, {})} | custom-call | flops 4294967296 | tf_op jit(solution)/shard_map/update/pallas_call | solution.py:415
  87.4 1.2 %next_logits.5.refs_1_ = f32[512,512]{1,0:T(8,128)S(1)} custom-call(bf16[1024,2048]{1,0:T(8,128)(2,1)S(1)} %get-tuple-element.109.plain_ref, bf16[2048,512]{1,0:T(8,128)(2,1)S(1)} %get-tuple-element.143.low_ref), custom_call_target="tpu_custom_call" | custom-call | flops 1073741824 | tf_op jit(solution)/shard_map/next_logits/pallas_call | solution.py:442
  88.6 0.6 collective-permute-start.29
  89.2 1.2 %next_logits.4.refs_1_ = f32[512,512]{1,0:T(8,128)S(1)} custom-call(bf16[1024,2048]{1,0:T(8,128)(2,1)S(1)} %get-tuple-element.109.plain_ref, bf16[2048,512]{1,0:T(8,128)(2,1)S(1)} %get-tuple-element.143.low_ref), custom_call_target="tpu_custom_call" | custom-call | flops 1073741824 | tf_op jit(solution)/shard_map/next_logits/pallas_call | solution.py:442
  90.5 1.0 collective-permute-done.29.refs_3_
  91.5 1.7 %last_stats.2 = (f32[512,1024]{1,0:T(8,128)S(1)}, f32[8,384]{1,0:T(8,128)S(1)}) custom-call(f32[1024,512]{1,0:T(8,128)S(1)} %next_logits.3.refs_0_, f32[512,512]{1,0:T(8,128)S(1)} %next_logits.5.refs_1_, f32[1024,512]{1,0:T(8,128)S(1)} %collective-permute-done.27.refs_2_, f32[512,512]{1,0:T(8,128)S(1)} %collective-permute-done.29.refs_3_, ...), custom_call_target="tpu_custom_call" | custom-call | bytes 12582912 | tf_op jit(solution)/shard_map/last_stats/pallas_call | solution.py:509
  93.2 1.7 %last_stats.3 = (f32[512,1024]{1,0:T(8,128)S(1)}, f32[8,384]{1,0:T(8,128)S(1)}, f32[8,8,384]{2,1,0:T(8,128)S(1)}) custom-call(f32[1024,512]{1,0:T(8,128)S(1)} %next_logits.3.refs_0_, f32[512,512]{1,0:T(8,128)S(1)} %next_logits.4.refs_1_, f32[1024,512]{1,0:T(8,128)S(1)} %collective-permute-done.27.refs_2_, f32[512,512]{1,0:T(8,128)S(1)} %collective-permute-done.28.refs_3_, ...), custom_call_target="tpu_custom_call" | custom-call | bytes 12582912 | tf_op jit(solution)/shard_map/last_stats/pallas_call | solution.py:509
  94.9 9.9 %all_to_all.11.all_ref = f32[8,8,384]{2,1,0:T(8,128)S(1)} all-to-all(f32[8,8,384]{2,1,0:T(8,128)S(1)} %get-tuple-element.147), channel_id=1, replica_groups=mesh['groups'=2,'example'=8,'cls'=2] {'example'}, dimensions={0} | all-to-all | bytes 196608 | tf_op jit(solution)/shard_map/all_to_all | solution.py:606
  104.7 7.1 %finish.1 = (f32[2048,1024]{1,0:T(8,128)}, f32[1,128]{1,0:T(1,128)}) custom-call(f32[8,384]{1,0:T(8,128)S(1)} %get-tuple-element.146.own_ref, f32[8,8,384]{2,1,0:T(8,128)S(1)} %all_to_all.11.all_ref, f32[8,128]{1,0:T(8,128)S(1)} %get-tuple-element.144.refs_4_.target_ref, ...), custom_call_target="tpu_custom_call" | custom-call | flops 4294967296 | tf_op jit(solution)/shard_map/finish/pallas_call | solution.py:584
  (45 shorter events, 3.2 us)
Async XLA Ops:
  1.7 12.7 %collective-permute-start = (bf16[64,2048]{1,0:T(8,128)(2,1)S(1)}, bf16[64,2048]{1,0:T(8,128)(2,1)S(1)}, u32[]{:S(2)}, u32[]{:S(2)}) collective-permute-start(bf16[64,2048]{1,0:T(8,128)(2,1)S(1)} %get-tuple-element.157.refs_0_), channel_id=1, source_target_pairs={{0,4},{2,6},{4,12},{6,14},{12,8},{14,10},{8,0},{10,2},{1,5},{3,7},... | collective-permute-start | bytes 786440 | tf_op jit(solution)/shard_map/ppermute | solution.py:97
  4.8 9.7 %collective-permute-start.4 = (bf16[64,2048]{1,0:T(8,128)(2,1)S(1)}, bf16[64,2048]{1,0:T(8,128)(2,1)S(1)}, u32[]{:S(2)}, u32[]{:S(2)}) collective-permute-start(bf16[64,2048]{1,0:T(8,128)(2,1)S(1)} %get-tuple-element.157.refs_0_), channel_id=1, source_target_pairs={{0,2},{2,0},{4,6},{6,4},{8,10},{10,8},{12,14},{14,12},{1,3},{3,1},... | collective-permute-start | bytes 786440 | tf_op jit(solution)/shard_map/ppermute | solution.py:35
  6.3 11.8 %collective-permute-start.2 = (bf16[64,2048]{1,0:T(8,128)(2,1)S(1)}, bf16[64,2048]{1,0:T(8,128)(2,1)S(1)}, u32[]{:S(2)}, u32[]{:S(2)}) collective-permute-start(bf16[64,2048]{1,0:T(8,128)(2,1)S(1)} %get-tuple-element.156.refs_1_), channel_id=1, source_target_pairs={{0,4},{2,6},{4,12},{6,14},{12,8},{14,10},{8,0},{10,2},{1,5},{3,7},... | collective-permute-start | bytes 786440 | tf_op jit(solution)/shard_map/ppermute | solution.py:97
  8.9 10.8 %collective-permute-start.7 = (bf16[64,2048]{1,0:T(8,128)(2,1)S(1)}, bf16[64,2048]{1,0:T(8,128)(2,1)S(1)}, u32[]{:S(2)}, u32[]{:S(2)}) collective-permute-start(bf16[64,2048]{1,0:T(8,128)(2,1)S(1)} %get-tuple-element.156.refs_1_), channel_id=1, source_target_pairs={{0,2},{2,0},{4,6},{6,4},{8,10},{10,8},{12,14},{14,12},{1,3},{3,1},... | collective-permute-start | bytes 786440 | tf_op jit(solution)/shard_map/ppermute | solution.py:35
  14.5 10.8 %collective-permute-start.5 = (bf16[64,2048]{1,0:T(8,128)(2,1)S(1)}, bf16[64,2048]{1,0:T(8,128)(2,1)S(1)}, u32[]{:S(2)}, u32[]{:S(2)}) collective-permute-start(bf16[64,2048]{1,0:T(8,128)(2,1)S(1)} %collective-permute-done.refs_5_.refs_0_), channel_id=1, source_target_pairs={{0,2},{2,0},{4,6},{6,4},{8,10},{10,8},{12,14},{14,12},{1,3},{3,1},... | collective-permute-start | bytes 786440 | tf_op jit(solution)/shard_map/ppermute | solution.py:35
  16.0 10.1 %collective-permute-start.1 = (bf16[64,2048]{1,0:T(8,128)(2,1)S(1)}, bf16[64,2048]{1,0:T(8,128)(2,1)S(1)}, u32[]{:S(2)}, u32[]{:S(2)}) collective-permute-start(bf16[64,2048]{1,0:T(8,128)(2,1)S(1)} %collective-permute-done.refs_5_.refs_0_), channel_id=1, source_target_pairs={{0,4},{2,6},{4,12},{6,14},{12,8},{14,10},{8,0},{10,2},{1,5},{3,7},... | collective-permute-start | bytes 786440 | tf_op jit(solution)/shard_map/ppermute | solution.py:97
  18.1 13.0 %collective-permute-start.3 = (bf16[64,2048]{1,0:T(8,128)(2,1)S(1)}, bf16[64,2048]{1,0:T(8,128)(2,1)S(1)}, u32[]{:S(2)}, u32[]{:S(2)}) collective-permute-start(bf16[64,2048]{1,0:T(8,128)(2,1)S(1)} %collective-permute-done.2.refs_6_.refs_1_), channel_id=1, source_target_pairs={{0,4},{2,6},{4,12},{6,14},{12,8},{14,10},{8,0},{10,2},{1,5},{3,7},... | collective-permute-start | bytes 786440 | tf_op jit(solution)/shard_map/ppermute | solution.py:97
  19.7 13.0 %collective-permute-start.8 = (bf16[64,2048]{1,0:T(8,128)(2,1)S(1)}, bf16[64,2048]{1,0:T(8,128)(2,1)S(1)}, u32[]{:S(2)}, u32[]{:S(2)}) collective-permute-start(bf16[64,2048]{1,0:T(8,128)(2,1)S(1)} %collective-permute-done.2.refs_6_.refs_1_), channel_id=1, source_target_pairs={{0,2},{2,0},{4,6},{6,4},{8,10},{10,8},{12,14},{14,12},{1,3},{3,1},... | collective-permute-start | bytes 786440 | tf_op jit(solution)/shard_map/ppermute | solution.py:35
  26.2 10.3 %collective-permute-start.6 = (bf16[64,2048]{1,0:T(8,128)(2,1)S(1)}, bf16[64,2048]{1,0:T(8,128)(2,1)S(1)}, u32[]{:S(2)}, u32[]{:S(2)}) collective-permute-start(bf16[64,2048]{1,0:T(8,128)(2,1)S(1)} %collective-permute-done.1.refs_8_.refs_0_), channel_id=1, source_target_pairs={{0,2},{2,0},{4,6},{6,4},{8,10},{10,8},{12,14},{14,12},{1,3},{3,1},... | collective-permute-start | bytes 786440 | tf_op jit(solution)/shard_map/ppermute | solution.py:35
  26.8 10.1 %collective-permute-start.14 = (bf16[64,2048]{1,0:T(8,128)(2,1)S(1)}, bf16[64,2048]{1,0:T(8,128)(2,1)S(1)}, u32[]{:S(2)}, u32[]{:S(2)}) collective-permute-start(bf16[64,2048]{1,0:T(8,128)(2,1)S(1)} %collective-permute-done.1.refs_8_.refs_0_), channel_id=1, source_target_pairs={{0,4},{2,6},{4,12},{6,14},{12,8},{14,10},{8,0},{10,2},{1,5},{3,7},... | collective-permute-start | bytes 786440 | tf_op jit(solution)/shard_map/ppermute | solution.py:97
  31.2 9.3 %collective-permute-start.15 = (bf16[64,2048]{1,0:T(8,128)(2,1)S(1)}, bf16[64,2048]{1,0:T(8,128)(2,1)S(1)}, u32[]{:S(2)}, u32[]{:S(2)}) collective-permute-start(bf16[64,2048]{1,0:T(8,128)(2,1)S(1)} %collective-permute-done.3.refs_9_.refs_1_), channel_id=1, source_target_pairs={{0,4},{2,6},{4,12},{6,14},{12,8},{14,10},{8,0},{10,2},{1,5},{3,7},... | collective-permute-start | bytes 786440 | tf_op jit(solution)/shard_map/ppermute | solution.py:97
  32.7 8.0 %collective-permute-start.9 = (bf16[64,2048]{1,0:T(8,128)(2,1)S(1)}, bf16[64,2048]{1,0:T(8,128)(2,1)S(1)}, u32[]{:S(2)}, u32[]{:S(2)}) collective-permute-start(bf16[64,2048]{1,0:T(8,128)(2,1)S(1)} %collective-permute-done.3.refs_9_.refs_1_), channel_id=1, source_target_pairs={{0,2},{2,0},{4,6},{6,4},{8,10},{10,8},{12,14},{14,12},{1,3},{3,1},... | collective-permute-start | bytes 786440 | tf_op jit(solution)/shard_map/ppermute | solution.py:35
  34.3 9.4 %collective-permute-start.10 = (f32[64,1024]{1,0:T(8,128)S(1)}, f32[64,1024]{1,0:T(8,128)S(1)}, u32[]{:S(2)}, u32[]{:S(2)}) collective-permute-start(f32[64,1024]{1,0:T(8,128)S(1)} %get-tuple-element.91.refs_0_), channel_id=1, source_target_pairs={{0,1},{1,0},{2,3},{3,2},{4,5},{5,4},{6,7},{7,6},{8,9},{9,8},{10,11... | collective-permute-start | bytes 786440 | tf_op jit(solution)/shard_map/ppermute | solution.py:35
  36.5 8.8 %collective-permute-start.11 = (f32[64,1024]{1,0:T(8,128)S(1)}, f32[64,1024]{1,0:T(8,128)S(1)}, u32[]{:S(2)}, u32[]{:S(2)}) collective-permute-start(f32[64,1024]{1,0:T(8,128)S(1)} %get-tuple-element.92.refs_1_), channel_id=1, source_target_pairs={{0,1},{1,0},{2,3},{3,2},{4,5},{5,4},{6,7},{7,6},{8,9},{9,8},{10,11... | collective-permute-start | bytes 786440 | tf_op jit(solution)/shard_map/ppermute | solution.py:35
  36.9 8.4 %collective-permute-start.12 = (f32[64,1024]{1,0:T(8,128)S(1)}, f32[64,1024]{1,0:T(8,128)S(1)}, u32[]{:S(2)}, u32[]{:S(2)}) collective-permute-start(f32[64,1024]{1,0:T(8,128)S(1)} %get-tuple-element.93.refs_2_), channel_id=1, source_target_pairs={{0,1},{1,0},{2,3},{3,2},{4,5},{5,4},{6,7},{7,6},{8,9},{9,8},{10,11... | collective-permute-start | bytes 786440 | tf_op jit(solution)/shard_map/ppermute | solution.py:35
  40.4 4.9 %collective-permute-start.13 = (f32[64,1024]{1,0:T(8,128)S(1)}, f32[64,1024]{1,0:T(8,128)S(1)}, u32[]{:S(2)}, u32[]{:S(2)}) collective-permute-start(f32[64,1024]{1,0:T(8,128)S(1)} %get-tuple-element.94.refs_3_), channel_id=1, source_target_pairs={{0,1},{1,0},{2,3},{3,2},{4,5},{5,4},{6,7},{7,6},{8,9},{9,8},{10,11... | collective-permute-start | bytes 786440 | tf_op jit(solution)/shard_map/ppermute | solution.py:35
  41.0 9.5 %collective-permute-start.17 = (bf16[64,2048]{1,0:T(8,128)(2,1)S(1)}, bf16[64,2048]{1,0:T(8,128)(2,1)S(1)}, u32[]{:S(2)}, u32[]{:S(2)}) collective-permute-start(bf16[64,2048]{1,0:T(8,128)(2,1)S(1)} %relay.3), channel_id=1, source_target_pairs={{0,4},{2,6},{4,12},{6,14},{12,8},{14,10},{8,0},{10,2},{1,5},{3,7},... | collective-permute-start | bytes 786440 | tf_op jit(solution)/shard_map/ppermute | solution.py:111
  43.7 6.8 %collective-permute-start.16 = (bf16[64,2048]{1,0:T(8,128)(2,1)S(1)}, bf16[64,2048]{1,0:T(8,128)(2,1)S(1)}, u32[]{:S(2)}, u32[]{:S(2)}) collective-permute-start(bf16[64,2048]{1,0:T(8,128)(2,1)S(1)} %relay.2), channel_id=1, source_target_pairs={{0,2},{2,0},{4,6},{6,4},{8,10},{10,8},{12,14},{14,12},{1,3},{3,1},... | collective-permute-start | bytes 786440 | tf_op jit(solution)/shard_map/ppermute | solution.py:35
  47.1 4.0 %collective-permute-start.23 = (f32[64,1024]{1,0:T(8,128)S(1)}, f32[64,1024]{1,0:T(8,128)S(1)}, u32[]{:S(2)}, u32[]{:S(2)}) collective-permute-start(f32[64,1024]{1,0:T(8,128)S(1)} %get-tuple-element.124.refs_0_), channel_id=1, source_target_pairs={{0,1},{1,0},{2,3},{3,2},{4,5},{5,4},{6,7},{7,6},{8,9},{9,8},{10,11... | collective-permute-start | bytes 786440 | tf_op jit(solution)/shard_map/ppermute | solution.py:35
  47.2 5.1 %collective-permute-start.24 = (f32[64,1024]{1,0:T(8,128)S(1)}, f32[64,1024]{1,0:T(8,128)S(1)}, u32[]{:S(2)}, u32[]{:S(2)}) collective-permute-start(f32[64,1024]{1,0:T(8,128)S(1)} %get-tuple-element.125.refs_1_), channel_id=1, source_target_pairs={{0,1},{1,0},{2,3},{3,2},{4,5},{5,4},{6,7},{7,6},{8,9},{9,8},{10,11... | collective-permute-start | bytes 786440 | tf_op jit(solution)/shard_map/ppermute | solution.py:35
  47.7 4.8 %collective-permute-start.25 = (f32[64,1024]{1,0:T(8,128)S(1)}, f32[64,1024]{1,0:T(8,128)S(1)}, u32[]{:S(2)}, u32[]{:S(2)}) collective-permute-start(f32[64,1024]{1,0:T(8,128)S(1)} %get-tuple-element.126.refs_2_), channel_id=1, source_target_pairs={{0,1},{1,0},{2,3},{3,2},{4,5},{5,4},{6,7},{7,6},{8,9},{9,8},{10,11... | collective-permute-start | bytes 786440 | tf_op jit(solution)/shard_map/ppermute | solution.py:35
  50.5 6.4 %collective-permute-start.20 = (f32[128,1024]{1,0:T(8,128)S(1)}, f32[128,1024]{1,0:T(8,128)S(1)}, u32[]{:S(2)}, u32[]{:S(2)}) collective-permute-start(f32[128,1024]{1,0:T(8,128)S(1)} %get-tuple-element.117.refs_0_), channel_id=1, source_target_pairs={{0,1},{1,0},{2,3},{3,2},{4,5},{5,4},{6,7},{7,6},{8,9},{9,8},{10,11... | collective-permute-start | bytes 1572872 | tf_op jit(solution)/shard_map/ppermute | solution.py:35
  51.0 5.4 %collective-permute-start.21 = (f32[128,1024]{1,0:T(8,128)S(1)}, f32[128,1024]{1,0:T(8,128)S(1)}, u32[]{:S(2)}, u32[]{:S(2)}) collective-permute-start(f32[128,1024]{1,0:T(8,128)S(1)} %get-tuple-element.118.refs_0_), channel_id=1, source_target_pairs={{0,1},{1,0},{2,3},{3,2},{4,5},{5,4},{6,7},{7,6},{8,9},{9,8},{10,11... | collective-permute-start | bytes 1572872 | tf_op jit(solution)/shard_map/ppermute | solution.py:35
  51.1 5.3 %collective-permute-start.22 = (f32[128,1024]{1,0:T(8,128)S(1)}, f32[128,1024]{1,0:T(8,128)S(1)}, u32[]{:S(2)}, u32[]{:S(2)}) collective-permute-start(f32[128,1024]{1,0:T(8,128)S(1)} %get-tuple-element.119.refs_1_), channel_id=1, source_target_pairs={{0,1},{1,0},{2,3},{3,2},{4,5},{5,4},{6,7},{7,6},{8,9},{9,8},{10,11... | collective-permute-start | bytes 1572872 | tf_op jit(solution)/shard_map/ppermute | solution.py:35
  52.3 4.9 %collective-permute-start.18 = (f32[128,1024]{1,0:T(8,128)S(1)}, f32[128,1024]{1,0:T(8,128)S(1)}, u32[]{:S(2)}, u32[]{:S(2)}) collective-permute-start(f32[128,1024]{1,0:T(8,128)S(1)} %get-tuple-element.114.refs_10_.refs_6_.refs_4_.refs_0_.refs_7_), channel_id=1, source_target_pairs={{0,1},{1,0},{2,3},{3,2},{4,5},{5,4},{6,7},{7,6},{8,9},{9,8},{10,11... | collective-permute-start | bytes 1572872 | tf_op jit(solution)/shard_map/ppermute | solution.py:35
  52.4 2.7 %collective-permute-start.26 = (f32[64,1024]{1,0:T(8,128)S(1)}, f32[64,1024]{1,0:T(8,128)S(1)}, u32[]{:S(2)}, u32[]{:S(2)}) collective-permute-start(f32[64,1024]{1,0:T(8,128)S(1)} %get-tuple-element.127.refs_3_), channel_id=1, source_target_pairs={{0,1},{1,0},{2,3},{3,2},{4,5},{5,4},{6,7},{7,6},{8,9},{9,8},{10,11... | collective-permute-start | bytes 786440 | tf_op jit(solution)/shard_map/ppermute | solution.py:35
  55.2 2.1 %collective-permute-start.19 = (f32[1,128]{1,0:T(1,128)S(1)}, f32[1,128]{1,0:T(1,128)S(1)}, u32[]{:S(2)}, u32[]{:S(2)}) collective-permute-start(f32[1,128]{1,0:T(1,128)S(1)} %get-tuple-element.116.refs_4_), channel_id=1, source_target_pairs={{0,1},{1,0},{2,3},{3,2},{4,5},{5,4},{6,7},{7,6},{8,9},{9,8},{10,11... | collective-permute-start | bytes 1544 | tf_op jit(solution)/shard_map/ppermute | solution.py:35
  80.8 10.6 %collective-permute-start.27 = (f32[1024,512]{1,0:T(8,128)S(1)}, f32[1024,512]{1,0:T(8,128)S(1)}, u32[]{:S(2)}, u32[]{:S(2)}) collective-permute-start(f32[1024,512]{1,0:T(8,128)S(1)} %next_logits.3.refs_0_), channel_id=1, source_target_pairs={{0,1},{1,0},{2,3},{3,2},{4,5},{5,4},{6,7},{7,6},{8,9},{9,8},{10,11... | collective-permute-start | bytes 6291464 | tf_op jit(solution)/shard_map/ppermute | solution.py:35
  88.6 2.8 %collective-permute-start.29 = (f32[512,512]{1,0:T(8,128)S(1)}, f32[512,512]{1,0:T(8,128)S(1)}, u32[]{:S(2)}, u32[]{:S(2)}) collective-permute-start(f32[512,512]{1,0:T(8,128)S(1)} %next_logits.5.refs_1_), channel_id=1, source_target_pairs={{0,1},{1,0},{2,3},{3,2},{4,5},{5,4},{6,7},{7,6},{8,9},{9,8},{10,11... | collective-permute-start | bytes 3145736 | tf_op jit(solution)/shard_map/ppermute | solution.py:35
  90.4 2.7 %collective-permute-start.28 = (f32[512,512]{1,0:T(8,128)S(1)}, f32[512,512]{1,0:T(8,128)S(1)}, u32[]{:S(2)}, u32[]{:S(2)}) collective-permute-start(f32[512,512]{1,0:T(8,128)S(1)} %next_logits.4.refs_1_), channel_id=1, source_target_pairs={{0,1},{1,0},{2,3},{3,2},{4,5},{5,4},{6,7},{7,6},{8,9},{9,8},{10,11... | collective-permute-start | bytes 3145736 | tf_op jit(solution)/shard_map/ppermute | solution.py:35
where the time goes:
time: 112 us
  Pallas kernels  42.2 us (38%)
  starting transfers between devices  27.1 us (24%)
  blocking collectives  22.9 us (20%)
  waiting for transfers between devices  16.3 us (15%)
  between operations  2.35 us (2%)
    all_to_all x2, blocking collectives, exchange(): return lax.all_to_all(copies, 'example', 0, 0)  22.9 us
    pallas_call x2, Pallas kernels, update(): pl.pallas_call(functools.partial(update_kernel, start, 512), out_shape=(p...  12.7 us
    ppermute x23, starting transfers between devices, swap(): return lax.ppermute(x, axis, [(i, i ^ offset) for i in range(n)])  12.4 us
    ppermute x6, starting transfers between devices, gather_blocks(): later.append(lax.ppermute(held[k], 'example', ring))  12.1 us
    ppermute x23, waiting for transfers between devices, swap(): return lax.ppermute(x, axis, [(i, i ^ offset) for i in range(n)])  9.69 us
    pallas_call x1, Pallas kernels, finish(): pl.pallas_call(functools.partial(finish_kernel, len(moved), len(e_parts),...  7.15 us
    ppermute x6, waiting for transfers between devices, gather_blocks(): later.append(lax.ppermute(held[k], 'example', ring))  6.62 us
    pallas_call x5, Pallas kernels, arriving_logits(): pl.pallas_call(functools.partial(arriving_kernel, count, pieces, start),...  5.33 us
  transfers between devices with their start and end apart: 30, of which 9 were waited for; matrix products, arithmetic and copies ran while one was open for 0% of the time, Pallas kernels for 20%

commit v1 on v0

--- a/solution.py
+++ b/solution.py
@@ -639,7 +639,7 @@
         parts = [part for slot in groups[g] for part in slots[slot]]
         tokens = tuple(stats[-1:]) + tuple(buffers[:1]) + tuple(waits[g] if g < n // 2 else ())
         start = groups[g][0] * rows
-        piece = STEP if g < behind else LANES
+        piece = (64,256,256,128,128)[g] if count == 5 else LANES
         block, found = arriving_logits(parts, w_low, plain, start, all_rows, piece, tokens)
         plain = (block,)
         logits.append(found)

time: 112 us -> 109 us (0.973)
  starting transfers between devices: 27.1 us -> 25.7 us
  waiting for transfers between devices: 16.3 us -> 14.9 us
    ppermute x23 -> x19, waiting for transfers between devices: 9.69 us -> 8.02 us  [swap(): return lax.ppermute(x, axis, [(i, i ^ offset) for i in range(n)])]
    ppermute x23 -> x19, starting transfers between devices: 12.4 us -> 10.9 us  [swap(): return lax.ppermute(x, axis, [(i, i ^ offset) for i in range(n)])]
  transfers between devices with their start and end apart: 30 -> 26, of which waited for: 9 -> 11; matrix products, arithmetic and copies ran while one was open for 0% -> 0% of each run, Pallas kernels for 20% -> 21%
where the time goes in v1:
time: 109 us
  Pallas kernels  42.2 us (39%)
  starting transfers between devices  25.7 us (24%)
  blocking collectives  23.1 us (21%)
  waiting for transfers between devices  14.9 us (14%)
  between operations  2.35 us (2%)
    all_to_all x2, blocking collectives, exchange(): return lax.all_to_all(copies, 'example', 0, 0)  23.1 us
    pallas_call x2, Pallas kernels, update(): pl.pallas_call(functools.partial(update_kernel, start, 512), out_shape=(p...  12.7 us
    ppermute x6, starting transfers between devices, gather_blocks(): later.append(lax.ppermute(held[k], 'example', ring))  12.1 us
    ppermute x19, starting transfers between devices, swap(): return lax.ppermute(x, axis, [(i, i ^ offset) for i in range(n)])  10.9 us
    ppermute x19, waiting for transfers between devices, swap(): return lax.ppermute(x, axis, [(i, i ^ offset) for i in range(n)])  8.02 us
    pallas_call x1, Pallas kernels, finish(): pl.pallas_call(functools.partial(finish_kernel, len(moved), len(e_parts),...  7.15 us
    ppermute x6, waiting for transfers between devices, gather_blocks(): later.append(lax.ppermute(held[k], 'example', ring))  6.62 us
    pallas_call x5, Pallas kernels, arriving_logits(): pl.pallas_call(functools.partial(arriving_kernel, count, pieces, start),...  5.31 us
  transfers between devices with their start and end apart: 26, of which 11 were waited for; matrix products, arithmetic and copies ran while one was open for 0% of the time, Pallas kernels for 21%

profile of v1, /device:TPU:0, one launch (start us, length us, event | category | flops | bytes accessed | tf_op | source)
XLA Modules:
  0.0 109.2 jit_solution(10357896402227270596)
XLA Ops:
  0.6 1.1 fusion
  1.7 3.1 %collective-permute-start = (bf16[64,2048]{1,0:T(8,128)(2,1)S(1)}, bf16[64,2048]{1,0:T(8,128)(2,1)S(1)}, u32[]{:S(2)}, u32[]{:S(2)}) collective-permute-start(bf16[64,2048]{1,0:T(8,128)(2,1)S(1)} %get-tuple-element.141.refs_0_), channel_id=1, source_target_pairs={{0,4},{2,6},{4,12},{6,14},{12,8},{14,10},{8,0},{10,2},{1,5},{3,7},... | collective-permute-start | bytes 786440 | tf_op jit(solution)/shard_map/ppermute | solution.py:97
  4.8 1.5 %collective-permute-start.4 = (bf16[64,2048]{1,0:T(8,128)(2,1)S(1)}, bf16[64,2048]{1,0:T(8,128)(2,1)S(1)}, u32[]{:S(2)}, u32[]{:S(2)}) collective-permute-start(bf16[64,2048]{1,0:T(8,128)(2,1)S(1)} %get-tuple-element.141.refs_0_), channel_id=1, source_target_pairs={{0,2},{2,0},{4,6},{6,4},{8,10},{10,8},{12,14},{14,12},{1,3},{3,1},... | collective-permute-start | bytes 786440 | tf_op jit(solution)/shard_map/ppermute | solution.py:35
  6.3 2.6 %collective-permute-start.2 = (bf16[64,2048]{1,0:T(8,128)(2,1)S(1)}, bf16[64,2048]{1,0:T(8,128)(2,1)S(1)}, u32[]{:S(2)}, u32[]{:S(2)}) collective-permute-start(bf16[64,2048]{1,0:T(8,128)(2,1)S(1)} %get-tuple-element.140.refs_1_), channel_id=1, source_target_pairs={{0,4},{2,6},{4,12},{6,14},{12,8},{14,10},{8,0},{10,2},{1,5},{3,7},... | collective-permute-start | bytes 786440 | tf_op jit(solution)/shard_map/ppermute | solution.py:97
  8.9 0.5 collective-permute-start.7
  10.7 3.7 %prepare.1 = (f32[2048,512]{1,0:T(8,128)S(1)}, f32[2048,512]{1,0:T(8,128)S(1)}, bf16[2048,1024]{1,0:T(8,128)(2,1)S(1)}, f32[1,128]{1,0:T(1,128)S(1)}, f32[1,128]{1,0:T(1,128)S(1)}) custom-call(f32[2048,1024]{1,0:T(8,128)} %w_ref.1, bf16[128,2048]{1,0:T(8,128)(2,1)} %x_ref.1, s32[1,128]{1,0:T(1,128)} %bitcast.2, s32[1]{0:T(128)S(6)} %copy.31.counts_ref, ...), custom_call_target="tpu_custom_call" | custom-call | flops 1 | bytes 1 | tf_op jit(solution)/shard_map/prepare/pallas_call | solution.py:153
  14.5 1.6 %collective-permute-start.5 = (bf16[64,2048]{1,0:T(8,128)(2,1)S(1)}, bf16[64,2048]{1,0:T(8,128)(2,1)S(1)}, u32[]{:S(2)}, u32[]{:S(2)}) collective-permute-start(bf16[64,2048]{1,0:T(8,128)(2,1)S(1)} %collective-permute-done.refs_5_.refs_0_), channel_id=1, source_target_pairs={{0,2},{2,0},{4,6},{6,4},{8,10},{10,8},{12,14},{14,12},{1,3},{3,1},... | collective-permute-start | bytes 786440 | tf_op jit(solution)/shard_map/ppermute | solution.py:35
  16.0 2.1 %collective-permute-start.1 = (bf16[64,2048]{1,0:T(8,128)(2,1)S(1)}, bf16[64,2048]{1,0:T(8,128)(2,1)S(1)}, u32[]{:S(2)}, u32[]{:S(2)}) collective-permute-start(bf16[64,2048]{1,0:T(8,128)(2,1)S(1)} %collective-permute-done.refs_5_.refs_0_), channel_id=1, source_target_pairs={{0,4},{2,6},{4,12},{6,14},{12,8},{14,10},{8,0},{10,2},{1,5},{3,7},... | collective-permute-start | bytes 786440 | tf_op jit(solution)/shard_map/ppermute | solution.py:97
  18.1 1.6 %collective-permute-start.3 = (bf16[64,2048]{1,0:T(8,128)(2,1)S(1)}, bf16[64,2048]{1,0:T(8,128)(2,1)S(1)}, u32[]{:S(2)}, u32[]{:S(2)}) collective-permute-start(bf16[64,2048]{1,0:T(8,128)(2,1)S(1)} %collective-permute-done.2.refs_6_.refs_1_), channel_id=1, source_target_pairs={{0,4},{2,6},{4,12},{6,14},{12,8},{14,10},{8,0},{10,2},{1,5},{3,7},... | collective-permute-start | bytes 786440 | tf_op jit(solution)/shard_map/ppermute | solution.py:97
  19.7 1.5 %collective-permute-start.8 = (bf16[64,2048]{1,0:T(8,128)(2,1)S(1)}, bf16[64,2048]{1,0:T(8,128)(2,1)S(1)}, u32[]{:S(2)}, u32[]{:S(2)}) collective-permute-start(bf16[64,2048]{1,0:T(8,128)(2,1)S(1)} %collective-permute-done.2.refs_6_.refs_1_), channel_id=1, source_target_pairs={{0,2},{2,0},{4,6},{6,4},{8,10},{10,8},{12,14},{14,12},{1,3},{3,1},... | collective-permute-start | bytes 786440 | tf_op jit(solution)/shard_map/ppermute | solution.py:35
  21.2 4.0 %collective-permute-done.5.refs_2_ = bf16[64,2048]{1,0:T(8,128)(2,1)S(1)} collective-permute-done((bf16[64,2048]{1,0:T(8,128)(2,1)S(1)}, bf16[64,2048]{1,0:T(8,128)(2,1)S(1)}, u32[]{:S(2)}, u32[]{:S(2)}) %collective-permute-start.5) | collective-permute-done | bytes 262176 | tf_op jit(solution)/shard_map/ppermute | solution.py:35
  25.2 0.9 collective-permute-done.1.refs_8_.refs_0_
  26.2 0.6 collective-permute-start.6
  26.8 2.6 %collective-permute-start.14 = (bf16[64,2048]{1,0:T(8,128)(2,1)S(1)}, bf16[64,2048]{1,0:T(8,128)(2,1)S(1)}, u32[]{:S(2)}, u32[]{:S(2)}) collective-permute-start(bf16[64,2048]{1,0:T(8,128)(2,1)S(1)} %collective-permute-done.1.refs_8_.refs_0_), channel_id=1, source_target_pairs={{0,4},{2,6},{4,12},{6,14},{12,8},{14,10},{8,0},{10,2},{1,5},{3,7},... | collective-permute-start | bytes 786440 | tf_op jit(solution)/shard_map/ppermute | solution.py:97
  29.4 1.8 %collective-permute-done.3.refs_9_.refs_1_ = bf16[64,2048]{1,0:T(8,128)(2,1)S(1)} collective-permute-done((bf16[64,2048]{1,0:T(8,128)(2,1)S(1)}, bf16[64,2048]{1,0:T(8,128)(2,1)S(1)}, u32[]{:S(2)}, u32[]{:S(2)}) %collective-permute-start.3) | collective-permute-done | bytes 262176 | tf_op jit(solution)/shard_map/ppermute | solution.py:97
  31.4 1.3 %arriving_logits.5 = (bf16[1024,2048]{1,0:T(8,128)(2,1)S(1)}, f32[64,1024]{1,0:T(8,128)S(1)}, f32[64,1024]{1,0:T(8,128)S(1)}, f32[64,1024]{1,0:T(8,128)S(1)}, f32[64,1024]{1,0:T(8,128)S(1)}) custom-call(bf16[64,2048]{1,0:T(8,128)(2,1)S(1)} %get-tuple-element.141.refs_0_, bf16[64,2048]{1,0:T(8,128)(2,1)S(1)} %get-tuple-element.140.refs_1_, ...), custom_call_target="tpu_custom_call" | custom-call | flops 1 | bytes 1 | tf_op jit(solution)/shard_map/arriving_logits/pallas_call | solution.py:195
  32.7 1.7 %collective-permute-start.9 = (bf16[64,2048]{1,0:T(8,128)(2,1)S(1)}, bf16[64,2048]{1,0:T(8,128)(2,1)S(1)}, u32[]{:S(2)}, u32[]{:S(2)}) collective-permute-start(bf16[64,2048]{1,0:T(8,128)(2,1)S(1)} %collective-permute-done.3.refs_9_.refs_1_), channel_id=1, source_target_pairs={{0,2},{2,0},{4,6},{6,4},{8,10},{10,8},{12,14},{14,12},{1,3},{3,1},... | collective-permute-start | bytes 786440 | tf_op jit(solution)/shard_map/ppermute | solution.py:35
  34.3 2.1 %collective-permute-done.6.refs_2_.refs_0_ = bf16[64,2048]{1,0:T(8,128)(2,1)S(1)} collective-permute-done((bf16[64,2048]{1,0:T(8,128)(2,1)S(1)}, bf16[64,2048]{1,0:T(8,128)(2,1)S(1)}, u32[]{:S(2)}, u32[]{:S(2)}) %collective-permute-start.6) | collective-permute-done | bytes 262176 | tf_op jit(solution)/shard_map/ppermute | solution.py:35
  36.5 0.4 collective-permute-done.14.refs_8_.refs_0_
  37.0 3.4 %collective-permute-done.15.refs_9_.refs_1_.refs_0_ = bf16[64,2048]{1,0:T(8,128)(2,1)S(1)} collective-permute-done((bf16[64,2048]{1,0:T(8,128)(2,1)S(1)}, bf16[64,2048]{1,0:T(8,128)(2,1)S(1)}, u32[]{:S(2)}, u32[]{:S(2)}) %collective-permute-start.15) | collective-permute-done | bytes 262176 | tf_op jit(solution)/shard_map/ppermute | solution.py:97
  40.7 2.6 %collective-permute-start.17 = (bf16[64,2048]{1,0:T(8,128)(2,1)S(1)}, bf16[64,2048]{1,0:T(8,128)(2,1)S(1)}, u32[]{:S(2)}, u32[]{:S(2)}) collective-permute-start(bf16[64,2048]{1,0:T(8,128)(2,1)S(1)} %relay.3), channel_id=1, source_target_pairs={{0,4},{2,6},{4,12},{6,14},{12,8},{14,10},{8,0},{10,2},{1,5},{3,7},... | collective-permute-start | bytes 786440 | tf_op jit(solution)/shard_map/ppermute | solution.py:111
  43.3 1.6 %collective-permute-start.16 = (bf16[64,2048]{1,0:T(8,128)(2,1)S(1)}, bf16[64,2048]{1,0:T(8,128)(2,1)S(1)}, u32[]{:S(2)}, u32[]{:S(2)}) collective-permute-start(bf16[64,2048]{1,0:T(8,128)(2,1)S(1)} %relay.2), channel_id=1, source_target_pairs={{0,2},{2,0},{4,6},{6,4},{8,10},{10,8},{12,14},{14,12},{1,3},{3,1},... | collective-permute-start | bytes 786440 | tf_op jit(solution)/shard_map/ppermute | solution.py:35
  44.9 0.4 turn.4
  45.3 0.5 first_stats.5
  45.8 1.3 %arriving_logits.6 = (bf16[1024,2048]{1,0:T(8,128)(2,1)S(1)}, f32[256,1024]{1,0:T(8,128)S(1)}) custom-call(bf16[64,2048]{1,0:T(8,128)(2,1)S(1)} %collective-permute-done.refs_5_.refs_0_, bf16[64,2048]{1,0:T(8,128)(2,1)S(1)} %collective-permute-done.2.refs_6_.refs_1_, ...), custom_call_target="tpu_custom_call", output_to_operand_aliasing={{0}: (5, {})} | custom-call | flops 1 | bytes 1 | tf_op jit(solution)/shard_map/arriving_logits/pallas_call | solution.py:195
  47.2 0.4 turn.5
  47.5 1.3 %arriving_logits.7 = (bf16[1024,2048]{1,0:T(8,128)(2,1)S(1)}, f32[256,1024]{1,0:T(8,128)S(1)}) custom-call(bf16[64,2048]{1,0:T(8,128)(2,1)S(1)} %collective-permute-done.1.refs_8_.refs_0_, bf16[64,2048]{1,0:T(8,128)(2,1)S(1)} %collective-permute-done.3.refs_9_.refs_1_, ...), custom_call_target="tpu_custom_call", output_to_operand_aliasing={{0}: (5, {})} | custom-call | flops 1 | bytes 1 | tf_op jit(solution)/shard_map/arriving_logits/pallas_call | solution.py:195
  48.8 0.4 turn.6
  49.2 0.7 arriving_logits.8
  50.7 0.7 arriving_logits.9
  51.4 0.4 collective-permute-start.18
  52.0 0.4 turn.7
  52.4 0.5 first_stats.6
  52.8 0.5 first_stats.7
  53.9 0.4 collective-permute-done.19.refs_5_
  54.7 13.2 %all_to_all.10.all_ref = f32[8,8,640]{2,1,0:T(8,128)S(1)} all-to-all(f32[8,8,640]{2,1,0:T(8,128)S(1)} %get-tuple-element.116), channel_id=1, replica_groups=mesh['groups'=2,'example'=8,'cls'=2] {'example'}, dimensions={0} | all-to-all | bytes 327680 | tf_op jit(solution)/shard_map/all_to_all | solution.py:606
  67.9 1.6 %first_weights.1 = (bf16[1024,1024]{1,0:T(8,128)(2,1)S(1)}, bf16[1024,1024]{1,0:T(8,128)(2,1)S(1)}, f32[8,128]{1,0:T(8,128)S(1)}, f32[8,128]{1,0:T(8,128)S(1)}) custom-call(f32[8,384]{1,0:T(8,128)S(1)} %get-tuple-element.115.own_ref, f32[8,8,640]{2,1,0:T(8,128)S(1)} %all_to_all.10.all_ref, f32[256,1024]{1,0:T(8,128)S(1)} %get-tuple-element.117.refs_0_, ...), custom_call_target="tpu_custom_call" | custom-call | bytes 8388608 | tf_op jit(solution)/shard_map/first_weights/pallas_call | solution.py:379
  69.5 6.2 %update.2 = (f32[2048,512]{1,0:T(8,128)S(1)}, f32[2048,512]{1,0:T(8,128)S(1)}, bf16[2048,512]{1,0:T(8,128)(2,1)S(1)}) custom-call(bf16[2048,1024]{1,0:T(8,128)(2,1)S(1)} %get-tuple-element.102.refs_5_.refs_8_.turned_ref, bf16[2048,1024]{1,0:T(8,128)(2,1)S(1)} %get-tuple-element.103.squares_ref, ...), custom_call_target="tpu_custom_call", output_to_operand_aliasing={{0}: (2, {})} | custom-call | flops 4294967296 | tf_op jit(solution)/shard_map/update/pallas_call | solution.py:415
  75.7 2.3 %next_logits.3.refs_0_ = f32[1024,512]{1,0:T(8,128)S(1)} custom-call(bf16[1024,2048]{1,0:T(8,128)(2,1)S(1)} %get-tuple-element.100.plain_ref, bf16[2048,512]{1,0:T(8,128)(2,1)S(1)} %get-tuple-element.125.low_ref), custom_call_target="tpu_custom_call" | custom-call | flops 2147483648 | tf_op jit(solution)/shard_map/next_logits/pallas_call | solution.py:442
  78.1 6.4 %update.3 = (f32[2048,512]{1,0:T(8,128)S(1)}, f32[2048,512]{1,0:T(8,128)S(1)}, bf16[2048,512]{1,0:T(8,128)(2,1)S(1)}) custom-call(bf16[2048,1024]{1,0:T(8,128)(2,1)S(1)} %get-tuple-element.102.refs_5_.refs_8_.turned_ref, bf16[2048,1024]{1,0:T(8,128)(2,1)S(1)} %get-tuple-element.103.squares_ref, ...), custom_call_target="tpu_custom_call", output_to_operand_aliasing={{0}: (2, {})} | custom-call | flops 4294967296 | tf_op jit(solution)/shard_map/update/pallas_call | solution.py:415
  84.6 1.2 %next_logits.5.refs_1_ = f32[512,512]{1,0:T(8,128)S(1)} custom-call(bf16[1024,2048]{1,0:T(8,128)(2,1)S(1)} %get-tuple-element.100.plain_ref, bf16[2048,512]{1,0:T(8,128)(2,1)S(1)} %get-tuple-element.127.low_ref), custom_call_target="tpu_custom_call" | custom-call | flops 1073741824 | tf_op jit(solution)/shard_map/next_logits/pallas_call | solution.py:442
  85.8 0.6 collective-permute-start.25
  86.4 1.2 %next_logits.4.refs_1_ = f32[512,512]{1,0:T(8,128)S(1)} custom-call(bf16[1024,2048]{1,0:T(8,128)(2,1)S(1)} %get-tuple-element.100.plain_ref, bf16[2048,512]{1,0:T(8,128)(2,1)S(1)} %get-tuple-element.127.low_ref), custom_call_target="tpu_custom_call" | custom-call | flops 1073741824 | tf_op jit(solution)/shard_map/next_logits/pallas_call | solution.py:442
  87.7 1.0 collective-permute-done.25.refs_3_
  88.6 1.7 %last_stats.2 = (f32[512,1024]{1,0:T(8,128)S(1)}, f32[8,384]{1,0:T(8,128)S(1)}) custom-call(f32[1024,512]{1,0:T(8,128)S(1)} %next_logits.3.refs_0_, f32[512,512]{1,0:T(8,128)S(1)} %next_logits.5.refs_1_, f32[1024,512]{1,0:T(8,128)S(1)} %collective-permute-done.23.refs_2_, f32[512,512]{1,0:T(8,128)S(1)} %collective-permute-done.25.refs_3_, ...), custom_call_target="tpu_custom_call" | custom-call | bytes 12582912 | tf_op jit(solution)/shard_map/last_stats/pallas_call | solution.py:509
  90.3 1.7 %last_stats.3 = (f32[512,1024]{1,0:T(8,128)S(1)}, f32[8,384]{1,0:T(8,128)S(1)}, f32[8,8,384]{2,1,0:T(8,128)S(1)}) custom-call(f32[1024,512]{1,0:T(8,128)S(1)} %next_logits.3.refs_0_, f32[512,512]{1,0:T(8,128)S(1)} %next_logits.4.refs_1_, f32[1024,512]{1,0:T(8,128)S(1)} %collective-permute-done.23.refs_2_, f32[512,512]{1,0:T(8,128)S(1)} %collective-permute-done.24.refs_3_, ...), custom_call_target="tpu_custom_call" | custom-call | bytes 12582912 | tf_op jit(solution)/shard_map/last_stats/pallas_call | solution.py:509
  92.1 9.9 %all_to_all.11.all_ref = f32[8,8,384]{2,1,0:T(8,128)S(1)} all-to-all(f32[8,8,384]{2,1,0:T(8,128)S(1)} %get-tuple-element.131), channel_id=1, replica_groups=mesh['groups'=2,'example'=8,'cls'=2] {'example'}, dimensions={0} | all-to-all | bytes 196608 | tf_op jit(solution)/shard_map/all_to_all | solution.py:606
  101.9 7.1 %finish.1 = (f32[2048,1024]{1,0:T(8,128)}, f32[1,128]{1,0:T(1,128)}) custom-call(f32[8,384]{1,0:T(8,128)S(1)} %get-tuple-element.130.own_ref, f32[8,8,384]{2,1,0:T(8,128)S(1)} %all_to_all.11.all_ref, f32[8,128]{1,0:T(8,128)S(1)} %get-tuple-element.128.refs_4_.target_ref, bf16[2048,1024]{1,0:T(8,128)(2,1)S(1)} %get-tuple-element.102.refs_5_.refs_8_.turned_ref, ...), custom_call_target="tpu_custom_call" | custom-call | flops 4294967296 | tf_op jit(solution)/shard_map/finish/pallas_call | solution.py:584
  (37 shorter events, 2.6 us)
Async XLA Ops:
  1.7 12.7 %collective-permute-start = (bf16[64,2048]{1,0:T(8,128)(2,1)S(1)}, bf16[64,2048]{1,0:T(8,128)(2,1)S(1)}, u32[]{:S(2)}, u32[]{:S(2)}) collective-permute-start(bf16[64,2048]{1,0:T(8,128)(2,1)S(1)} %get-tuple-element.141.refs_0_), channel_id=1, source_target_pairs={{0,4},{2,6},{4,12},{6,14},{12,8},{14,10},{8,0},{10,2},{1,5},{3,7},... | collective-permute-start | bytes 786440 | tf_op jit(solution)/shard_map/ppermute | solution.py:97
  4.8 9.7 %collective-permute-start.4 = (bf16[64,2048]{1,0:T(8,128)(2,1)S(1)}, bf16[64,2048]{1,0:T(8,128)(2,1)S(1)}, u32[]{:S(2)}, u32[]{:S(2)}) collective-permute-start(bf16[64,2048]{1,0:T(8,128)(2,1)S(1)} %get-tuple-element.141.refs_0_), channel_id=1, source_target_pairs={{0,2},{2,0},{4,6},{6,4},{8,10},{10,8},{12,14},{14,12},{1,3},{3,1},... | collective-permute-start | bytes 786440 | tf_op jit(solution)/shard_map/ppermute | solution.py:35
  6.3 11.8 %collective-permute-start.2 = (bf16[64,2048]{1,0:T(8,128)(2,1)S(1)}, bf16[64,2048]{1,0:T(8,128)(2,1)S(1)}, u32[]{:S(2)}, u32[]{:S(2)}) collective-permute-start(bf16[64,2048]{1,0:T(8,128)(2,1)S(1)} %get-tuple-element.140.refs_1_), channel_id=1, source_target_pairs={{0,4},{2,6},{4,12},{6,14},{12,8},{14,10},{8,0},{10,2},{1,5},{3,7},... | collective-permute-start | bytes 786440 | tf_op jit(solution)/shard_map/ppermute | solution.py:97
  8.9 10.8 %collective-permute-start.7 = (bf16[64,2048]{1,0:T(8,128)(2,1)S(1)}, bf16[64,2048]{1,0:T(8,128)(2,1)S(1)}, u32[]{:S(2)}, u32[]{:S(2)}) collective-permute-start(bf16[64,2048]{1,0:T(8,128)(2,1)S(1)} %get-tuple-element.140.refs_1_), channel_id=1, source_target_pairs={{0,2},{2,0},{4,6},{6,4},{8,10},{10,8},{12,14},{14,12},{1,3},{3,1},... | collective-permute-start | bytes 786440 | tf_op jit(solution)/shard_map/ppermute | solution.py:35
  14.5 10.8 %collective-permute-start.5 = (bf16[64,2048]{1,0:T(8,128)(2,1)S(1)}, bf16[64,2048]{1,0:T(8,128)(2,1)S(1)}, u32[]{:S(2)}, u32[]{:S(2)}) collective-permute-start(bf16[64,2048]{1,0:T(8,128)(2,1)S(1)} %collective-permute-done.refs_5_.refs_0_), channel_id=1, source_target_pairs={{0,2},{2,0},{4,6},{6,4},{8,10},{10,8},{12,14},{14,12},{1,3},{3,1},... | collective-permute-start | bytes 786440 | tf_op jit(solution)/shard_map/ppermute | solution.py:35
  16.0 10.1 %collective-permute-start.1 = (bf16[64,2048]{1,0:T(8,128)(2,1)S(1)}, bf16[64,2048]{1,0:T(8,128)(2,1)S(1)}, u32[]{:S(2)}, u32[]{:S(2)}) collective-permute-start(bf16[64,2048]{1,0:T(8,128)(2,1)S(1)} %collective-permute-done.refs_5_.refs_0_), channel_id=1, source_target_pairs={{0,4},{2,6},{4,12},{6,14},{12,8},{14,10},{8,0},{10,2},{1,5},{3,7},... | collective-permute-start | bytes 786440 | tf_op jit(solution)/shard_map/ppermute | solution.py:97
  18.1 13.0 %collective-permute-start.3 = (bf16[64,2048]{1,0:T(8,128)(2,1)S(1)}, bf16[64,2048]{1,0:T(8,128)(2,1)S(1)}, u32[]{:S(2)}, u32[]{:S(2)}) collective-permute-start(bf16[64,2048]{1,0:T(8,128)(2,1)S(1)} %collective-permute-done.2.refs_6_.refs_1_), channel_id=1, source_target_pairs={{0,4},{2,6},{4,12},{6,14},{12,8},{14,10},{8,0},{10,2},{1,5},{3,7},... | collective-permute-start | bytes 786440 | tf_op jit(solution)/shard_map/ppermute | solution.py:97
  19.7 13.0 %collective-permute-start.8 = (bf16[64,2048]{1,0:T(8,128)(2,1)S(1)}, bf16[64,2048]{1,0:T(8,128)(2,1)S(1)}, u32[]{:S(2)}, u32[]{:S(2)}) collective-permute-start(bf16[64,2048]{1,0:T(8,128)(2,1)S(1)} %collective-permute-done.2.refs_6_.refs_1_), channel_id=1, source_target_pairs={{0,2},{2,0},{4,6},{6,4},{8,10},{10,8},{12,14},{14,12},{1,3},{3,1},... | collective-permute-start | bytes 786440 | tf_op jit(solution)/shard_map/ppermute | solution.py:35
  26.2 10.3 %collective-permute-start.6 = (bf16[64,2048]{1,0:T(8,128)(2,1)S(1)}, bf16[64,2048]{1,0:T(8,128)(2,1)S(1)}, u32[]{:S(2)}, u32[]{:S(2)}) collective-permute-start(bf16[64,2048]{1,0:T(8,128)(2,1)S(1)} %collective-permute-done.1.refs_8_.refs_0_), channel_id=1, source_target_pairs={{0,2},{2,0},{4,6},{6,4},{8,10},{10,8},{12,14},{14,12},{1,3},{3,1},... | collective-permute-start | bytes 786440 | tf_op jit(solution)/shard_map/ppermute | solution.py:35
  26.8 10.1 %collective-permute-start.14 = (bf16[64,2048]{1,0:T(8,128)(2,1)S(1)}, bf16[64,2048]{1,0:T(8,128)(2,1)S(1)}, u32[]{:S(2)}, u32[]{:S(2)}) collective-permute-start(bf16[64,2048]{1,0:T(8,128)(2,1)S(1)} %collective-permute-done.1.refs_8_.refs_0_), channel_id=1, source_target_pairs={{0,4},{2,6},{4,12},{6,14},{12,8},{14,10},{8,0},{10,2},{1,5},{3,7},... | collective-permute-start | bytes 786440 | tf_op jit(solution)/shard_map/ppermute | solution.py:97
  31.2 9.3 %collective-permute-start.15 = (bf16[64,2048]{1,0:T(8,128)(2,1)S(1)}, bf16[64,2048]{1,0:T(8,128)(2,1)S(1)}, u32[]{:S(2)}, u32[]{:S(2)}) collective-permute-start(bf16[64,2048]{1,0:T(8,128)(2,1)S(1)} %collective-permute-done.3.refs_9_.refs_1_), channel_id=1, source_target_pairs={{0,4},{2,6},{4,12},{6,14},{12,8},{14,10},{8,0},{10,2},{1,5},{3,7},... | collective-permute-start | bytes 786440 | tf_op jit(solution)/shard_map/ppermute | solution.py:97
  32.7 8.0 %collective-permute-start.9 = (bf16[64,2048]{1,0:T(8,128)(2,1)S(1)}, bf16[64,2048]{1,0:T(8,128)(2,1)S(1)}, u32[]{:S(2)}, u32[]{:S(2)}) collective-permute-start(bf16[64,2048]{1,0:T(8,128)(2,1)S(1)} %collective-permute-done.3.refs_9_.refs_1_), channel_id=1, source_target_pairs={{0,2},{2,0},{4,6},{6,4},{8,10},{10,8},{12,14},{14,12},{1,3},{3,1},... | collective-permute-start | bytes 786440 | tf_op jit(solution)/shard_map/ppermute | solution.py:35
  34.3 9.0 %collective-permute-start.10 = (f32[64,1024]{1,0:T(8,128)S(1)}, f32[64,1024]{1,0:T(8,128)S(1)}, u32[]{:S(2)}, u32[]{:S(2)}) collective-permute-start(f32[64,1024]{1,0:T(8,128)S(1)} %get-tuple-element.83.refs_0_), channel_id=1, source_target_pairs={{0,1},{1,0},{2,3},{3,2},{4,5},{5,4},{6,7},{7,6},{8,9},{9,8},{10,11... | collective-permute-start | bytes 786440 | tf_op jit(solution)/shard_map/ppermute | solution.py:35
  36.5 8.8 %collective-permute-start.11 = (f32[64,1024]{1,0:T(8,128)S(1)}, f32[64,1024]{1,0:T(8,128)S(1)}, u32[]{:S(2)}, u32[]{:S(2)}) collective-permute-start(f32[64,1024]{1,0:T(8,128)S(1)} %get-tuple-element.84.refs_1_), channel_id=1, source_target_pairs={{0,1},{1,0},{2,3},{3,2},{4,5},{5,4},{6,7},{7,6},{8,9},{9,8},{10,11... | collective-permute-start | bytes 786440 | tf_op jit(solution)/shard_map/ppermute | solution.py:35
  36.9 8.4 %collective-permute-start.12 = (f32[64,1024]{1,0:T(8,128)S(1)}, f32[64,1024]{1,0:T(8,128)S(1)}, u32[]{:S(2)}, u32[]{:S(2)}) collective-permute-start(f32[64,1024]{1,0:T(8,128)S(1)} %get-tuple-element.85.refs_2_), channel_id=1, source_target_pairs={{0,1},{1,0},{2,3},{3,2},{4,5},{5,4},{6,7},{7,6},{8,9},{9,8},{10,11... | collective-permute-start | bytes 786440 | tf_op jit(solution)/shard_map/ppermute | solution.py:35
  40.4 4.9 %collective-permute-start.13 = (f32[64,1024]{1,0:T(8,128)S(1)}, f32[64,1024]{1,0:T(8,128)S(1)}, u32[]{:S(2)}, u32[]{:S(2)}) collective-permute-start(f32[64,1024]{1,0:T(8,128)S(1)} %get-tuple-element.86.refs_3_), channel_id=1, source_target_pairs={{0,1},{1,0},{2,3},{3,2},{4,5},{5,4},{6,7},{7,6},{8,9},{9,8},{10,11... | collective-permute-start | bytes 786440 | tf_op jit(solution)/shard_map/ppermute | solution.py:35
  40.7 9.5 %collective-permute-start.17 = (bf16[64,2048]{1,0:T(8,128)(2,1)S(1)}, bf16[64,2048]{1,0:T(8,128)(2,1)S(1)}, u32[]{:S(2)}, u32[]{:S(2)}) collective-permute-start(bf16[64,2048]{1,0:T(8,128)(2,1)S(1)} %relay.3), channel_id=1, source_target_pairs={{0,4},{2,6},{4,12},{6,14},{12,8},{14,10},{8,0},{10,2},{1,5},{3,7},... | collective-permute-start | bytes 786440 | tf_op jit(solution)/shard_map/ppermute | solution.py:111
  43.3 6.8 %collective-permute-start.16 = (bf16[64,2048]{1,0:T(8,128)(2,1)S(1)}, bf16[64,2048]{1,0:T(8,128)(2,1)S(1)}, u32[]{:S(2)}, u32[]{:S(2)}) collective-permute-start(bf16[64,2048]{1,0:T(8,128)(2,1)S(1)} %relay.2), channel_id=1, source_target_pairs={{0,2},{2,0},{4,6},{6,4},{8,10},{10,8},{12,14},{14,12},{1,3},{3,1},... | collective-permute-start | bytes 786440 | tf_op jit(solution)/shard_map/ppermute | solution.py:35
  47.1 5.3 %collective-permute-start.22 = (f32[256,1024]{1,0:T(8,128)S(1)}, f32[256,1024]{1,0:T(8,128)S(1)}, u32[]{:S(2)}, u32[]{:S(2)}) collective-permute-start(f32[256,1024]{1,0:T(8,128)S(1)} %get-tuple-element.111.refs_0_), channel_id=1, source_target_pairs={{0,1},{1,0},{2,3},{3,2},{4,5},{5,4},{6,7},{7,6},{8,9},{9,8},{10,11... | collective-permute-start | bytes 3145736 | tf_op jit(solution)/shard_map/ppermute | solution.py:35
  50.2 2.7 %collective-permute-start.21 = (f32[256,1024]{1,0:T(8,128)S(1)}, f32[256,1024]{1,0:T(8,128)S(1)}, u32[]{:S(2)}, u32[]{:S(2)}) collective-permute-start(f32[256,1024]{1,0:T(8,128)S(1)} %get-tuple-element.109.refs_0_), channel_id=1, source_target_pairs={{0,1},{1,0},{2,3},{3,2},{4,5},{5,4},{6,7},{7,6},{8,9},{9,8},{10,11... | collective-permute-start | bytes 3145736 | tf_op jit(solution)/shard_map/ppermute | solution.py:35
  50.5 3.1 %collective-permute-start.20 = (f32[128,1024]{1,0:T(8,128)S(1)}, f32[128,1024]{1,0:T(8,128)S(1)}, u32[]{:S(2)}, u32[]{:S(2)}) collective-permute-start(f32[128,1024]{1,0:T(8,128)S(1)} %get-tuple-element.108.refs_0_), channel_id=1, source_target_pairs={{0,1},{1,0},{2,3},{3,2},{4,5},{5,4},{6,7},{7,6},{8,9},{9,8},{10,11... | collective-permute-start | bytes 1572872 | tf_op jit(solution)/shard_map/ppermute | solution.py:35
  51.4 2.9 %collective-permute-start.18 = (f32[128,1024]{1,0:T(8,128)S(1)}, f32[128,1024]{1,0:T(8,128)S(1)}, u32[]{:S(2)}, u32[]{:S(2)}) collective-permute-start(f32[128,1024]{1,0:T(8,128)S(1)} %get-tuple-element.105.refs_4_.refs_0_.refs_7_), channel_id=1, source_target_pairs={{0,1},{1,0},{2,3},{3,2},{4,5},{5,4},{6,7},{7,6},{8,9},{9,8},{10,11... | collective-permute-start | bytes 1572872 | tf_op jit(solution)/shard_map/ppermute | solution.py:35
  51.8 2.5 %collective-permute-start.19 = (f32[1,128]{1,0:T(1,128)S(1)}, f32[1,128]{1,0:T(1,128)S(1)}, u32[]{:S(2)}, u32[]{:S(2)}) collective-permute-start(f32[1,128]{1,0:T(1,128)S(1)} %get-tuple-element.107.refs_4_), channel_id=1, source_target_pairs={{0,1},{1,0},{2,3},{3,2},{4,5},{5,4},{6,7},{7,6},{8,9},{9,8},{10,11... | collective-permute-start | bytes 1544 | tf_op jit(solution)/shard_map/ppermute | solution.py:35
  78.0 10.6 %collective-permute-start.23 = (f32[1024,512]{1,0:T(8,128)S(1)}, f32[1024,512]{1,0:T(8,128)S(1)}, u32[]{:S(2)}, u32[]{:S(2)}) collective-permute-start(f32[1024,512]{1,0:T(8,128)S(1)} %next_logits.3.refs_0_), channel_id=1, source_target_pairs={{0,1},{1,0},{2,3},{3,2},{4,5},{5,4},{6,7},{7,6},{8,9},{9,8},{10,11... | collective-permute-start | bytes 6291464 | tf_op jit(solution)/shard_map/ppermute | solution.py:35
  85.8 2.8 %collective-permute-start.25 = (f32[512,512]{1,0:T(8,128)S(1)}, f32[512,512]{1,0:T(8,128)S(1)}, u32[]{:S(2)}, u32[]{:S(2)}) collective-permute-start(f32[512,512]{1,0:T(8,128)S(1)} %next_logits.5.refs_1_), channel_id=1, source_target_pairs={{0,1},{1,0},{2,3},{3,2},{4,5},{5,4},{6,7},{7,6},{8,9},{9,8},{10,11... | collective-permute-start | bytes 3145736 | tf_op jit(solution)/shard_map/ppermute | solution.py:35
  87.6 2.7 %collective-permute-start.24 = (f32[512,512]{1,0:T(8,128)S(1)}, f32[512,512]{1,0:T(8,128)S(1)}, u32[]{:S(2)}, u32[]{:S(2)}) collective-permute-start(f32[512,512]{1,0:T(8,128)S(1)} %next_logits.4.refs_1_), channel_id=1, source_target_pairs={{0,1},{1,0},{2,3},{3,2},{4,5},{5,4},{6,7},{7,6},{8,9},{9,8},{10,11... | collective-permute-start | bytes 3145736 | tf_op jit(solution)/shard_map/ppermute | solution.py:35

commit v2 on v1

--- a/solution.py
+++ b/solution.py
@@ -286,7 +286,7 @@
     last = len(side) > 0
     shapes = [jax.ShapeDtypeStruct((rows, classes), F32), jax.ShapeDtypeStruct((n, 3 * LANES), F32)]
     if last:
-        shapes.append(jax.ShapeDtypeStruct((n, n, 5 * LANES), F32))
+        shapes.append(jax.ShapeDtypeStruct((lines_of(n)[0], n, 5 * LANES), F32))
     extra = list(side) + list(earlier)
     return pl.pallas_call(
         functools.partial(
@@ -302,13 +302,49 @@
     )(*own, *other, active, *extra, *tokens)
 
 
-def combine(own_ref, all_ref):
-    n = all_ref.shape[0]
+def lines_of(n):
+    return (4, 2) if n == 8 else (n, 1)
+
+
+def merge_kernel(squares, across, all_ref, out_ref):
+    count, n, width = all_ref.shape
+    first = lax.rem(lax.axis_index("example"), across)
     part = lambda d, k: all_ref[d, :, k * LANES : (k + 1) * LANES]
-    peaks = [part(d, 0) for d in range(n)]
-    peak = functools.reduce(jnp.maximum, peaks)
-    scales = [jnp.exp(p - peak) for p in peaks]
-    total = sum(part(d, 1) * scales[d] for d in range(n))
+    peak = functools.reduce(jnp.maximum, [part(d, 0) for d in range(count)])
+    scales = [jnp.exp(part(d, 0) - peak) for d in range(count)]
+    weights = [x * x if squares else 1.0 for x in scales]
+    out_ref[:, 0:LANES] = peak
+    out_ref[:, LANES : 2 * LANES] = sum(part(d, 1) * scales[d] for d in range(count))
+    out_ref[:, 2 * LANES : 3 * LANES] = sum(part(d, 2) * weights[d] for d in range(count))
+    row = lax.broadcasted_iota(jnp.int32, (n, LANES), 0)
+    for k in range(3, width // LANES):
+        own = [jnp.where(row == d * across + first, part(d, k), 0.0) for d in range(count)]
+        out_ref[:, k * LANES : (k + 1) * LANES] = sum(own)
+
+
+def exchange(copies, squares):
+    count, n, width = copies.shape
+    across = lines_of(n)[1]
+    groups = [[d * across + y for d in range(count)] for y in range(across)]
+    every = lax.all_to_all(copies, "example", 0, 0, axis_index_groups=groups)
+    merged = pl.pallas_call(
+        functools.partial(merge_kernel, squares, across),
+        out_shape=jax.ShapeDtypeStruct((n, width), F32),
+        in_specs=[VMEM],
+        out_specs=VMEM,
+        compiler_params=params(),
+        cost_estimate=cost(1, 1),
+        name="merge",
+    )(every)
+    return [merged] + [swap(merged, "example", n, 1)] * (across - 1)
+
+
+def combine(own_ref, sources):
+    part = lambda d, k: sources[d][:, k * LANES : (k + 1) * LANES]
+    count = len(sources)
+    peak = functools.reduce(jnp.maximum, [part(d, 0) for d in range(count)])
+    scales = [jnp.exp(part(d, 0) - peak) for d in range(count)]
+    total = sum(part(d, 1) * scales[d] for d in range(count))
     own_scale = jnp.exp(own_ref[:, 0:LANES] - peak)
     return part, peak, scales, total, own_scale
 
@@ -325,19 +361,20 @@
     return jnp.concatenate([stacked, rest], axis=0).T
 
 
-def first_weights_kernel(entries, parts, own_ref, all_ref, *refs):
+def first_weights_kernel(entries, parts, count, own_ref, *refs):
+    sources, refs = refs[:count], refs[count:]
     e_refs = refs[:parts]
     residual_ref, fisher_ref, damping_ref, target_ref, column_ref, line_ref = refs[parts:]
-    n = all_ref.shape[0]
+    n = own_ref.shape[0]
     classes = residual_ref.shape[1]
     place = lax.axis_index("example")
     class_start = place * classes
-    part, peak, scales, total, own_scale = combine(own_ref, all_ref)
-    square = sum(part(d, 2) * (scales[d] * scales[d]) for d in range(n))
+    part, peak, scales, total, own_scale = combine(own_ref, sources)
+    square = sum(part(d, 2) * (scales[d] * scales[d]) for d in range(count))
     inverse = 1.0 / total
     spread = 1.0 - square * inverse * inverse
-    target = jnp.concatenate([all_ref[d, 0:1, 3 * LANES : 4 * LANES] for d in range(n)], axis=0)
-    norm = jnp.concatenate([all_ref[d, 0:1, 4 * LANES : 5 * LANES] for d in range(n)], axis=0)
+    target = sum(part(d, 3) for d in range(count))
+    norm = sum(part(d, 4) for d in range(count))
     valid = (target >= 0.0).astype(F32)
     share = valid / jnp.sum(valid)
     fisher_sum = jnp.sum(norm * share * spread)
@@ -377,20 +414,20 @@
     classes = e_parts[0].shape[1]
     weight = pltpu.VMEM((n * LANES, classes), BF16)
     return pl.pallas_call(
-        functools.partial(first_weights_kernel, float(entries), len(e_parts)),
+        functools.partial(first_weights_kernel, float(entries), len(e_parts), len(every)),
         out_shape=(
             weight,
             weight,
             jax.ShapeDtypeStruct((8, LANES), F32),
             jax.ShapeDtypeStruct((n, LANES), F32),
         ),
-        in_specs=[VMEM] * (2 + len(e_parts)),
+        in_specs=[VMEM] * (1 + len(every) + len(e_parts)),
         out_specs=(VMEM,) * 4,
         scratch_shapes=[pltpu.VMEM((LANES, LANES), F32), pltpu.VMEM((n, LANES), F32)],
         compiler_params=params(),
         cost_estimate=cost(0, 8 * n * LANES * classes),
         name="first_weights",
-    )(own, every, *e_parts)
+    )(own, *every, *e_parts)
 
 
 def update_kernel(start, tile, turned_ref, squares_ref, w_ref, residual_ref, fisher_ref,
@@ -398,15 +435,24 @@
     features, columns = moved_ref.shape
     damping = damping_ref[0:1, 0:1]
     own = slice(start, start + columns)
-    for k in range(features // tile):
+
+    def settle(k, gradient, fisher):
         at = slice(k * tile, (k + 1) * tile)
-        fisher = jnp.dot(squares_ref[at, :], fisher_ref[:, own], preferred_element_type=F32)
-        gradient = jnp.dot(turned_ref[at, :], residual_ref[:, own], preferred_element_type=F32)
         inverse = 1.0 / (fisher + damping)
         change = gradient * inverse
         inverse_ref[at, :] = inverse
         low_ref[at, :] = (w_ref[at, :] - LEARNING_RATE * change).astype(BF16)
         moved_ref[at, :] = -change
+
+    before = None
+    for k in range(features // tile):
+        at = slice(k * tile, (k + 1) * tile)
+        fisher = jnp.dot(squares_ref[at, :], fisher_ref[:, own], preferred_element_type=F32)
+        if before is not None:
+            settle(*before)
+        gradient = jnp.dot(turned_ref[at, :], residual_ref[:, own], preferred_element_type=F32)
+        before = (k, gradient, fisher)
+    settle(*before)
 
 
 def update(turned, squares, weights, residual, fisher_weight, damping, start):
@@ -505,7 +551,7 @@
         jax.ShapeDtypeStruct((n, 3 * LANES), F32),
     ]
     if last:
-        shapes.append(jax.ShapeDtypeStruct((n, n, 3 * LANES), F32))
+        shapes.append(jax.ShapeDtypeStruct((lines_of(n)[0], n, 3 * LANES), F32))
     return pl.pallas_call(
         functools.partial(
             last_stats_kernel, slot, last, len(own), tuple(offsets), len(earlier)
@@ -520,17 +566,18 @@
     )(*own, *other, target, active, *earlier)
 
 
-def finish_kernel(chunks, e_parts, tile, own_ref, all_ref, target_ref, turned_ref, *refs):
+def finish_kernel(chunks, e_parts, tile, count, own_ref, target_ref, turned_ref, *refs):
+    sources, refs = refs[:count], refs[count:]
     e_refs = refs[:e_parts]
     refs = refs[e_parts:]
     moved_refs, inverse_refs = refs[:chunks], refs[chunks : 2 * chunks]
     out_ref, loss_ref, residual_ref, column_ref, line_ref, held_ref, sems = refs[2 * chunks :]
-    n = all_ref.shape[0]
+    n = own_ref.shape[0]
     classes = residual_ref.shape[1]
     place = lax.axis_index("example")
     class_start = place * classes
-    part, peak, scales, total, own_scale = combine(own_ref, all_ref)
-    label = sum(part(d, 2) for d in range(n))
+    part, peak, scales, total, own_scale = combine(own_ref, sources)
+    label = sum(part(d, 2) for d in range(count))
     target = target_ref[...]
     valid = (target >= 0.0).astype(F32)
     share = valid / jnp.sum(valid)
@@ -582,12 +629,12 @@
     classes = e_parts[0].shape[1]
     tile = 512
     return pl.pallas_call(
-        functools.partial(finish_kernel, len(moved), len(e_parts), tile),
+        functools.partial(finish_kernel, len(moved), len(e_parts), tile, len(every)),
         out_shape=(
             jax.ShapeDtypeStruct((features, classes), F32),
             jax.ShapeDtypeStruct((1, LANES), F32),
         ),
-        in_specs=[VMEM] * (4 + len(e_parts) + 2 * len(moved)),
+        in_specs=[VMEM] * (3 + len(every) + len(e_parts) + 2 * len(moved)),
         out_specs=(ANY, VMEM),
         scratch_shapes=[
             pltpu.VMEM((all_rows, classes), BF16),
@@ -599,11 +646,7 @@
         compiler_params=params(16),
         cost_estimate=cost(2 * all_rows * features * classes),
         name="finish",
-    )(own, every, target, turned, *e_parts, *moved, *inverse)
-
-
-def exchange(copies):
-    return lax.all_to_all(copies, "example", 0, 0)
+    )(own, target, turned, *every, *e_parts, *moved, *inverse)
 
 
 def body(n, n_cls, features, weights, labels, counts, active):
@@ -654,7 +697,7 @@
     for g in range(max(behind - 1, 0), count):
         copies = statistics(g, (logits[-1][0], turned))
     own_stats = stats[-1]
-    every = exchange(copies[0])
+    every = exchange(copies[0], True)
     residual, fisher_weight, damping, target = first_weights(own_stats, every, e_parts, entries)
 
     moved, inverse, own, other = [], [], [], []
@@ -678,7 +721,7 @@
         )
         e_parts.append(e)
         earlier = (own_stats,)
-    every = exchange(copies[0])
+    every = exchange(copies[0], False)
     out, losses = finish(own_stats, every, target, e_parts, turned, moved, inverse)
     return out, losses.reshape(rows)
 

time: 109 us -> 113 us (1.037)
  blocking collectives: 23.1 us -> 18.3 us
  waiting for transfers between devices: 14.9 us -> 19.3 us
  starting transfers between devices: 25.7 us -> 28.8 us
    all_to_all x2, blocking collectives: 23.1 us -> 18.3 us  [exchange(): every = lax.all_to_all(copies, 'example', 0, 0, axis_index_groups=groups)]
    ppermute x19 -> x21, waiting for transfers between devices: 8.02 us -> 12.5 us  [swap(): return lax.ppermute(x, axis, [(i, i ^ offset) for i in range(n)])]
    ppermute x19 -> x21, starting transfers between devices: 10.9 us -> 14.1 us  [swap(): return lax.ppermute(x, axis, [(i, i ^ offset) for i in range(n)])]
  transfers between devices with their start and end apart: 26 -> 28, of which waited for: 11 -> 13; matrix products, arithmetic and copies ran while one was open for 0% -> 0% of each run, Pallas kernels for 21% -> 20%
where the time goes in v2:
time: 113 us; the launch traced here: 112 us
  Pallas kernels  42.6 us (38%)
  starting transfers between devices  28.8 us (25%)
  waiting for transfers between devices  19.3 us (17%)
  blocking collectives  18.3 us (16%)
  between operations  2.35 us (2%)
    all_to_all x2, blocking collectives, exchange(): every = lax.all_to_all(copies, 'example', 0, 0, axis_index_groups=groups)  18.3 us
    ppermute x21, starting transfers between devices, swap(): return lax.ppermute(x, axis, [(i, i ^ offset) for i in range(n)])  14.1 us
    pallas_call x2, Pallas kernels, update(): pl.pallas_call(functools.partial(update_kernel, start, 512), out_shape=(p...  12.7 us
    ppermute x21, waiting for transfers between devices, swap(): return lax.ppermute(x, axis, [(i, i ^ offset) for i in range(n)])  12.5 us
    ppermute x6, starting transfers between devices, gather_blocks(): later.append(lax.ppermute(held[k], 'example', ring))  12.1 us
    pallas_call x1, Pallas kernels, finish(): pl.pallas_call(functools.partial(finish_kernel, len(moved), len(e_parts),...  7.4 us
    ppermute x6, waiting for transfers between devices, gather_blocks(): later.append(lax.ppermute(held[k], 'example', ring))  6.62 us
    pallas_call x5, Pallas kernels, arriving_logits(): pl.pallas_call(functools.partial(arriving_kernel, count, pieces, start),...  5.31 us
  transfers between devices with their start and end apart: 28, of which 13 were waited for; matrix products, arithmetic and copies ran while one was open for 0% of the time, Pallas kernels for 20%

profile of v2, /device:TPU:0, one launch (start us, length us, event | category | flops | bytes accessed | tf_op | source)
XLA Modules:
  0.0 112.5 jit_solution(16121600798394801038)
XLA Ops:
  0.6 1.1 fusion
  1.7 3.1 %collective-permute-start = (bf16[64,2048]{1,0:T(8,128)(2,1)S(1)}, bf16[64,2048]{1,0:T(8,128)(2,1)S(1)}, u32[]{:S(2)}, u32[]{:S(2)}) collective-permute-start(bf16[64,2048]{1,0:T(8,128)(2,1)S(1)} %get-tuple-element.141.refs_0_), channel_id=1, source_target_pairs={{0,4},{2,6},{4,12},{6,14},{12,8},{14,10},{8,0},{10,2},{1,5},{3,7},... | collective-permute-start | bytes 786440 | tf_op jit(solution)/shard_map/ppermute | solution.py:97
  4.8 1.5 %collective-permute-start.4 = (bf16[64,2048]{1,0:T(8,128)(2,1)S(1)}, bf16[64,2048]{1,0:T(8,128)(2,1)S(1)}, u32[]{:S(2)}, u32[]{:S(2)}) collective-permute-start(bf16[64,2048]{1,0:T(8,128)(2,1)S(1)} %get-tuple-element.141.refs_0_), channel_id=1, source_target_pairs={{0,2},{2,0},{4,6},{6,4},{8,10},{10,8},{12,14},{14,12},{1,3},{3,1},... | collective-permute-start | bytes 786440 | tf_op jit(solution)/shard_map/ppermute | solution.py:35
  6.3 2.6 %collective-permute-start.2 = (bf16[64,2048]{1,0:T(8,128)(2,1)S(1)}, bf16[64,2048]{1,0:T(8,128)(2,1)S(1)}, u32[]{:S(2)}, u32[]{:S(2)}) collective-permute-start(bf16[64,2048]{1,0:T(8,128)(2,1)S(1)} %get-tuple-element.140.refs_1_), channel_id=1, source_target_pairs={{0,4},{2,6},{4,12},{6,14},{12,8},{14,10},{8,0},{10,2},{1,5},{3,7},... | collective-permute-start | bytes 786440 | tf_op jit(solution)/shard_map/ppermute | solution.py:97
  8.9 0.5 collective-permute-start.7
  10.7 3.7 %prepare.1 = (f32[2048,512]{1,0:T(8,128)S(1)}, f32[2048,512]{1,0:T(8,128)S(1)}, bf16[2048,1024]{1,0:T(8,128)(2,1)S(1)}, f32[1,128]{1,0:T(1,128)S(1)}, f32[1,128]{1,0:T(1,128)S(1)}) custom-call(f32[2048,1024]{1,0:T(8,128)} %w_ref.1, bf16[128,2048]{1,0:T(8,128)(2,1)} %x_ref.1, s32[1,128]{1,0:T(1,128)} %bitcast.2, s32[1]{0:T(128)S(6)} %copy.31.counts_ref, ...), custom_call_target="tpu_custom_call" | custom-call | flops 1 | bytes 1 | tf_op jit(solution)/shard_map/prepare/pallas_call | solution.py:153
  14.5 1.6 %collective-permute-start.5 = (bf16[64,2048]{1,0:T(8,128)(2,1)S(1)}, bf16[64,2048]{1,0:T(8,128)(2,1)S(1)}, u32[]{:S(2)}, u32[]{:S(2)}) collective-permute-start(bf16[64,2048]{1,0:T(8,128)(2,1)S(1)} %collective-permute-done.refs_5_.refs_0_), channel_id=1, source_target_pairs={{0,2},{2,0},{4,6},{6,4},{8,10},{10,8},{12,14},{14,12},{1,3},{3,1},... | collective-permute-start | bytes 786440 | tf_op jit(solution)/shard_map/ppermute | solution.py:35
  16.0 2.1 %collective-permute-start.1 = (bf16[64,2048]{1,0:T(8,128)(2,1)S(1)}, bf16[64,2048]{1,0:T(8,128)(2,1)S(1)}, u32[]{:S(2)}, u32[]{:S(2)}) collective-permute-start(bf16[64,2048]{1,0:T(8,128)(2,1)S(1)} %collective-permute-done.refs_5_.refs_0_), channel_id=1, source_target_pairs={{0,4},{2,6},{4,12},{6,14},{12,8},{14,10},{8,0},{10,2},{1,5},{3,7},... | collective-permute-start | bytes 786440 | tf_op jit(solution)/shard_map/ppermute | solution.py:97
  18.1 1.6 %collective-permute-start.3 = (bf16[64,2048]{1,0:T(8,128)(2,1)S(1)}, bf16[64,2048]{1,0:T(8,128)(2,1)S(1)}, u32[]{:S(2)}, u32[]{:S(2)}) collective-permute-start(bf16[64,2048]{1,0:T(8,128)(2,1)S(1)} %collective-permute-done.2.refs_6_.refs_1_), channel_id=1, source_target_pairs={{0,4},{2,6},{4,12},{6,14},{12,8},{14,10},{8,0},{10,2},{1,5},{3,7},... | collective-permute-start | bytes 786440 | tf_op jit(solution)/shard_map/ppermute | solution.py:97
  19.7 1.5 %collective-permute-start.8 = (bf16[64,2048]{1,0:T(8,128)(2,1)S(1)}, bf16[64,2048]{1,0:T(8,128)(2,1)S(1)}, u32[]{:S(2)}, u32[]{:S(2)}) collective-permute-start(bf16[64,2048]{1,0:T(8,128)(2,1)S(1)} %collective-permute-done.2.refs_6_.refs_1_), channel_id=1, source_target_pairs={{0,2},{2,0},{4,6},{6,4},{8,10},{10,8},{12,14},{14,12},{1,3},{3,1},... | collective-permute-start | bytes 786440 | tf_op jit(solution)/shard_map/ppermute | solution.py:35
  21.2 4.0 %collective-permute-done.5.refs_2_ = bf16[64,2048]{1,0:T(8,128)(2,1)S(1)} collective-permute-done((bf16[64,2048]{1,0:T(8,128)(2,1)S(1)}, bf16[64,2048]{1,0:T(8,128)(2,1)S(1)}, u32[]{:S(2)}, u32[]{:S(2)}) %collective-permute-start.5) | collective-permute-done | bytes 262176 | tf_op jit(solution)/shard_map/ppermute | solution.py:35
  25.2 0.9 collective-permute-done.1.refs_8_.refs_0_
  26.2 0.6 collective-permute-start.6
  26.8 2.6 %collective-permute-start.14 = (bf16[64,2048]{1,0:T(8,128)(2,1)S(1)}, bf16[64,2048]{1,0:T(8,128)(2,1)S(1)}, u32[]{:S(2)}, u32[]{:S(2)}) collective-permute-start(bf16[64,2048]{1,0:T(8,128)(2,1)S(1)} %collective-permute-done.1.refs_8_.refs_0_), channel_id=1, source_target_pairs={{0,4},{2,6},{4,12},{6,14},{12,8},{14,10},{8,0},{10,2},{1,5},{3,7},... | collective-permute-start | bytes 786440 | tf_op jit(solution)/shard_map/ppermute | solution.py:97
  29.4 1.8 %collective-permute-done.3.refs_9_.refs_1_ = bf16[64,2048]{1,0:T(8,128)(2,1)S(1)} collective-permute-done((bf16[64,2048]{1,0:T(8,128)(2,1)S(1)}, bf16[64,2048]{1,0:T(8,128)(2,1)S(1)}, u32[]{:S(2)}, u32[]{:S(2)}) %collective-permute-start.3) | collective-permute-done | bytes 262176 | tf_op jit(solution)/shard_map/ppermute | solution.py:97
  31.4 1.3 %arriving_logits.5 = (bf16[1024,2048]{1,0:T(8,128)(2,1)S(1)}, f32[64,1024]{1,0:T(8,128)S(1)}, f32[64,1024]{1,0:T(8,128)S(1)}, f32[64,1024]{1,0:T(8,128)S(1)}, f32[64,1024]{1,0:T(8,128)S(1)}) custom-call(bf16[64,2048]{1,0:T(8,128)(2,1)S(1)} %get-tuple-element.141.refs_0_, bf16[64,2048]{1,0:T(8,128)(2,1)S(1)} %get-tuple-element.140.refs_1_, ...), custom_call_target="tpu_custom_call" | custom-call | flops 1 | bytes 1 | tf_op jit(solution)/shard_map/arriving_logits/pallas_call | solution.py:195
  32.7 1.7 %collective-permute-start.9 = (bf16[64,2048]{1,0:T(8,128)(2,1)S(1)}, bf16[64,2048]{1,0:T(8,128)(2,1)S(1)}, u32[]{:S(2)}, u32[]{:S(2)}) collective-permute-start(bf16[64,2048]{1,0:T(8,128)(2,1)S(1)} %collective-permute-done.3.refs_9_.refs_1_), channel_id=1, source_target_pairs={{0,2},{2,0},{4,6},{6,4},{8,10},{10,8},{12,14},{14,12},{1,3},{3,1},... | collective-permute-start | bytes 786440 | tf_op jit(solution)/shard_map/ppermute | solution.py:35
  34.3 2.1 %collective-permute-done.6.refs_2_.refs_0_ = bf16[64,2048]{1,0:T(8,128)(2,1)S(1)} collective-permute-done((bf16[64,2048]{1,0:T(8,128)(2,1)S(1)}, bf16[64,2048]{1,0:T(8,128)(2,1)S(1)}, u32[]{:S(2)}, u32[]{:S(2)}) %collective-permute-start.6) | collective-permute-done | bytes 262176 | tf_op jit(solution)/shard_map/ppermute | solution.py:35
  36.5 0.4 collective-permute-done.14.refs_8_.refs_0_
  37.0 3.4 %collective-permute-done.15.refs_9_.refs_1_.refs_0_ = bf16[64,2048]{1,0:T(8,128)(2,1)S(1)} collective-permute-done((bf16[64,2048]{1,0:T(8,128)(2,1)S(1)}, bf16[64,2048]{1,0:T(8,128)(2,1)S(1)}, u32[]{:S(2)}, u32[]{:S(2)}) %collective-permute-start.15) | collective-permute-done | bytes 262176 | tf_op jit(solution)/shard_map/ppermute | solution.py:97
  40.7 2.6 %collective-permute-start.17 = (bf16[64,2048]{1,0:T(8,128)(2,1)S(1)}, bf16[64,2048]{1,0:T(8,128)(2,1)S(1)}, u32[]{:S(2)}, u32[]{:S(2)}) collective-permute-start(bf16[64,2048]{1,0:T(8,128)(2,1)S(1)} %relay.3), channel_id=1, source_target_pairs={{0,4},{2,6},{4,12},{6,14},{12,8},{14,10},{8,0},{10,2},{1,5},{3,7},... | collective-permute-start | bytes 786440 | tf_op jit(solution)/shard_map/ppermute | solution.py:111
  43.3 1.6 %collective-permute-start.16 = (bf16[64,2048]{1,0:T(8,128)(2,1)S(1)}, bf16[64,2048]{1,0:T(8,128)(2,1)S(1)}, u32[]{:S(2)}, u32[]{:S(2)}) collective-permute-start(bf16[64,2048]{1,0:T(8,128)(2,1)S(1)} %relay.2), channel_id=1, source_target_pairs={{0,2},{2,0},{4,6},{6,4},{8,10},{10,8},{12,14},{14,12},{1,3},{3,1},... | collective-permute-start | bytes 786440 | tf_op jit(solution)/shard_map/ppermute | solution.py:35
  45.3 0.5 first_stats.5
  45.8 1.3 %arriving_logits.6 = (bf16[1024,2048]{1,0:T(8,128)(2,1)S(1)}, f32[256,1024]{1,0:T(8,128)S(1)}) custom-call(bf16[64,2048]{1,0:T(8,128)(2,1)S(1)} %collective-permute-done.refs_5_.refs_0_, bf16[64,2048]{1,0:T(8,128)(2,1)S(1)} %collective-permute-done.2.refs_6_.refs_1_, ...), custom_call_target="tpu_custom_call", output_to_operand_aliasing={{0}: (5, {})} | custom-call | flops 1 | bytes 1 | tf_op jit(solution)/shard_map/arriving_logits/pallas_call | solution.py:195
  47.5 1.3 %arriving_logits.7 = (bf16[1024,2048]{1,0:T(8,128)(2,1)S(1)}, f32[256,1024]{1,0:T(8,128)S(1)}) custom-call(bf16[64,2048]{1,0:T(8,128)(2,1)S(1)} %collective-permute-done.1.refs_8_.refs_0_, bf16[64,2048]{1,0:T(8,128)(2,1)S(1)} %collective-permute-done.3.refs_9_.refs_1_, ...), custom_call_target="tpu_custom_call", output_to_operand_aliasing={{0}: (5, {})} | custom-call | flops 1 | bytes 1 | tf_op jit(solution)/shard_map/arriving_logits/pallas_call | solution.py:195
  49.2 0.7 arriving_logits.8
  50.7 0.7 arriving_logits.9
  51.4 0.4 collective-permute-start.18
  52.4 0.5 first_stats.6
  52.9 0.5 first_stats.7
  53.9 0.4 collective-permute-done.19.refs_5_
  54.6 10.3 %all_to_all.10.all_ref = f32[4,8,640]{2,1,0:T(8,128)S(1)} all-to-all(f32[4,8,640]{2,1,0:T(8,128)S(1)} %get-tuple-element.116), channel_id=1, replica_groups={{0,4,8,12},{2,6,10,14},{1,5,9,13},{3,7,11,15},{16,20,24,28},{18,22,26,3..., dimensions={0} | all-to-all | bytes 163840 | tf_op jit(solution)/shard_map/all_to_all | solution.py:329
  64.9 1.6 %collective-permute-start.23 = (f32[8,640]{1,0:T(8,128)S(1)}, f32[8,640]{1,0:T(8,128)S(1)}, u32[]{:S(2)}, u32[]{:S(2)}) collective-permute-start(f32[8,640]{1,0:T(8,128)S(1)} %merge.2.refs_0_), channel_id=1, source_target_pairs={{0,2},{2,0},{4,6},{6,4},{8,10},{10,8},{12,14},{14,12},{1,3},{3,1},... | collective-permute-start | bytes 61448 | tf_op jit(solution)/shard_map/ppermute | solution.py:35
  66.5 2.3 %collective-permute-done.23.refs_1_ = f32[8,640]{1,0:T(8,128)S(1)} collective-permute-done((f32[8,640]{1,0:T(8,128)S(1)}, f32[8,640]{1,0:T(8,128)S(1)}, u32[]{:S(2)}, u32[]{:S(2)}) %collective-permute-start.23) | collective-permute-done | bytes 20512 | tf_op jit(solution)/shard_map/ppermute | solution.py:35
  68.8 1.6 %first_weights.1 = (bf16[1024,1024]{1,0:T(8,128)(2,1)S(1)}, bf16[1024,1024]{1,0:T(8,128)(2,1)S(1)}, f32[8,128]{1,0:T(8,128)S(1)}, f32[8,128]{1,0:T(8,128)S(1)}) custom-call(f32[8,384]{1,0:T(8,128)S(1)} %get-tuple-element.115.own_ref, f32[8,640]{1,0:T(8,128)S(1)} %merge.2.refs_0_, f32[8,640]{1,0:T(8,128)S(1)} %collective-permute-done.23.refs_1_, ...), custom_call_target="tpu_custom_call" | custom-call | bytes 8388608 | tf_op jit(solution)/shard_map/first_weights/pallas_call | solution.py:416
  70.4 6.2 %update.2 = (f32[2048,512]{1,0:T(8,128)S(1)}, f32[2048,512]{1,0:T(8,128)S(1)}, bf16[2048,512]{1,0:T(8,128)(2,1)S(1)}) custom-call(bf16[2048,1024]{1,0:T(8,128)(2,1)S(1)} %get-tuple-element.102.refs_5_.refs_8_.turned_ref, bf16[2048,1024]{1,0:T(8,128)(2,1)S(1)} %get-tuple-element.103.squares_ref, ...), custom_call_target="tpu_custom_call", output_to_operand_aliasing={{0}: (2, {})} | custom-call | flops 4294967296 | tf_op jit(solution)/shard_map/update/pallas_call | solution.py:461
  76.7 2.3 %next_logits.3.refs_0_ = f32[1024,512]{1,0:T(8,128)S(1)} custom-call(bf16[1024,2048]{1,0:T(8,128)(2,1)S(1)} %get-tuple-element.100.plain_ref, bf16[2048,512]{1,0:T(8,128)(2,1)S(1)} %get-tuple-element.125.low_ref), custom_call_target="tpu_custom_call" | custom-call | flops 2147483648 | tf_op jit(solution)/shard_map/next_logits/pallas_call | solution.py:488
  79.1 6.5 %update.3 = (f32[2048,512]{1,0:T(8,128)S(1)}, f32[2048,512]{1,0:T(8,128)S(1)}, bf16[2048,512]{1,0:T(8,128)(2,1)S(1)}) custom-call(bf16[2048,1024]{1,0:T(8,128)(2,1)S(1)} %get-tuple-element.102.refs_5_.refs_8_.turned_ref, bf16[2048,1024]{1,0:T(8,128)(2,1)S(1)} %get-tuple-element.103.squares_ref, ...), custom_call_target="tpu_custom_call", output_to_operand_aliasing={{0}: (2, {})} | custom-call | flops 4294967296 | tf_op jit(solution)/shard_map/update/pallas_call | solution.py:461
  85.6 1.2 %next_logits.5.refs_1_ = f32[512,512]{1,0:T(8,128)S(1)} custom-call(bf16[1024,2048]{1,0:T(8,128)(2,1)S(1)} %get-tuple-element.100.plain_ref, bf16[2048,512]{1,0:T(8,128)(2,1)S(1)} %get-tuple-element.127.low_ref), custom_call_target="tpu_custom_call" | custom-call | flops 1073741824 | tf_op jit(solution)/shard_map/next_logits/pallas_call | solution.py:488
  86.8 0.6 collective-permute-start.26
  87.4 1.2 %next_logits.4.refs_1_ = f32[512,512]{1,0:T(8,128)S(1)} custom-call(bf16[1024,2048]{1,0:T(8,128)(2,1)S(1)} %get-tuple-element.100.plain_ref, bf16[2048,512]{1,0:T(8,128)(2,1)S(1)} %get-tuple-element.127.low_ref), custom_call_target="tpu_custom_call" | custom-call | flops 1073741824 | tf_op jit(solution)/shard_map/next_logits/pallas_call | solution.py:488
  88.7 1.0 collective-permute-done.26.refs_3_
  89.7 1.7 %last_stats.2 = (f32[512,1024]{1,0:T(8,128)S(1)}, f32[8,384]{1,0:T(8,128)S(1)}) custom-call(f32[1024,512]{1,0:T(8,128)S(1)} %next_logits.3.refs_0_, f32[512,512]{1,0:T(8,128)S(1)} %next_logits.5.refs_1_, f32[1024,512]{1,0:T(8,128)S(1)} %collective-permute-done.24.refs_2_, f32[512,512]{1,0:T(8,128)S(1)} %collective-permute-done.26.refs_3_, ...), custom_call_target="tpu_custom_call" | custom-call | bytes 12582912 | tf_op jit(solution)/shard_map/last_stats/pallas_call | solution.py:555
  91.4 1.7 %last_stats.3 = (f32[512,1024]{1,0:T(8,128)S(1)}, f32[8,384]{1,0:T(8,128)S(1)}, f32[4,8,384]{2,1,0:T(8,128)S(1)}) custom-call(f32[1024,512]{1,0:T(8,128)S(1)} %next_logits.3.refs_0_, f32[512,512]{1,0:T(8,128)S(1)} %next_logits.4.refs_1_, f32[1024,512]{1,0:T(8,128)S(1)} %collective-permute-done.24.refs_2_, f32[512,512]{1,0:T(8,128)S(1)} %collective-permute-done.25.refs_3_, ...), custom_call_target="tpu_custom_call" | custom-call | bytes 12582912 | tf_op jit(solution)/shard_map/last_stats/pallas_call | solution.py:555
  93.1 8.1 %all_to_all.11.all_ref = f32[4,8,384]{2,1,0:T(8,128)S(1)} all-to-all(f32[4,8,384]{2,1,0:T(8,128)S(1)} %get-tuple-element.131), channel_id=1, replica_groups={{0,4,8,12},{2,6,10,14},{1,5,9,13},{3,7,11,15},{16,20,24,28},{18,22,26,3..., dimensions={0} | all-to-all | bytes 98304 | tf_op jit(solution)/shard_map/all_to_all | solution.py:329
  101.1 1.6 %collective-permute-start.27 = (f32[8,384]{1,0:T(8,128)S(1)}, f32[8,384]{1,0:T(8,128)S(1)}, u32[]{:S(2)}, u32[]{:S(2)}) collective-permute-start(f32[8,384]{1,0:T(8,128)S(1)} %merge.3.refs_0_), channel_id=1, source_target_pairs={{0,2},{2,0},{4,6},{6,4},{8,10},{10,8},{12,14},{14,12},{1,3},{3,1},... | collective-permute-start | bytes 36872 | tf_op jit(solution)/shard_map/ppermute | solution.py:35
  102.7 2.2 %collective-permute-done.27.refs_1_ = f32[8,384]{1,0:T(8,128)S(1)} collective-permute-done((f32[8,384]{1,0:T(8,128)S(1)}, f32[8,384]{1,0:T(8,128)S(1)}, u32[]{:S(2)}, u32[]{:S(2)}) %collective-permute-start.27) | collective-permute-done | bytes 12320 | tf_op jit(solution)/shard_map/ppermute | solution.py:35
  104.9 7.4 %finish.1 = (f32[2048,1024]{1,0:T(8,128)}, f32[1,128]{1,0:T(1,128)}) custom-call(f32[8,384]{1,0:T(8,128)S(1)} %get-tuple-element.130.own_ref, f32[8,128]{1,0:T(8,128)S(1)} %get-tuple-element.128.refs_4_.target_ref, bf16[2048,1024]{1,0:T(8,128)(2,1)S(1)} %get-tuple-element.102.refs_5_.refs_8_.turned_ref, f32[8,384]{1,0:T(8,128)S(1)} %merge.3.refs_0_, ...), custom_call_target="tpu_custom_call" | custom-call | flops 4294967296 | tf_op jit(solution)/shard_map/finish/pallas_call | solution.py:631
  (43 shorter events, 4.0 us)
Async XLA Ops:
  1.7 12.7 %collective-permute-start = (bf16[64,2048]{1,0:T(8,128)(2,1)S(1)}, bf16[64,2048]{1,0:T(8,128)(2,1)S(1)}, u32[]{:S(2)}, u32[]{:S(2)}) collective-permute-start(bf16[64,2048]{1,0:T(8,128)(2,1)S(1)} %get-tuple-element.141.refs_0_), channel_id=1, source_target_pairs={{0,4},{2,6},{4,12},{6,14},{12,8},{14,10},{8,0},{10,2},{1,5},{3,7},... | collective-permute-start | bytes 786440 | tf_op jit(solution)/shard_map/ppermute | solution.py:97
  4.8 9.7 %collective-permute-start.4 = (bf16[64,2048]{1,0:T(8,128)(2,1)S(1)}, bf16[64,2048]{1,0:T(8,128)(2,1)S(1)}, u32[]{:S(2)}, u32[]{:S(2)}) collective-permute-start(bf16[64,2048]{1,0:T(8,128)(2,1)S(1)} %get-tuple-element.141.refs_0_), channel_id=1, source_target_pairs={{0,2},{2,0},{4,6},{6,4},{8,10},{10,8},{12,14},{14,12},{1,3},{3,1},... | collective-permute-start | bytes 786440 | tf_op jit(solution)/shard_map/ppermute | solution.py:35
  6.3 11.8 %collective-permute-start.2 = (bf16[64,2048]{1,0:T(8,128)(2,1)S(1)}, bf16[64,2048]{1,0:T(8,128)(2,1)S(1)}, u32[]{:S(2)}, u32[]{:S(2)}) collective-permute-start(bf16[64,2048]{1,0:T(8,128)(2,1)S(1)} %get-tuple-element.140.refs_1_), channel_id=1, source_target_pairs={{0,4},{2,6},{4,12},{6,14},{12,8},{14,10},{8,0},{10,2},{1,5},{3,7},... | collective-permute-start | bytes 786440 | tf_op jit(solution)/shard_map/ppermute | solution.py:97
  8.9 10.8 %collective-permute-start.7 = (bf16[64,2048]{1,0:T(8,128)(2,1)S(1)}, bf16[64,2048]{1,0:T(8,128)(2,1)S(1)}, u32[]{:S(2)}, u32[]{:S(2)}) collective-permute-start(bf16[64,2048]{1,0:T(8,128)(2,1)S(1)} %get-tuple-element.140.refs_1_), channel_id=1, source_target_pairs={{0,2},{2,0},{4,6},{6,4},{8,10},{10,8},{12,14},{14,12},{1,3},{3,1},... | collective-permute-start | bytes 786440 | tf_op jit(solution)/shard_map/ppermute | solution.py:35
  14.5 10.8 %collective-permute-start.5 = (bf16[64,2048]{1,0:T(8,128)(2,1)S(1)}, bf16[64,2048]{1,0:T(8,128)(2,1)S(1)}, u32[]{:S(2)}, u32[]{:S(2)}) collective-permute-start(bf16[64,2048]{1,0:T(8,128)(2,1)S(1)} %collective-permute-done.refs_5_.refs_0_), channel_id=1, source_target_pairs={{0,2},{2,0},{4,6},{6,4},{8,10},{10,8},{12,14},{14,12},{1,3},{3,1},... | collective-permute-start | bytes 786440 | tf_op jit(solution)/shard_map/ppermute | solution.py:35
  16.0 10.1 %collective-permute-start.1 = (bf16[64,2048]{1,0:T(8,128)(2,1)S(1)}, bf16[64,2048]{1,0:T(8,128)(2,1)S(1)}, u32[]{:S(2)}, u32[]{:S(2)}) collective-permute-start(bf16[64,2048]{1,0:T(8,128)(2,1)S(1)} %collective-permute-done.refs_5_.refs_0_), channel_id=1, source_target_pairs={{0,4},{2,6},{4,12},{6,14},{12,8},{14,10},{8,0},{10,2},{1,5},{3,7},... | collective-permute-start | bytes 786440 | tf_op jit(solution)/shard_map/ppermute | solution.py:97
  18.1 13.0 %collective-permute-start.3 = (bf16[64,2048]{1,0:T(8,128)(2,1)S(1)}, bf16[64,2048]{1,0:T(8,128)(2,1)S(1)}, u32[]{:S(2)}, u32[]{:S(2)}) collective-permute-start(bf16[64,2048]{1,0:T(8,128)(2,1)S(1)} %collective-permute-done.2.refs_6_.refs_1_), channel_id=1, source_target_pairs={{0,4},{2,6},{4,12},{6,14},{12,8},{14,10},{8,0},{10,2},{1,5},{3,7},... | collective-permute-start | bytes 786440 | tf_op jit(solution)/shard_map/ppermute | solution.py:97
  19.7 13.0 %collective-permute-start.8 = (bf16[64,2048]{1,0:T(8,128)(2,1)S(1)}, bf16[64,2048]{1,0:T(8,128)(2,1)S(1)}, u32[]{:S(2)}, u32[]{:S(2)}) collective-permute-start(bf16[64,2048]{1,0:T(8,128)(2,1)S(1)} %collective-permute-done.2.refs_6_.refs_1_), channel_id=1, source_target_pairs={{0,2},{2,0},{4,6},{6,4},{8,10},{10,8},{12,14},{14,12},{1,3},{3,1},... | collective-permute-start | bytes 786440 | tf_op jit(solution)/shard_map/ppermute | solution.py:35
  26.2 10.3 %collective-permute-start.6 = (bf16[64,2048]{1,0:T(8,128)(2,1)S(1)}, bf16[64,2048]{1,0:T(8,128)(2,1)S(1)}, u32[]{:S(2)}, u32[]{:S(2)}) collective-permute-start(bf16[64,2048]{1,0:T(8,128)(2,1)S(1)} %collective-permute-done.1.refs_8_.refs_0_), channel_id=1, source_target_pairs={{0,2},{2,0},{4,6},{6,4},{8,10},{10,8},{12,14},{14,12},{1,3},{3,1},... | collective-permute-start | bytes 786440 | tf_op jit(solution)/shard_map/ppermute | solution.py:35
  26.8 10.1 %collective-permute-start.14 = (bf16[64,2048]{1,0:T(8,128)(2,1)S(1)}, bf16[64,2048]{1,0:T(8,128)(2,1)S(1)}, u32[]{:S(2)}, u32[]{:S(2)}) collective-permute-start(bf16[64,2048]{1,0:T(8,128)(2,1)S(1)} %collective-permute-done.1.refs_8_.refs_0_), channel_id=1, source_target_pairs={{0,4},{2,6},{4,12},{6,14},{12,8},{14,10},{8,0},{10,2},{1,5},{3,7},... | collective-permute-start | bytes 786440 | tf_op jit(solution)/shard_map/ppermute | solution.py:97
  31.2 9.3 %collective-permute-start.15 = (bf16[64,2048]{1,0:T(8,128)(2,1)S(1)}, bf16[64,2048]{1,0:T(8,128)(2,1)S(1)}, u32[]{:S(2)}, u32[]{:S(2)}) collective-permute-start(bf16[64,2048]{1,0:T(8,128)(2,1)S(1)} %collective-permute-done.3.refs_9_.refs_1_), channel_id=1, source_target_pairs={{0,4},{2,6},{4,12},{6,14},{12,8},{14,10},{8,0},{10,2},{1,5},{3,7},... | collective-permute-start | bytes 786440 | tf_op jit(solution)/shard_map/ppermute | solution.py:97
  32.7 8.0 %collective-permute-start.9 = (bf16[64,2048]{1,0:T(8,128)(2,1)S(1)}, bf16[64,2048]{1,0:T(8,128)(2,1)S(1)}, u32[]{:S(2)}, u32[]{:S(2)}) collective-permute-start(bf16[64,2048]{1,0:T(8,128)(2,1)S(1)} %collective-permute-done.3.refs_9_.refs_1_), channel_id=1, source_target_pairs={{0,2},{2,0},{4,6},{6,4},{8,10},{10,8},{12,14},{14,12},{1,3},{3,1},... | collective-permute-start | bytes 786440 | tf_op jit(solution)/shard_map/ppermute | solution.py:35
  34.3 9.0 %collective-permute-start.10 = (f32[64,1024]{1,0:T(8,128)S(1)}, f32[64,1024]{1,0:T(8,128)S(1)}, u32[]{:S(2)}, u32[]{:S(2)}) collective-permute-start(f32[64,1024]{1,0:T(8,128)S(1)} %get-tuple-element.83.refs_0_), channel_id=1, source_target_pairs={{0,1},{1,0},{2,3},{3,2},{4,5},{5,4},{6,7},{7,6},{8,9},{9,8},{10,11... | collective-permute-start | bytes 786440 | tf_op jit(solution)/shard_map/ppermute | solution.py:35
  36.5 8.8 %collective-permute-start.11 = (f32[64,1024]{1,0:T(8,128)S(1)}, f32[64,1024]{1,0:T(8,128)S(1)}, u32[]{:S(2)}, u32[]{:S(2)}) collective-permute-start(f32[64,1024]{1,0:T(8,128)S(1)} %get-tuple-element.84.refs_1_), channel_id=1, source_target_pairs={{0,1},{1,0},{2,3},{3,2},{4,5},{5,4},{6,7},{7,6},{8,9},{9,8},{10,11... | collective-permute-start | bytes 786440 | tf_op jit(solution)/shard_map/ppermute | solution.py:35
  36.9 8.4 %collective-permute-start.12 = (f32[64,1024]{1,0:T(8,128)S(1)}, f32[64,1024]{1,0:T(8,128)S(1)}, u32[]{:S(2)}, u32[]{:S(2)}) collective-permute-start(f32[64,1024]{1,0:T(8,128)S(1)} %get-tuple-element.85.refs_2_), channel_id=1, source_target_pairs={{0,1},{1,0},{2,3},{3,2},{4,5},{5,4},{6,7},{7,6},{8,9},{9,8},{10,11... | collective-permute-start | bytes 786440 | tf_op jit(solution)/shard_map/ppermute | solution.py:35
  40.4 4.9 %collective-permute-start.13 = (f32[64,1024]{1,0:T(8,128)S(1)}, f32[64,1024]{1,0:T(8,128)S(1)}, u32[]{:S(2)}, u32[]{:S(2)}) collective-permute-start(f32[64,1024]{1,0:T(8,128)S(1)} %get-tuple-element.86.refs_3_), channel_id=1, source_target_pairs={{0,1},{1,0},{2,3},{3,2},{4,5},{5,4},{6,7},{7,6},{8,9},{9,8},{10,11... | collective-permute-start | bytes 786440 | tf_op jit(solution)/shard_map/ppermute | solution.py:35
  40.7 9.5 %collective-permute-start.17 = (bf16[64,2048]{1,0:T(8,128)(2,1)S(1)}, bf16[64,2048]{1,0:T(8,128)(2,1)S(1)}, u32[]{:S(2)}, u32[]{:S(2)}) collective-permute-start(bf16[64,2048]{1,0:T(8,128)(2,1)S(1)} %relay.3), channel_id=1, source_target_pairs={{0,4},{2,6},{4,12},{6,14},{12,8},{14,10},{8,0},{10,2},{1,5},{3,7},... | collective-permute-start | bytes 786440 | tf_op jit(solution)/shard_map/ppermute | solution.py:111
  43.3 6.8 %collective-permute-start.16 = (bf16[64,2048]{1,0:T(8,128)(2,1)S(1)}, bf16[64,2048]{1,0:T(8,128)(2,1)S(1)}, u32[]{:S(2)}, u32[]{:S(2)}) collective-permute-start(bf16[64,2048]{1,0:T(8,128)(2,1)S(1)} %relay.2), channel_id=1, source_target_pairs={{0,2},{2,0},{4,6},{6,4},{8,10},{10,8},{12,14},{14,12},{1,3},{3,1},... | collective-permute-start | bytes 786440 | tf_op jit(solution)/shard_map/ppermute | solution.py:35
  47.1 5.3 %collective-permute-start.22 = (f32[256,1024]{1,0:T(8,128)S(1)}, f32[256,1024]{1,0:T(8,128)S(1)}, u32[]{:S(2)}, u32[]{:S(2)}) collective-permute-start(f32[256,1024]{1,0:T(8,128)S(1)} %get-tuple-element.111.refs_0_), channel_id=1, source_target_pairs={{0,1},{1,0},{2,3},{3,2},{4,5},{5,4},{6,7},{7,6},{8,9},{9,8},{10,11... | collective-permute-start | bytes 3145736 | tf_op jit(solution)/shard_map/ppermute | solution.py:35
  50.2 2.7 %collective-permute-start.21 = (f32[256,1024]{1,0:T(8,128)S(1)}, f32[256,1024]{1,0:T(8,128)S(1)}, u32[]{:S(2)}, u32[]{:S(2)}) collective-permute-start(f32[256,1024]{1,0:T(8,128)S(1)} %get-tuple-element.109.refs_0_), channel_id=1, source_target_pairs={{0,1},{1,0},{2,3},{3,2},{4,5},{5,4},{6,7},{7,6},{8,9},{9,8},{10,11... | collective-permute-start | bytes 3145736 | tf_op jit(solution)/shard_map/ppermute | solution.py:35
  50.5 3.1 %collective-permute-start.20 = (f32[128,1024]{1,0:T(8,128)S(1)}, f32[128,1024]{1,0:T(8,128)S(1)}, u32[]{:S(2)}, u32[]{:S(2)}) collective-permute-start(f32[128,1024]{1,0:T(8,128)S(1)} %get-tuple-element.108.refs_0_), channel_id=1, source_target_pairs={{0,1},{1,0},{2,3},{3,2},{4,5},{5,4},{6,7},{7,6},{8,9},{9,8},{10,11... | collective-permute-start | bytes 1572872 | tf_op jit(solution)/shard_map/ppermute | solution.py:35
  51.4 2.9 %collective-permute-start.18 = (f32[128,1024]{1,0:T(8,128)S(1)}, f32[128,1024]{1,0:T(8,128)S(1)}, u32[]{:S(2)}, u32[]{:S(2)}) collective-permute-start(f32[128,1024]{1,0:T(8,128)S(1)} %get-tuple-element.105.refs_4_.refs_0_.refs_7_), channel_id=1, source_target_pairs={{0,1},{1,0},{2,3},{3,2},{4,5},{5,4},{6,7},{7,6},{8,9},{9,8},{10,11... | collective-permute-start | bytes 1572872 | tf_op jit(solution)/shard_map/ppermute | solution.py:35
  51.8 2.5 %collective-permute-start.19 = (f32[1,128]{1,0:T(1,128)S(1)}, f32[1,128]{1,0:T(1,128)S(1)}, u32[]{:S(2)}, u32[]{:S(2)}) collective-permute-start(f32[1,128]{1,0:T(1,128)S(1)} %get-tuple-element.107.refs_4_), channel_id=1, source_target_pairs={{0,1},{1,0},{2,3},{3,2},{4,5},{5,4},{6,7},{7,6},{8,9},{9,8},{10,11... | collective-permute-start | bytes 1544 | tf_op jit(solution)/shard_map/ppermute | solution.py:35
  64.9 3.8 %collective-permute-start.23 = (f32[8,640]{1,0:T(8,128)S(1)}, f32[8,640]{1,0:T(8,128)S(1)}, u32[]{:S(2)}, u32[]{:S(2)}) collective-permute-start(f32[8,640]{1,0:T(8,128)S(1)} %merge.2.refs_0_), channel_id=1, source_target_pairs={{0,2},{2,0},{4,6},{6,4},{8,10},{10,8},{12,14},{14,12},{1,3},{3,1},... | collective-permute-start | bytes 61448 | tf_op jit(solution)/shard_map/ppermute | solution.py:35
  79.0 10.7 %collective-permute-start.24 = (f32[1024,512]{1,0:T(8,128)S(1)}, f32[1024,512]{1,0:T(8,128)S(1)}, u32[]{:S(2)}, u32[]{:S(2)}) collective-permute-start(f32[1024,512]{1,0:T(8,128)S(1)} %next_logits.3.refs_0_), channel_id=1, source_target_pairs={{0,1},{1,0},{2,3},{3,2},{4,5},{5,4},{6,7},{7,6},{8,9},{9,8},{10,11... | collective-permute-start | bytes 6291464 | tf_op jit(solution)/shard_map/ppermute | solution.py:35
  86.8 2.8 %collective-permute-start.26 = (f32[512,512]{1,0:T(8,128)S(1)}, f32[512,512]{1,0:T(8,128)S(1)}, u32[]{:S(2)}, u32[]{:S(2)}) collective-permute-start(f32[512,512]{1,0:T(8,128)S(1)} %next_logits.5.refs_1_), channel_id=1, source_target_pairs={{0,1},{1,0},{2,3},{3,2},{4,5},{5,4},{6,7},{7,6},{8,9},{9,8},{10,11... | collective-permute-start | bytes 3145736 | tf_op jit(solution)/shard_map/ppermute | solution.py:35
  88.6 2.7 %collective-permute-start.25 = (f32[512,512]{1,0:T(8,128)S(1)}, f32[512,512]{1,0:T(8,128)S(1)}, u32[]{:S(2)}, u32[]{:S(2)}) collective-permute-start(f32[512,512]{1,0:T(8,128)S(1)} %next_logits.4.refs_1_), channel_id=1, source_target_pairs={{0,1},{1,0},{2,3},{3,2},{4,5},{5,4},{6,7},{7,6},{8,9},{9,8},{10,11... | collective-permute-start | bytes 3145736 | tf_op jit(solution)/shard_map/ppermute | solution.py:35
  101.1 3.8 %collective-permute-start.27 = (f32[8,384]{1,0:T(8,128)S(1)}, f32[8,384]{1,0:T(8,128)S(1)}, u32[]{:S(2)}, u32[]{:S(2)}) collective-permute-start(f32[8,384]{1,0:T(8,128)S(1)} %merge.3.refs_0_), channel_id=1, source_target_pairs={{0,2},{2,0},{4,6},{6,4},{8,10},{10,8},{12,14},{14,12},{1,3},{3,1},... | collective-permute-start | bytes 36872 | tf_op jit(solution)/shard_map/ppermute | solution.py:35

commit v3 on v1

--- a/solution.py
+++ b/solution.py
@@ -44,6 +44,32 @@
         return lax.rem(place + n - slot, n)
     z, y = place // 2, place % 2
     return gray((gray(z) + 4 - slot // 2) & 3) * 2 + (y ^ (slot % 2))
+
+
+def split_kernel(x_ref, upper_ref, lower_ref, sems):
+    rows = upper_ref.shape[0]
+    copies = [
+        pltpu.make_async_copy(x_ref.at[k * rows : (k + 1) * rows, :], ref, sems.at[k])
+        for k, ref in enumerate((upper_ref, lower_ref))
+    ]
+    for copy in copies:
+        copy.start()
+    for copy in copies:
+        copy.wait()
+
+
+def split(x):
+    half = pltpu.VMEM((x.shape[0] // 2, x.shape[1]), x.dtype)
+    return pl.pallas_call(
+        split_kernel,
+        out_shape=(half, half),
+        in_specs=[HBM],
+        out_specs=(VMEM, VMEM),
+        scratch_shapes=[pltpu.SemaphoreType.DMA((2,))],
+        compiler_params=params(),
+        cost_estimate=cost(1, 1),
+        name="split",
+    )(pltpu.with_memory_space_constraint(x, pltpu.HBM))
 
 
 def token_kernel(*refs):
@@ -88,8 +114,8 @@
     hops = ((0, 1), (1, 3), (3, 2), (2, 0))
     ring = [(a * 2 + y, b * 2 + y) for a, b in hops for y in range(2)]
     tie = lax.optimization_barrier
-    rows = x.shape[0] // 2
-    held, ready = [x[:rows], x[rows:]], [x[:rows], x[rows:]]
+    held = list(split(x))
+    ready = list(held)
     slots = []
     for step in range(3):
         across, later = [], []
@@ -402,7 +428,9 @@
         at = slice(k * tile, (k + 1) * tile)
         fisher = jnp.dot(squares_ref[at, :], fisher_ref[:, own], preferred_element_type=F32)
         gradient = jnp.dot(turned_ref[at, :], residual_ref[:, own], preferred_element_type=F32)
-        inverse = 1.0 / (fisher + damping)
+        denominator = fisher + damping
+        inverse = pl.reciprocal(denominator, approx=True)
+        inverse = inverse * (2.0 - denominator * inverse)
         change = gradient * inverse
         inverse_ref[at, :] = inverse
         low_ref[at, :] = (w_ref[at, :] - LEARNING_RATE * change).astype(BF16)
@@ -413,7 +441,7 @@
     features, rows = turned.shape
     columns = weights.shape[1]
     return pl.pallas_call(
-        functools.partial(update_kernel, start, 512),
+        functools.partial(update_kernel, start, 512 if start else 1024),
         out_shape=(
             pltpu.VMEM((features, columns), F32),
             pltpu.VMEM((features, columns), F32),
@@ -422,7 +450,7 @@
         in_specs=[VMEM] * 6,
         out_specs=(VMEM, VMEM, VMEM),
         input_output_aliases={2: 0},
-        compiler_params=params(),
+        compiler_params=params(16),
         cost_estimate=cost(4 * rows * features * columns),
         name="update",
     )(turned, squares, weights, residual, fisher_weight, damping)
@@ -570,8 +598,12 @@
             )
             held_ref[k, :, own] = moved_ref[at, :] - gradient * inverse_ref[at, :]
             done += moved_ref.shape[1]
-        copies.append(pltpu.make_async_copy(held_ref.at[k], out_ref.at[at, :], sems.at[k]))
-        copies[-1].start()
+            copies.append(
+                pltpu.make_async_copy(
+                    held_ref.at[k, :, own], out_ref.at[at, own], sems.at[len(copies)]
+                )
+            )
+            copies[-1].start()
     for copy in copies:
         copy.wait()
 
@@ -594,7 +626,7 @@
             pltpu.VMEM((LANES, LANES), F32),
             pltpu.VMEM((n, LANES), F32),
             pltpu.VMEM((features // tile, tile, classes), F32),
-            pltpu.SemaphoreType.DMA((features // tile,)),
+            pltpu.SemaphoreType.DMA((features // tile * len(moved),)),
         ],
         compiler_params=params(16),
         cost_estimate=cost(2 * all_rows * features * classes),
@@ -652,7 +684,7 @@
     plain = plain[0]
     turned, squares = turn(plain, (n - 2) * rows, 2 * rows, buffers)
     for g in range(max(behind - 1, 0), count):
-        copies = statistics(g, (logits[-1][0], turned))
+        copies = statistics(g, (logits[-2 if g < behind else -1][0], turned if g >= behind else buffers[0]))
     own_stats = stats[-1]
     every = exchange(copies[0])
     residual, fisher_weight, damping, target = first_weights(own_stats, every, e_parts, entries)

time: 109 us -> 110 us (level)
  Pallas kernels: 42.2 us -> 44.5 us
    pallas_call x2 -> x3, Pallas kernels: 12.7 us -> 14.6 us  [the longest x2 13.5 us: update(): pl.pallas_call(functools.partial(update_kernel, start, 512 if start else...]
  transfers between devices with their start and end apart: 26 -> 26, of which waited for: 11 -> 10; matrix products, arithmetic and copies ran while one was open for 0% -> 0% of each run, Pallas kernels for 21% -> 22%
where the time goes in v3:
time: 110 us
  Pallas kernels  44.5 us (40%)
  starting transfers between devices  25.8 us (23%)
  blocking collectives  22.8 us (21%)
  waiting for transfers between devices  14.6 us (13%)
  between operations  2.37 us (2%)
    all_to_all x2, blocking collectives, exchange(): return lax.all_to_all(copies, 'example', 0, 0)  22.8 us
    pallas_call x2, Pallas kernels, update(): pl.pallas_call(functools.partial(update_kernel, start, 512 if start else...  13.5 us
    ppermute x6, starting transfers between devices, gather_blocks(): later.append(lax.ppermute(held[k], 'example', ring))  12.1 us
    ppermute x19, starting transfers between devices, swap(): return lax.ppermute(x, axis, [(i, i ^ offset) for i in range(n)])  11.1 us
    ppermute x19, waiting for transfers between devices, swap(): return lax.ppermute(x, axis, [(i, i ^ offset) for i in range(n)])  7.99 us
    pallas_call x1, Pallas kernels, finish(): pl.pallas_call(functools.partial(finish_kernel, len(moved), len(e_parts),...  7.07 us
    ppermute x6, waiting for transfers between devices, gather_blocks(): later.append(lax.ppermute(held[k], 'example', ring))  6.62 us
    pallas_call x5, Pallas kernels, arriving_logits(): pl.pallas_call(functools.partial(arriving_kernel, count, pieces, start),...  5.29 us
  transfers between devices with their start and end apart: 26, of which 10 were waited for; matrix products, arithmetic and copies ran while one was open for 0% of the time, Pallas kernels for 22%

profile of v3, /device:TPU:0, one launch (start us, length us, event | category | flops | bytes accessed | tf_op | source)
XLA Modules:
  0.0 110.1 jit_solution(11922260681997735415)
XLA Ops:
  0.6 1.1 split.1
  1.7 3.1 %collective-permute-start = (bf16[64,2048]{1,0:T(8,128)(2,1)S(1)}, bf16[64,2048]{1,0:T(8,128)(2,1)S(1)}, u32[]{:S(2)}, u32[]{:S(2)}) collective-permute-start(bf16[64,2048]{1,0:T(8,128)(2,1)S(1)} %get-tuple-element.73.refs_0_), channel_id=1, source_target_pairs={{0,4},{2,6},{4,12},{6,14},{12,8},{14,10},{8,0},{10,2},{1,5},{3,7},... | collective-permute-start | bytes 786440 | tf_op jit(solution)/shard_map/ppermute | solution.py:123
  4.8 1.5 %collective-permute-start.4 = (bf16[64,2048]{1,0:T(8,128)(2,1)S(1)}, bf16[64,2048]{1,0:T(8,128)(2,1)S(1)}, u32[]{:S(2)}, u32[]{:S(2)}) collective-permute-start(bf16[64,2048]{1,0:T(8,128)(2,1)S(1)} %get-tuple-element.73.refs_0_), channel_id=1, source_target_pairs={{0,2},{2,0},{4,6},{6,4},{8,10},{10,8},{12,14},{14,12},{1,3},{3,1},... | collective-permute-start | bytes 786440 | tf_op jit(solution)/shard_map/ppermute | solution.py:35
  6.3 2.6 %collective-permute-start.2 = (bf16[64,2048]{1,0:T(8,128)(2,1)S(1)}, bf16[64,2048]{1,0:T(8,128)(2,1)S(1)}, u32[]{:S(2)}, u32[]{:S(2)}) collective-permute-start(bf16[64,2048]{1,0:T(8,128)(2,1)S(1)} %get-tuple-element.76.refs_1_), channel_id=1, source_target_pairs={{0,4},{2,6},{4,12},{6,14},{12,8},{14,10},{8,0},{10,2},{1,5},{3,7},... | collective-permute-start | bytes 786440 | tf_op jit(solution)/shard_map/ppermute | solution.py:123
  8.9 0.5 collective-permute-start.7
  10.7 3.7 %prepare.1 = (f32[2048,512]{1,0:T(8,128)S(1)}, f32[2048,512]{1,0:T(8,128)S(1)}, bf16[2048,1024]{1,0:T(8,128)(2,1)S(1)}, f32[1,128]{1,0:T(1,128)S(1)}, f32[1,128]{1,0:T(1,128)S(1)}) custom-call(f32[2048,1024]{1,0:T(8,128)} %w_ref.1, bf16[128,2048]{1,0:T(8,128)(2,1)} %x_ref.3, s32[1,128]{1,0:T(1,128)} %bitcast.2, s32[1]{0:T(128)S(6)} %copy.31.counts_ref, ...), custom_call_target="tpu_custom_call" | custom-call | flops 1 | bytes 1 | tf_op jit(solution)/shard_map/prepare/pallas_call | solution.py:179
  14.4 1.6 %collective-permute-start.5 = (bf16[64,2048]{1,0:T(8,128)(2,1)S(1)}, bf16[64,2048]{1,0:T(8,128)(2,1)S(1)}, u32[]{:S(2)}, u32[]{:S(2)}) collective-permute-start(bf16[64,2048]{1,0:T(8,128)(2,1)S(1)} %collective-permute-done.refs_5_.refs_0_), channel_id=1, source_target_pairs={{0,2},{2,0},{4,6},{6,4},{8,10},{10,8},{12,14},{14,12},{1,3},{3,1},... | collective-permute-start | bytes 786440 | tf_op jit(solution)/shard_map/ppermute | solution.py:35
  16.0 2.1 %collective-permute-start.1 = (bf16[64,2048]{1,0:T(8,128)(2,1)S(1)}, bf16[64,2048]{1,0:T(8,128)(2,1)S(1)}, u32[]{:S(2)}, u32[]{:S(2)}) collective-permute-start(bf16[64,2048]{1,0:T(8,128)(2,1)S(1)} %collective-permute-done.refs_5_.refs_0_), channel_id=1, source_target_pairs={{0,4},{2,6},{4,12},{6,14},{12,8},{14,10},{8,0},{10,2},{1,5},{3,7},... | collective-permute-start | bytes 786440 | tf_op jit(solution)/shard_map/ppermute | solution.py:123
  18.1 1.6 %collective-permute-start.3 = (bf16[64,2048]{1,0:T(8,128)(2,1)S(1)}, bf16[64,2048]{1,0:T(8,128)(2,1)S(1)}, u32[]{:S(2)}, u32[]{:S(2)}) collective-permute-start(bf16[64,2048]{1,0:T(8,128)(2,1)S(1)} %collective-permute-done.2.refs_6_.refs_1_), channel_id=1, source_target_pairs={{0,4},{2,6},{4,12},{6,14},{12,8},{14,10},{8,0},{10,2},{1,5},{3,7},... | collective-permute-start | bytes 786440 | tf_op jit(solution)/shard_map/ppermute | solution.py:123
  19.7 1.5 %collective-permute-start.8 = (bf16[64,2048]{1,0:T(8,128)(2,1)S(1)}, bf16[64,2048]{1,0:T(8,128)(2,1)S(1)}, u32[]{:S(2)}, u32[]{:S(2)}) collective-permute-start(bf16[64,2048]{1,0:T(8,128)(2,1)S(1)} %collective-permute-done.2.refs_6_.refs_1_), channel_id=1, source_target_pairs={{0,2},{2,0},{4,6},{6,4},{8,10},{10,8},{12,14},{14,12},{1,3},{3,1},... | collective-permute-start | bytes 786440 | tf_op jit(solution)/shard_map/ppermute | solution.py:35
  21.2 4.0 %collective-permute-done.5.refs_2_ = bf16[64,2048]{1,0:T(8,128)(2,1)S(1)} collective-permute-done((bf16[64,2048]{1,0:T(8,128)(2,1)S(1)}, bf16[64,2048]{1,0:T(8,128)(2,1)S(1)}, u32[]{:S(2)}, u32[]{:S(2)}) %collective-permute-start.5) | collective-permute-done | bytes 262176 | tf_op jit(solution)/shard_map/ppermute | solution.py:35
  25.2 0.9 collective-permute-done.1.refs_8_.refs_0_
  26.2 0.6 collective-permute-start.6
  26.8 2.6 %collective-permute-start.14 = (bf16[64,2048]{1,0:T(8,128)(2,1)S(1)}, bf16[64,2048]{1,0:T(8,128)(2,1)S(1)}, u32[]{:S(2)}, u32[]{:S(2)}) collective-permute-start(bf16[64,2048]{1,0:T(8,128)(2,1)S(1)} %collective-permute-done.1.refs_8_.refs_0_), channel_id=1, source_target_pairs={{0,4},{2,6},{4,12},{6,14},{12,8},{14,10},{8,0},{10,2},{1,5},{3,7},... | collective-permute-start | bytes 786440 | tf_op jit(solution)/shard_map/ppermute | solution.py:123
  29.3 1.8 %collective-permute-done.3.refs_9_.refs_1_ = bf16[64,2048]{1,0:T(8,128)(2,1)S(1)} collective-permute-done((bf16[64,2048]{1,0:T(8,128)(2,1)S(1)}, bf16[64,2048]{1,0:T(8,128)(2,1)S(1)}, u32[]{:S(2)}, u32[]{:S(2)}) %collective-permute-start.3) | collective-permute-done | bytes 262176 | tf_op jit(solution)/shard_map/ppermute | solution.py:123
  31.4 1.3 %arriving_logits.5 = (bf16[1024,2048]{1,0:T(8,128)(2,1)S(1)}, f32[64,1024]{1,0:T(8,128)S(1)}, f32[64,1024]{1,0:T(8,128)S(1)}, f32[64,1024]{1,0:T(8,128)S(1)}, f32[64,1024]{1,0:T(8,128)S(1)}) custom-call(bf16[64,2048]{1,0:T(8,128)(2,1)S(1)} %get-tuple-element.73.refs_0_, bf16[64,2048]{1,0:T(8,128)(2,1)S(1)} %get-tuple-element.76.refs_1_, ...), custom_call_target="tpu_custom_call" | custom-call | flops 1 | bytes 1 | tf_op jit(solution)/shard_map/arriving_logits/pallas_call | solution.py:221
  32.6 1.7 %collective-permute-start.9 = (bf16[64,2048]{1,0:T(8,128)(2,1)S(1)}, bf16[64,2048]{1,0:T(8,128)(2,1)S(1)}, u32[]{:S(2)}, u32[]{:S(2)}) collective-permute-start(bf16[64,2048]{1,0:T(8,128)(2,1)S(1)} %collective-permute-done.3.refs_9_.refs_1_), channel_id=1, source_target_pairs={{0,2},{2,0},{4,6},{6,4},{8,10},{10,8},{12,14},{14,12},{1,3},{3,1},... | collective-permute-start | bytes 786440 | tf_op jit(solution)/shard_map/ppermute | solution.py:35
  34.3 2.2 %collective-permute-done.6.refs_2_.refs_0_ = bf16[64,2048]{1,0:T(8,128)(2,1)S(1)} collective-permute-done((bf16[64,2048]{1,0:T(8,128)(2,1)S(1)}, bf16[64,2048]{1,0:T(8,128)(2,1)S(1)}, u32[]{:S(2)}, u32[]{:S(2)}) %collective-permute-start.6) | collective-permute-done | bytes 262176 | tf_op jit(solution)/shard_map/ppermute | solution.py:35
  37.0 3.4 %collective-permute-done.15.refs_9_.refs_1_.refs_0_ = bf16[64,2048]{1,0:T(8,128)(2,1)S(1)} collective-permute-done((bf16[64,2048]{1,0:T(8,128)(2,1)S(1)}, bf16[64,2048]{1,0:T(8,128)(2,1)S(1)}, u32[]{:S(2)}, u32[]{:S(2)}) %collective-permute-start.15) | collective-permute-done | bytes 262176 | tf_op jit(solution)/shard_map/ppermute | solution.py:123
  40.6 2.6 %collective-permute-start.17 = (bf16[64,2048]{1,0:T(8,128)(2,1)S(1)}, bf16[64,2048]{1,0:T(8,128)(2,1)S(1)}, u32[]{:S(2)}, u32[]{:S(2)}) collective-permute-start(bf16[64,2048]{1,0:T(8,128)(2,1)S(1)} %relay.3), channel_id=1, source_target_pairs={{0,4},{2,6},{4,12},{6,14},{12,8},{14,10},{8,0},{10,2},{1,5},{3,7},... | collective-permute-start | bytes 786440 | tf_op jit(solution)/shard_map/ppermute | solution.py:137
  43.3 1.6 %collective-permute-start.16 = (bf16[64,2048]{1,0:T(8,128)(2,1)S(1)}, bf16[64,2048]{1,0:T(8,128)(2,1)S(1)}, u32[]{:S(2)}, u32[]{:S(2)}) collective-permute-start(bf16[64,2048]{1,0:T(8,128)(2,1)S(1)} %relay.2), channel_id=1, source_target_pairs={{0,2},{2,0},{4,6},{6,4},{8,10},{10,8},{12,14},{14,12},{1,3},{3,1},... | collective-permute-start | bytes 786440 | tf_op jit(solution)/shard_map/ppermute | solution.py:35
  44.9 0.5 turn.4
  45.4 0.5 first_stats.5
  45.9 1.3 %arriving_logits.6 = (bf16[1024,2048]{1,0:T(8,128)(2,1)S(1)}, f32[256,1024]{1,0:T(8,128)S(1)}) custom-call(bf16[64,2048]{1,0:T(8,128)(2,1)S(1)} %collective-permute-done.refs_5_.refs_0_, bf16[64,2048]{1,0:T(8,128)(2,1)S(1)} %collective-permute-done.2.refs_6_.refs_1_, ...), custom_call_target="tpu_custom_call", output_to_operand_aliasing={{0}: (5, {})} | custom-call | flops 1 | bytes 1 | tf_op jit(solution)/shard_map/arriving_logits/pallas_call | solution.py:221
  47.3 0.5 turn.5
  47.7 1.3 %arriving_logits.7 = (bf16[1024,2048]{1,0:T(8,128)(2,1)S(1)}, f32[256,1024]{1,0:T(8,128)S(1)}) custom-call(bf16[64,2048]{1,0:T(8,128)(2,1)S(1)} %collective-permute-done.1.refs_8_.refs_0_, bf16[64,2048]{1,0:T(8,128)(2,1)S(1)} %collective-permute-done.3.refs_9_.refs_1_, ...), custom_call_target="tpu_custom_call", output_to_operand_aliasing={{0}: (5, {})} | custom-call | flops 1 | bytes 1 | tf_op jit(solution)/shard_map/arriving_logits/pallas_call | solution.py:221
  49.0 0.5 turn.6
  49.5 0.7 arriving_logits.8
  50.2 0.6 collective-permute-start.21
  50.9 0.7 arriving_logits.9
  51.6 0.5 collective-permute-start.18
  52.2 0.5 first_stats.6
  52.6 0.5 turn.7
  53.1 0.5 first_stats.7
  54.1 0.4 collective-permute-done.19.refs_5_
  54.9 12.9 %all_to_all.10.all_ref = f32[8,8,640]{2,1,0:T(8,128)S(1)} all-to-all(f32[8,8,640]{2,1,0:T(8,128)S(1)} %get-tuple-element.120), channel_id=1, replica_groups=mesh['groups'=2,'example'=8,'cls'=2] {'example'}, dimensions={0} | all-to-all | bytes 327680 | tf_op jit(solution)/shard_map/all_to_all | solution.py:638
  67.8 1.6 %first_weights.1 = (bf16[1024,1024]{1,0:T(8,128)(2,1)S(1)}, bf16[1024,1024]{1,0:T(8,128)(2,1)S(1)}, f32[8,128]{1,0:T(8,128)S(1)}, f32[8,128]{1,0:T(8,128)S(1)}) custom-call(f32[8,384]{1,0:T(8,128)S(1)} %get-tuple-element.119.own_ref, f32[8,8,640]{2,1,0:T(8,128)S(1)} %all_to_all.10.all_ref, f32[256,1024]{1,0:T(8,128)S(1)} %get-tuple-element.121.refs_0_, ...), custom_call_target="tpu_custom_call" | custom-call | bytes 8388608 | tf_op jit(solution)/shard_map/first_weights/pallas_call | solution.py:405
  69.5 6.7 %update.2 = (f32[2048,512]{1,0:T(8,128)S(1)}, f32[2048,512]{1,0:T(8,128)S(1)}, bf16[2048,512]{1,0:T(8,128)(2,1)S(1)}) custom-call(bf16[2048,1024]{1,0:T(8,128)(2,1)S(1)} %get-tuple-element.106.refs_5_.refs_8_.turned_ref, bf16[2048,1024]{1,0:T(8,128)(2,1)S(1)} %get-tuple-element.107.squares_ref, ...), custom_call_target="tpu_custom_call", output_to_operand_aliasing={{0}: (2, {})} | custom-call | flops 4294967296 | tf_op jit(solution)/shard_map/update/pallas_call | solution.py:443
  76.1 2.3 %next_logits.3.refs_0_ = f32[1024,512]{1,0:T(8,128)S(1)} custom-call(bf16[1024,2048]{1,0:T(8,128)(2,1)S(1)} %get-tuple-element.104.plain_ref, bf16[2048,512]{1,0:T(8,128)(2,1)S(1)} %get-tuple-element.129.low_ref), custom_call_target="tpu_custom_call" | custom-call | flops 2147483648 | tf_op jit(solution)/shard_map/next_logits/pallas_call | solution.py:470
  78.6 6.9 %update.3 = (f32[2048,512]{1,0:T(8,128)S(1)}, f32[2048,512]{1,0:T(8,128)S(1)}, bf16[2048,512]{1,0:T(8,128)(2,1)S(1)}) custom-call(bf16[2048,1024]{1,0:T(8,128)(2,1)S(1)} %get-tuple-element.106.refs_5_.refs_8_.turned_ref, bf16[2048,1024]{1,0:T(8,128)(2,1)S(1)} %get-tuple-element.107.squares_ref, ...), custom_call_target="tpu_custom_call", output_to_operand_aliasing={{0}: (2, {})} | custom-call | flops 4294967296 | tf_op jit(solution)/shard_map/update/pallas_call | solution.py:443
  85.4 1.3 %next_logits.5.refs_1_ = f32[512,512]{1,0:T(8,128)S(1)} custom-call(bf16[1024,2048]{1,0:T(8,128)(2,1)S(1)} %get-tuple-element.104.plain_ref, bf16[2048,512]{1,0:T(8,128)(2,1)S(1)} %get-tuple-element.131.low_ref), custom_call_target="tpu_custom_call" | custom-call | flops 1073741824 | tf_op jit(solution)/shard_map/next_logits/pallas_call | solution.py:470
  86.7 0.6 collective-permute-start.25
  87.2 1.2 %next_logits.4.refs_1_ = f32[512,512]{1,0:T(8,128)S(1)} custom-call(bf16[1024,2048]{1,0:T(8,128)(2,1)S(1)} %get-tuple-element.104.plain_ref, bf16[2048,512]{1,0:T(8,128)(2,1)S(1)} %get-tuple-element.131.low_ref), custom_call_target="tpu_custom_call" | custom-call | flops 1073741824 | tf_op jit(solution)/shard_map/next_logits/pallas_call | solution.py:470
  88.6 0.9 collective-permute-done.25.refs_3_
  89.5 1.7 %last_stats.2 = (f32[512,1024]{1,0:T(8,128)S(1)}, f32[8,384]{1,0:T(8,128)S(1)}) custom-call(f32[1024,512]{1,0:T(8,128)S(1)} %next_logits.3.refs_0_, f32[512,512]{1,0:T(8,128)S(1)} %next_logits.5.refs_1_, f32[1024,512]{1,0:T(8,128)S(1)} %collective-permute-done.23.refs_2_, f32[512,512]{1,0:T(8,128)S(1)} %collective-permute-done.25.refs_3_, ...), custom_call_target="tpu_custom_call" | custom-call | bytes 12582912 | tf_op jit(solution)/shard_map/last_stats/pallas_call | solution.py:537
  91.2 1.7 %last_stats.3 = (f32[512,1024]{1,0:T(8,128)S(1)}, f32[8,384]{1,0:T(8,128)S(1)}, f32[8,8,384]{2,1,0:T(8,128)S(1)}) custom-call(f32[1024,512]{1,0:T(8,128)S(1)} %next_logits.3.refs_0_, f32[512,512]{1,0:T(8,128)S(1)} %next_logits.4.refs_1_, f32[1024,512]{1,0:T(8,128)S(1)} %collective-permute-done.23.refs_2_, f32[512,512]{1,0:T(8,128)S(1)} %collective-permute-done.24.refs_3_, ...), custom_call_target="tpu_custom_call" | custom-call | bytes 12582912 | tf_op jit(solution)/shard_map/last_stats/pallas_call | solution.py:537
  92.9 9.9 %all_to_all.11.all_ref = f32[8,8,384]{2,1,0:T(8,128)S(1)} all-to-all(f32[8,8,384]{2,1,0:T(8,128)S(1)} %get-tuple-element.135), channel_id=1, replica_groups=mesh['groups'=2,'example'=8,'cls'=2] {'example'}, dimensions={0} | all-to-all | bytes 196608 | tf_op jit(solution)/shard_map/all_to_all | solution.py:638
  102.8 7.1 %finish.1 = (f32[2048,1024]{1,0:T(8,128)}, f32[1,128]{1,0:T(1,128)}) custom-call(f32[8,384]{1,0:T(8,128)S(1)} %get-tuple-element.134.own_ref, f32[8,8,384]{2,1,0:T(8,128)S(1)} %all_to_all.11.all_ref, f32[8,128]{1,0:T(8,128)S(1)} %get-tuple-element.132.refs_4_.target_ref, bf16[2048,1024]{1,0:T(8,128)(2,1)S(1)} %get-tuple-element.106.refs_5_.refs_8_.turned_ref, ...), custom_call_target="tpu_custom_call" | custom-call | flops 4294967296 | tf_op jit(solution)/shard_map/finish/pallas_call | solution.py:616
  (37 shorter events, 2.2 us)
Async XLA Ops:
  1.7 12.7 %collective-permute-start = (bf16[64,2048]{1,0:T(8,128)(2,1)S(1)}, bf16[64,2048]{1,0:T(8,128)(2,1)S(1)}, u32[]{:S(2)}, u32[]{:S(2)}) collective-permute-start(bf16[64,2048]{1,0:T(8,128)(2,1)S(1)} %get-tuple-element.73.refs_0_), channel_id=1, source_target_pairs={{0,4},{2,6},{4,12},{6,14},{12,8},{14,10},{8,0},{10,2},{1,5},{3,7},... | collective-permute-start | bytes 786440 | tf_op jit(solution)/shard_map/ppermute | solution.py:123
  4.8 9.7 %collective-permute-start.4 = (bf16[64,2048]{1,0:T(8,128)(2,1)S(1)}, bf16[64,2048]{1,0:T(8,128)(2,1)S(1)}, u32[]{:S(2)}, u32[]{:S(2)}) collective-permute-start(bf16[64,2048]{1,0:T(8,128)(2,1)S(1)} %get-tuple-element.73.refs_0_), channel_id=1, source_target_pairs={{0,2},{2,0},{4,6},{6,4},{8,10},{10,8},{12,14},{14,12},{1,3},{3,1},... | collective-permute-start | bytes 786440 | tf_op jit(solution)/shard_map/ppermute | solution.py:35
  6.3 11.8 %collective-permute-start.2 = (bf16[64,2048]{1,0:T(8,128)(2,1)S(1)}, bf16[64,2048]{1,0:T(8,128)(2,1)S(1)}, u32[]{:S(2)}, u32[]{:S(2)}) collective-permute-start(bf16[64,2048]{1,0:T(8,128)(2,1)S(1)} %get-tuple-element.76.refs_1_), channel_id=1, source_target_pairs={{0,4},{2,6},{4,12},{6,14},{12,8},{14,10},{8,0},{10,2},{1,5},{3,7},... | collective-permute-start | bytes 786440 | tf_op jit(solution)/shard_map/ppermute | solution.py:123
  8.9 10.8 %collective-permute-start.7 = (bf16[64,2048]{1,0:T(8,128)(2,1)S(1)}, bf16[64,2048]{1,0:T(8,128)(2,1)S(1)}, u32[]{:S(2)}, u32[]{:S(2)}) collective-permute-start(bf16[64,2048]{1,0:T(8,128)(2,1)S(1)} %get-tuple-element.76.refs_1_), channel_id=1, source_target_pairs={{0,2},{2,0},{4,6},{6,4},{8,10},{10,8},{12,14},{14,12},{1,3},{3,1},... | collective-permute-start | bytes 786440 | tf_op jit(solution)/shard_map/ppermute | solution.py:35
  14.4 10.8 %collective-permute-start.5 = (bf16[64,2048]{1,0:T(8,128)(2,1)S(1)}, bf16[64,2048]{1,0:T(8,128)(2,1)S(1)}, u32[]{:S(2)}, u32[]{:S(2)}) collective-permute-start(bf16[64,2048]{1,0:T(8,128)(2,1)S(1)} %collective-permute-done.refs_5_.refs_0_), channel_id=1, source_target_pairs={{0,2},{2,0},{4,6},{6,4},{8,10},{10,8},{12,14},{14,12},{1,3},{3,1},... | collective-permute-start | bytes 786440 | tf_op jit(solution)/shard_map/ppermute | solution.py:35
  16.0 10.1 %collective-permute-start.1 = (bf16[64,2048]{1,0:T(8,128)(2,1)S(1)}, bf16[64,2048]{1,0:T(8,128)(2,1)S(1)}, u32[]{:S(2)}, u32[]{:S(2)}) collective-permute-start(bf16[64,2048]{1,0:T(8,128)(2,1)S(1)} %collective-permute-done.refs_5_.refs_0_), channel_id=1, source_target_pairs={{0,4},{2,6},{4,12},{6,14},{12,8},{14,10},{8,0},{10,2},{1,5},{3,7},... | collective-permute-start | bytes 786440 | tf_op jit(solution)/shard_map/ppermute | solution.py:123
  18.1 13.0 %collective-permute-start.3 = (bf16[64,2048]{1,0:T(8,128)(2,1)S(1)}, bf16[64,2048]{1,0:T(8,128)(2,1)S(1)}, u32[]{:S(2)}, u32[]{:S(2)}) collective-permute-start(bf16[64,2048]{1,0:T(8,128)(2,1)S(1)} %collective-permute-done.2.refs_6_.refs_1_), channel_id=1, source_target_pairs={{0,4},{2,6},{4,12},{6,14},{12,8},{14,10},{8,0},{10,2},{1,5},{3,7},... | collective-permute-start | bytes 786440 | tf_op jit(solution)/shard_map/ppermute | solution.py:123
  19.7 12.9 %collective-permute-start.8 = (bf16[64,2048]{1,0:T(8,128)(2,1)S(1)}, bf16[64,2048]{1,0:T(8,128)(2,1)S(1)}, u32[]{:S(2)}, u32[]{:S(2)}) collective-permute-start(bf16[64,2048]{1,0:T(8,128)(2,1)S(1)} %collective-permute-done.2.refs_6_.refs_1_), channel_id=1, source_target_pairs={{0,2},{2,0},{4,6},{6,4},{8,10},{10,8},{12,14},{14,12},{1,3},{3,1},... | collective-permute-start | bytes 786440 | tf_op jit(solution)/shard_map/ppermute | solution.py:35
  26.2 10.3 %collective-permute-start.6 = (bf16[64,2048]{1,0:T(8,128)(2,1)S(1)}, bf16[64,2048]{1,0:T(8,128)(2,1)S(1)}, u32[]{:S(2)}, u32[]{:S(2)}) collective-permute-start(bf16[64,2048]{1,0:T(8,128)(2,1)S(1)} %collective-permute-done.1.refs_8_.refs_0_), channel_id=1, source_target_pairs={{0,2},{2,0},{4,6},{6,4},{8,10},{10,8},{12,14},{14,12},{1,3},{3,1},... | collective-permute-start | bytes 786440 | tf_op jit(solution)/shard_map/ppermute | solution.py:35
  26.8 10.1 %collective-permute-start.14 = (bf16[64,2048]{1,0:T(8,128)(2,1)S(1)}, bf16[64,2048]{1,0:T(8,128)(2,1)S(1)}, u32[]{:S(2)}, u32[]{:S(2)}) collective-permute-start(bf16[64,2048]{1,0:T(8,128)(2,1)S(1)} %collective-permute-done.1.refs_8_.refs_0_), channel_id=1, source_target_pairs={{0,4},{2,6},{4,12},{6,14},{12,8},{14,10},{8,0},{10,2},{1,5},{3,7},... | collective-permute-start | bytes 786440 | tf_op jit(solution)/shard_map/ppermute | solution.py:123
  31.2 9.3 %collective-permute-start.15 = (bf16[64,2048]{1,0:T(8,128)(2,1)S(1)}, bf16[64,2048]{1,0:T(8,128)(2,1)S(1)}, u32[]{:S(2)}, u32[]{:S(2)}) collective-permute-start(bf16[64,2048]{1,0:T(8,128)(2,1)S(1)} %collective-permute-done.3.refs_9_.refs_1_), channel_id=1, source_target_pairs={{0,4},{2,6},{4,12},{6,14},{12,8},{14,10},{8,0},{10,2},{1,5},{3,7},... | collective-permute-start | bytes 786440 | tf_op jit(solution)/shard_map/ppermute | solution.py:123
  32.6 8.0 %collective-permute-start.9 = (bf16[64,2048]{1,0:T(8,128)(2,1)S(1)}, bf16[64,2048]{1,0:T(8,128)(2,1)S(1)}, u32[]{:S(2)}, u32[]{:S(2)}) collective-permute-start(bf16[64,2048]{1,0:T(8,128)(2,1)S(1)} %collective-permute-done.3.refs_9_.refs_1_), channel_id=1, source_target_pairs={{0,2},{2,0},{4,6},{6,4},{8,10},{10,8},{12,14},{14,12},{1,3},{3,1},... | collective-permute-start | bytes 786440 | tf_op jit(solution)/shard_map/ppermute | solution.py:35
  34.3 9.0 %collective-permute-start.10 = (f32[64,1024]{1,0:T(8,128)S(1)}, f32[64,1024]{1,0:T(8,128)S(1)}, u32[]{:S(2)}, u32[]{:S(2)}) collective-permute-start(f32[64,1024]{1,0:T(8,128)S(1)} %get-tuple-element.87.refs_0_), channel_id=1, source_target_pairs={{0,1},{1,0},{2,3},{3,2},{4,5},{5,4},{6,7},{7,6},{8,9},{9,8},{10,11... | collective-permute-start | bytes 786440 | tf_op jit(solution)/shard_map/ppermute | solution.py:35
  36.5 8.9 %collective-permute-start.11 = (f32[64,1024]{1,0:T(8,128)S(1)}, f32[64,1024]{1,0:T(8,128)S(1)}, u32[]{:S(2)}, u32[]{:S(2)}) collective-permute-start(f32[64,1024]{1,0:T(8,128)S(1)} %get-tuple-element.88.refs_1_), channel_id=1, source_target_pairs={{0,1},{1,0},{2,3},{3,2},{4,5},{5,4},{6,7},{7,6},{8,9},{9,8},{10,11... | collective-permute-start | bytes 786440 | tf_op jit(solution)/shard_map/ppermute | solution.py:35
  36.9 8.5 %collective-permute-start.12 = (f32[64,1024]{1,0:T(8,128)S(1)}, f32[64,1024]{1,0:T(8,128)S(1)}, u32[]{:S(2)}, u32[]{:S(2)}) collective-permute-start(f32[64,1024]{1,0:T(8,128)S(1)} %get-tuple-element.89.refs_2_), channel_id=1, source_target_pairs={{0,1},{1,0},{2,3},{3,2},{4,5},{5,4},{6,7},{7,6},{8,9},{9,8},{10,11... | collective-permute-start | bytes 786440 | tf_op jit(solution)/shard_map/ppermute | solution.py:35
  40.4 5.0 %collective-permute-start.13 = (f32[64,1024]{1,0:T(8,128)S(1)}, f32[64,1024]{1,0:T(8,128)S(1)}, u32[]{:S(2)}, u32[]{:S(2)}) collective-permute-start(f32[64,1024]{1,0:T(8,128)S(1)} %get-tuple-element.90.refs_3_), channel_id=1, source_target_pairs={{0,1},{1,0},{2,3},{3,2},{4,5},{5,4},{6,7},{7,6},{8,9},{9,8},{10,11... | collective-permute-start | bytes 786440 | tf_op jit(solution)/shard_map/ppermute | solution.py:35
  40.6 9.6 %collective-permute-start.17 = (bf16[64,2048]{1,0:T(8,128)(2,1)S(1)}, bf16[64,2048]{1,0:T(8,128)(2,1)S(1)}, u32[]{:S(2)}, u32[]{:S(2)}) collective-permute-start(bf16[64,2048]{1,0:T(8,128)(2,1)S(1)} %relay.3), channel_id=1, source_target_pairs={{0,4},{2,6},{4,12},{6,14},{12,8},{14,10},{8,0},{10,2},{1,5},{3,7},... | collective-permute-start | bytes 786440 | tf_op jit(solution)/shard_map/ppermute | solution.py:137
  43.3 6.9 %collective-permute-start.16 = (bf16[64,2048]{1,0:T(8,128)(2,1)S(1)}, bf16[64,2048]{1,0:T(8,128)(2,1)S(1)}, u32[]{:S(2)}, u32[]{:S(2)}) collective-permute-start(bf16[64,2048]{1,0:T(8,128)(2,1)S(1)} %relay.2), channel_id=1, source_target_pairs={{0,2},{2,0},{4,6},{6,4},{8,10},{10,8},{12,14},{14,12},{1,3},{3,1},... | collective-permute-start | bytes 786440 | tf_op jit(solution)/shard_map/ppermute | solution.py:35
  47.2 5.0 %collective-permute-start.22 = (f32[256,1024]{1,0:T(8,128)S(1)}, f32[256,1024]{1,0:T(8,128)S(1)}, u32[]{:S(2)}, u32[]{:S(2)}) collective-permute-start(f32[256,1024]{1,0:T(8,128)S(1)} %get-tuple-element.115.refs_0_), channel_id=1, source_target_pairs={{0,1},{1,0},{2,3},{3,2},{4,5},{5,4},{6,7},{7,6},{8,9},{9,8},{10,11... | collective-permute-start | bytes 3145736 | tf_op jit(solution)/shard_map/ppermute | solution.py:35
  50.2 2.9 %collective-permute-start.21 = (f32[256,1024]{1,0:T(8,128)S(1)}, f32[256,1024]{1,0:T(8,128)S(1)}, u32[]{:S(2)}, u32[]{:S(2)}) collective-permute-start(f32[256,1024]{1,0:T(8,128)S(1)} %get-tuple-element.113.refs_0_), channel_id=1, source_target_pairs={{0,1},{1,0},{2,3},{3,2},{4,5},{5,4},{6,7},{7,6},{8,9},{9,8},{10,11... | collective-permute-start | bytes 3145736 | tf_op jit(solution)/shard_map/ppermute | solution.py:35
  50.8 3.0 %collective-permute-start.20 = (f32[128,1024]{1,0:T(8,128)S(1)}, f32[128,1024]{1,0:T(8,128)S(1)}, u32[]{:S(2)}, u32[]{:S(2)}) collective-permute-start(f32[128,1024]{1,0:T(8,128)S(1)} %get-tuple-element.112.refs_4_.refs_0_), channel_id=1, source_target_pairs={{0,1},{1,0},{2,3},{3,2},{4,5},{5,4},{6,7},{7,6},{8,9},{9,8},{10,11... | collective-permute-start | bytes 1572872 | tf_op jit(solution)/shard_map/ppermute | solution.py:35
  51.6 3.0 %collective-permute-start.18 = (f32[128,1024]{1,0:T(8,128)S(1)}, f32[128,1024]{1,0:T(8,128)S(1)}, u32[]{:S(2)}, u32[]{:S(2)}) collective-permute-start(f32[128,1024]{1,0:T(8,128)S(1)} %get-tuple-element.109.refs_4_.refs_0_.refs_7_), channel_id=1, source_target_pairs={{0,1},{1,0},{2,3},{3,2},{4,5},{5,4},{6,7},{7,6},{8,9},{9,8},{10,11... | collective-permute-start | bytes 1572872 | tf_op jit(solution)/shard_map/ppermute | solution.py:35
  52.1 2.5 %collective-permute-start.19 = (f32[1,128]{1,0:T(1,128)S(1)}, f32[1,128]{1,0:T(1,128)S(1)}, u32[]{:S(2)}, u32[]{:S(2)}) collective-permute-start(f32[1,128]{1,0:T(1,128)S(1)} %get-tuple-element.111.refs_4_), channel_id=1, source_target_pairs={{0,1},{1,0},{2,3},{3,2},{4,5},{5,4},{6,7},{7,6},{8,9},{9,8},{10,11... | collective-permute-start | bytes 1544 | tf_op jit(solution)/shard_map/ppermute | solution.py:35
  78.5 11.1 %collective-permute-start.23 = (f32[1024,512]{1,0:T(8,128)S(1)}, f32[1024,512]{1,0:T(8,128)S(1)}, u32[]{:S(2)}, u32[]{:S(2)}) collective-permute-start(f32[1024,512]{1,0:T(8,128)S(1)} %next_logits.3.refs_0_), channel_id=1, source_target_pairs={{0,1},{1,0},{2,3},{3,2},{4,5},{5,4},{6,7},{7,6},{8,9},{9,8},{10,11... | collective-permute-start | bytes 6291464 | tf_op jit(solution)/shard_map/ppermute | solution.py:35
  86.7 2.8 %collective-permute-start.25 = (f32[512,512]{1,0:T(8,128)S(1)}, f32[512,512]{1,0:T(8,128)S(1)}, u32[]{:S(2)}, u32[]{:S(2)}) collective-permute-start(f32[512,512]{1,0:T(8,128)S(1)} %next_logits.5.refs_1_), channel_id=1, source_target_pairs={{0,1},{1,0},{2,3},{3,2},{4,5},{5,4},{6,7},{7,6},{8,9},{9,8},{10,11... | collective-permute-start | bytes 3145736 | tf_op jit(solution)/shard_map/ppermute | solution.py:35
  88.5 2.7 %collective-permute-start.24 = (f32[512,512]{1,0:T(8,128)S(1)}, f32[512,512]{1,0:T(8,128)S(1)}, u32[]{:S(2)}, u32[]{:S(2)}) collective-permute-start(f32[512,512]{1,0:T(8,128)S(1)} %next_logits.4.refs_1_), channel_id=1, source_target_pairs={{0,1},{1,0},{2,3},{3,2},{4,5},{5,4},{6,7},{7,6},{8,9},{9,8},{10,11... | collective-permute-start | bytes 3145736 | tf_op jit(solution)/shard_map/ppermute | solution.py:35

commit v4 on v1

--- a/solution.py
+++ b/solution.py
@@ -78,13 +78,13 @@
     )(block, *tokens)
 
 
-def gather_blocks(x, n, early):
+def gather_blocks(x, n, early, first_logits):
     if n != 8:
         ring = [(i, (i + 1) % n) for i in range(n)]
         slots = [x]
         for _ in range(n - 1):
             slots.append(lax.ppermute(slots[-1], "example", ring))
-        return [[slot] for slot in slots], [()] * (n // 2), early, [slot for slot in slots[3::2]]
+        return [[slot] for slot in slots], [()] * (n // 2), early, [slot for slot in slots[3::2]], None
     hops = ((0, 1), (1, 3), (3, 2), (2, 0))
     ring = [(a * 2 + y, b * 2 + y) for a, b in hops for y in range(2)]
     tie = lax.optimization_barrier
@@ -94,6 +94,9 @@
     for step in range(3):
         across, later = [], []
         for k in range(2):
+            if step == 2 and k == 1:
+                begun = first_logits(slots[0] + slots[1], early, tuple(slots[2]))
+                held[k], *begun[1] = tie((held[k], *begun[1]))
             later.append(lax.ppermute(held[k], "example", ring))
             across.append(swap(ready[k], "example", n, 1))
         slots += [held, list(across)]
@@ -110,7 +113,7 @@
     upper = relay(held[0], (seen,))
     last = [swap(upper, "example", n, 1), lax.ppermute(lower, "example", ring)]
     slots += [held, last]
-    return slots, [tuple(slots[2 * k + 2]) for k in range(3)] + [()], early, [slots[3][1], upper]
+    return slots, [tuple(slots[2 * k + 2]) for k in range(3)] + [()], early, [slots[3][1], upper], begun
 
 
 def prepare_kernel(tile, chunks, w_ref, x_ref, labels_ref, counts_ref, active_ref, *refs):
@@ -570,8 +573,12 @@
             )
             held_ref[k, :, own] = moved_ref[at, :] - gradient * inverse_ref[at, :]
             done += moved_ref.shape[1]
-        copies.append(pltpu.make_async_copy(held_ref.at[k], out_ref.at[at, :], sems.at[k]))
-        copies[-1].start()
+            copies.append(
+                pltpu.make_async_copy(
+                    held_ref.at[k, :, own], out_ref.at[at, own], sems.at[len(copies)]
+                )
+            )
+            copies[-1].start()
     for copy in copies:
         copy.wait()
 
@@ -594,7 +601,7 @@
             pltpu.VMEM((LANES, LANES), F32),
             pltpu.VMEM((n, LANES), F32),
             pltpu.VMEM((features // tile, tile, classes), F32),
-            pltpu.SemaphoreType.DMA((features // tile,)),
+            pltpu.SemaphoreType.DMA((features // tile * len(moved),)),
         ],
         compiler_params=params(16),
         cost_estimate=cost(2 * all_rows * features * classes),
@@ -614,7 +621,10 @@
     weights = pltpu.with_memory_space_constraint(weights, pltpu.HBM)
     columns = min(512, classes)
     kept, w_low, target, norm = prepare(weights, features, labels, counts, active, columns)
-    slots, waits, w_low, gates = gather_blocks(features, n, w_low)
+    def first_logits(parts, low, tokens):
+        return list(arriving_logits(parts, low, (), 0, all_rows, STEP, tokens))
+
+    slots, waits, w_low, gates, begun = gather_blocks(features, n, w_low, first_logits)
     side = (target, norm, swap(norm, "cls", n_cls, 1))
 
     groups = [[k, k + 1] for k in range(0, n - 2, 2)] + [[n - 2], [n - 1]]
@@ -638,9 +648,14 @@
             logits[behind:], slots[-1] = lax.optimization_barrier((logits[behind:], slots[-1]))
         parts = [part for slot in groups[g] for part in slots[slot]]
         tokens = tuple(stats[-1:]) + tuple(buffers[:1]) + tuple(waits[g] if g < n // 2 else ())
+        if g == 2:
+            tokens += side[2:]
         start = groups[g][0] * rows
         piece = (64,256,256,128,128)[g] if count == 5 else LANES
-        block, found = arriving_logits(parts, w_low, plain, start, all_rows, piece, tokens)
+        if g == 0 and begun is not None:
+            block, found = begun
+        else:
+            block, found = arriving_logits(parts, w_low, plain, start, all_rows, piece, tokens)
         plain = (block,)
         logits.append(found)
         if g < n // 2 - 1:

time: 109 us -> 109 us (level)
  no operation moved by 1% of the time
where the time goes in v4:
time: 109 us
  Pallas kernels  41.9 us (38%)
  starting transfers between devices  25.8 us (24%)
  blocking collectives  22.6 us (21%)
  waiting for transfers between devices  15.2 us (14%)
  between operations  2.36 us (2%)
    all_to_all x2, blocking collectives, exchange(): return lax.all_to_all(copies, 'example', 0, 0)  22.6 us
    pallas_call x2, Pallas kernels, update(): pl.pallas_call(functools.partial(update_kernel, start, 512), out_shape=(p...  12.7 us
    ppermute x6, starting transfers between devices, gather_blocks(): later.append(lax.ppermute(held[k], 'example', ring))  12.1 us
    ppermute x19, starting transfers between devices, swap(): return lax.ppermute(x, axis, [(i, i ^ offset) for i in range(n)])  11 us
    ppermute x19, waiting for transfers between devices, swap(): return lax.ppermute(x, axis, [(i, i ^ offset) for i in range(n)])  8.55 us
    pallas_call x1, Pallas kernels, finish(): pl.pallas_call(functools.partial(finish_kernel, len(moved), len(e_parts),...  6.85 us
    ppermute x6, waiting for transfers between devices, gather_blocks(): later.append(lax.ppermute(held[k], 'example', ring))  6.62 us
    pallas_call x5, Pallas kernels, arriving_logits(): pl.pallas_call(functools.partial(arriving_kernel, count, pieces, start),...  5.34 us
  transfers between devices with their start and end apart: 26, of which 11 were waited for; matrix products, arithmetic and copies ran while one was open for 0% of the time, Pallas kernels for 21%

profile of v4, /device:TPU:0, one launch (start us, length us, event | category | flops | bytes accessed | tf_op | source)
XLA Modules:
  0.0 108.9 jit_solution(12690226462395622996)
XLA Ops:
  0.6 1.1 fusion
  1.7 3.1 %collective-permute-start = (bf16[64,2048]{1,0:T(8,128)(2,1)S(1)}, bf16[64,2048]{1,0:T(8,128)(2,1)S(1)}, u32[]{:S(2)}, u32[]{:S(2)}) collective-permute-start(bf16[64,2048]{1,0:T(8,128)(2,1)S(1)} %get-tuple-element.151.refs_0_), channel_id=1, source_target_pairs={{0,4},{2,6},{4,12},{6,14},{12,8},{14,10},{8,0},{10,2},{1,5},{3,7},... | collective-permute-start | bytes 786440 | tf_op jit(solution)/shard_map/ppermute | solution.py:100
  4.8 1.5 %collective-permute-start.4 = (bf16[64,2048]{1,0:T(8,128)(2,1)S(1)}, bf16[64,2048]{1,0:T(8,128)(2,1)S(1)}, u32[]{:S(2)}, u32[]{:S(2)}) collective-permute-start(bf16[64,2048]{1,0:T(8,128)(2,1)S(1)} %get-tuple-element.151.refs_0_), channel_id=1, source_target_pairs={{0,2},{2,0},{4,6},{6,4},{8,10},{10,8},{12,14},{14,12},{1,3},{3,1},... | collective-permute-start | bytes 786440 | tf_op jit(solution)/shard_map/ppermute | solution.py:35
  6.3 2.6 %collective-permute-start.2 = (bf16[64,2048]{1,0:T(8,128)(2,1)S(1)}, bf16[64,2048]{1,0:T(8,128)(2,1)S(1)}, u32[]{:S(2)}, u32[]{:S(2)}) collective-permute-start(bf16[64,2048]{1,0:T(8,128)(2,1)S(1)} %get-tuple-element.150.refs_1_), channel_id=1, source_target_pairs={{0,4},{2,6},{4,12},{6,14},{12,8},{14,10},{8,0},{10,2},{1,5},{3,7},... | collective-permute-start | bytes 786440 | tf_op jit(solution)/shard_map/ppermute | solution.py:100
  8.9 0.5 collective-permute-start.5
  10.7 3.7 %prepare.1 = (f32[2048,512]{1,0:T(8,128)S(1)}, f32[2048,512]{1,0:T(8,128)S(1)}, bf16[2048,1024]{1,0:T(8,128)(2,1)S(1)}, f32[1,128]{1,0:T(1,128)S(1)}, f32[1,128]{1,0:T(1,128)S(1)}) custom-call(f32[2048,1024]{1,0:T(8,128)} %w_ref.1, bf16[128,2048]{1,0:T(8,128)(2,1)} %x_ref.1, s32[1,128]{1,0:T(1,128)} %bitcast.2, s32[1]{0:T(128)S(6)} %copy.31.counts_ref, ...), custom_call_target="tpu_custom_call" | custom-call | flops 1 | bytes 1 | tf_op jit(solution)/shard_map/prepare/pallas_call | solution.py:156
  14.4 1.6 %collective-permute-start.6 = (bf16[64,2048]{1,0:T(8,128)(2,1)S(1)}, bf16[64,2048]{1,0:T(8,128)(2,1)S(1)}, u32[]{:S(2)}, u32[]{:S(2)}) collective-permute-start(bf16[64,2048]{1,0:T(8,128)(2,1)S(1)} %collective-permute-done.refs_5_.refs_0_), channel_id=1, source_target_pairs={{0,2},{2,0},{4,6},{6,4},{8,10},{10,8},{12,14},{14,12},{1,3},{3,1},... | collective-permute-start | bytes 786440 | tf_op jit(solution)/shard_map/ppermute | solution.py:35
  16.0 2.1 %collective-permute-start.1 = (bf16[64,2048]{1,0:T(8,128)(2,1)S(1)}, bf16[64,2048]{1,0:T(8,128)(2,1)S(1)}, u32[]{:S(2)}, u32[]{:S(2)}) collective-permute-start(bf16[64,2048]{1,0:T(8,128)(2,1)S(1)} %collective-permute-done.refs_5_.refs_0_), channel_id=1, source_target_pairs={{0,4},{2,6},{4,12},{6,14},{12,8},{14,10},{8,0},{10,2},{1,5},{3,7},... | collective-permute-start | bytes 786440 | tf_op jit(solution)/shard_map/ppermute | solution.py:100
  18.1 1.6 %collective-permute-start.3 = (bf16[64,2048]{1,0:T(8,128)(2,1)S(1)}, bf16[64,2048]{1,0:T(8,128)(2,1)S(1)}, u32[]{:S(2)}, u32[]{:S(2)}) collective-permute-start(bf16[64,2048]{1,0:T(8,128)(2,1)S(1)} %collective-permute-done.2.refs_6_.refs_1_), channel_id=1, source_target_pairs={{0,4},{2,6},{4,12},{6,14},{12,8},{14,10},{8,0},{10,2},{1,5},{3,7},... | collective-permute-start | bytes 786440 | tf_op jit(solution)/shard_map/ppermute | solution.py:100
  19.7 1.5 %collective-permute-start.8 = (bf16[64,2048]{1,0:T(8,128)(2,1)S(1)}, bf16[64,2048]{1,0:T(8,128)(2,1)S(1)}, u32[]{:S(2)}, u32[]{:S(2)}) collective-permute-start(bf16[64,2048]{1,0:T(8,128)(2,1)S(1)} %collective-permute-done.2.refs_6_.refs_1_), channel_id=1, source_target_pairs={{0,2},{2,0},{4,6},{6,4},{8,10},{10,8},{12,14},{14,12},{1,3},{3,1},... | collective-permute-start | bytes 786440 | tf_op jit(solution)/shard_map/ppermute | solution.py:35
  21.2 1.3 %arriving_logits.5 = (bf16[1024,2048]{1,0:T(8,128)(2,1)S(1)}, f32[64,1024]{1,0:T(8,128)S(1)}, f32[64,1024]{1,0:T(8,128)S(1)}, f32[64,1024]{1,0:T(8,128)S(1)}, f32[64,1024]{1,0:T(8,128)S(1)}) custom-call(bf16[64,2048]{1,0:T(8,128)(2,1)S(1)} %get-tuple-element.151.refs_0_, bf16[64,2048]{1,0:T(8,128)(2,1)S(1)} %get-tuple-element.150.refs_1_, ...), custom_call_target="tpu_custom_call" | custom-call | flops 1 | bytes 1 | tf_op jit(solution)/shard_map/arriving_logits/pallas_call | solution.py:198
  22.5 2.7 %collective-permute-done.6.refs_2_ = bf16[64,2048]{1,0:T(8,128)(2,1)S(1)} collective-permute-done((bf16[64,2048]{1,0:T(8,128)(2,1)S(1)}, bf16[64,2048]{1,0:T(8,128)(2,1)S(1)}, u32[]{:S(2)}, u32[]{:S(2)}) %collective-permute-start.6) | collective-permute-done | bytes 262176 | tf_op jit(solution)/shard_map/ppermute | solution.py:35
  25.2 0.9 collective-permute-done.1.refs_8_.refs_0_
  26.2 0.6 collective-permute-start.7
  26.8 2.6 %collective-permute-start.14 = (bf16[64,2048]{1,0:T(8,128)(2,1)S(1)}, bf16[64,2048]{1,0:T(8,128)(2,1)S(1)}, u32[]{:S(2)}, u32[]{:S(2)}) collective-permute-start(bf16[64,2048]{1,0:T(8,128)(2,1)S(1)} %collective-permute-done.1.refs_8_.refs_0_), channel_id=1, source_target_pairs={{0,4},{2,6},{4,12},{6,14},{12,8},{14,10},{8,0},{10,2},{1,5},{3,7},... | collective-permute-start | bytes 786440 | tf_op jit(solution)/shard_map/ppermute | solution.py:100
  29.4 1.8 %collective-permute-done.3.refs_9_.refs_1_ = bf16[64,2048]{1,0:T(8,128)(2,1)S(1)} collective-permute-done((bf16[64,2048]{1,0:T(8,128)(2,1)S(1)}, bf16[64,2048]{1,0:T(8,128)(2,1)S(1)}, u32[]{:S(2)}, u32[]{:S(2)}) %collective-permute-start.3) | collective-permute-done | bytes 262176 | tf_op jit(solution)/shard_map/ppermute | solution.py:100
  31.4 1.6 %collective-permute-start.9 = (bf16[64,2048]{1,0:T(8,128)(2,1)S(1)}, bf16[64,2048]{1,0:T(8,128)(2,1)S(1)}, u32[]{:S(2)}, u32[]{:S(2)}) collective-permute-start(bf16[64,2048]{1,0:T(8,128)(2,1)S(1)} %collective-permute-done.3.refs_9_.refs_1_), channel_id=1, source_target_pairs={{0,2},{2,0},{4,6},{6,4},{8,10},{10,8},{12,14},{14,12},{1,3},{3,1},... | collective-permute-start | bytes 786440 | tf_op jit(solution)/shard_map/ppermute | solution.py:35
  33.0 3.5 %collective-permute-done.7.refs_2_.refs_0_ = bf16[64,2048]{1,0:T(8,128)(2,1)S(1)} collective-permute-done((bf16[64,2048]{1,0:T(8,128)(2,1)S(1)}, bf16[64,2048]{1,0:T(8,128)(2,1)S(1)}, u32[]{:S(2)}, u32[]{:S(2)}) %collective-permute-start.7) | collective-permute-done | bytes 262176 | tf_op jit(solution)/shard_map/ppermute | solution.py:35
  36.5 0.4 collective-permute-done.14.refs_8_.refs_0_
  37.0 3.4 %collective-permute-done.15.refs_9_.refs_1_.refs_0_ = bf16[64,2048]{1,0:T(8,128)(2,1)S(1)} collective-permute-done((bf16[64,2048]{1,0:T(8,128)(2,1)S(1)}, bf16[64,2048]{1,0:T(8,128)(2,1)S(1)}, u32[]{:S(2)}, u32[]{:S(2)}) %collective-permute-start.15) | collective-permute-done | bytes 262176 | tf_op jit(solution)/shard_map/ppermute | solution.py:100
  40.7 2.6 %collective-permute-start.18 = (bf16[64,2048]{1,0:T(8,128)(2,1)S(1)}, bf16[64,2048]{1,0:T(8,128)(2,1)S(1)}, u32[]{:S(2)}, u32[]{:S(2)}) collective-permute-start(bf16[64,2048]{1,0:T(8,128)(2,1)S(1)} %relay.3), channel_id=1, source_target_pairs={{0,4},{2,6},{4,12},{6,14},{12,8},{14,10},{8,0},{10,2},{1,5},{3,7},... | collective-permute-start | bytes 786440 | tf_op jit(solution)/shard_map/ppermute | solution.py:114
  43.3 1.6 %collective-permute-start.17 = (bf16[64,2048]{1,0:T(8,128)(2,1)S(1)}, bf16[64,2048]{1,0:T(8,128)(2,1)S(1)}, u32[]{:S(2)}, u32[]{:S(2)}) collective-permute-start(bf16[64,2048]{1,0:T(8,128)(2,1)S(1)} %relay.2), channel_id=1, source_target_pairs={{0,2},{2,0},{4,6},{6,4},{8,10},{10,8},{12,14},{14,12},{1,3},{3,1},... | collective-permute-start | bytes 786440 | tf_op jit(solution)/shard_map/ppermute | solution.py:35
  44.9 0.4 turn.4
  45.4 0.5 first_stats.5
  45.9 1.3 %arriving_logits.6 = (bf16[1024,2048]{1,0:T(8,128)(2,1)S(1)}, f32[256,1024]{1,0:T(8,128)S(1)}) custom-call(bf16[64,2048]{1,0:T(8,128)(2,1)S(1)} %collective-permute-done.refs_5_.refs_0_, bf16[64,2048]{1,0:T(8,128)(2,1)S(1)} %collective-permute-done.2.refs_6_.refs_1_, ...), custom_call_target="tpu_custom_call", output_to_operand_aliasing={{0}: (5, {})} | custom-call | flops 1 | bytes 1 | tf_op jit(solution)/shard_map/arriving_logits/pallas_call | solution.py:198
  47.2 0.5 collective-permute-start.22
  48.1 1.3 %arriving_logits.7 = (bf16[1024,2048]{1,0:T(8,128)(2,1)S(1)}, f32[256,1024]{1,0:T(8,128)S(1)}) custom-call(bf16[64,2048]{1,0:T(8,128)(2,1)S(1)} %collective-permute-done.1.refs_8_.refs_0_, bf16[64,2048]{1,0:T(8,128)(2,1)S(1)} %collective-permute-done.3.refs_9_.refs_1_, ...), custom_call_target="tpu_custom_call", output_to_operand_aliasing={{0}: (5, {})} | custom-call | flops 1 | bytes 1 | tf_op jit(solution)/shard_map/arriving_logits/pallas_call | solution.py:198
  49.4 0.4 turn.6
  49.8 0.7 arriving_logits.8
  50.6 0.5 collective-permute-start.20
  51.1 0.7 arriving_logits.9
  52.4 0.5 first_stats.6
  52.8 0.4 collective-permute-done.21.refs_1_
  53.3 0.5 first_stats.7
  54.3 0.4 collective-permute-done.19.refs_1_
  55.1 12.8 %all_to_all.10.all_ref = f32[8,8,640]{2,1,0:T(8,128)S(1)} all-to-all(f32[8,8,640]{2,1,0:T(8,128)S(1)} %get-tuple-element.126), channel_id=1, replica_groups=mesh['groups'=2,'example'=8,'cls'=2] {'example'}, dimensions={0} | all-to-all | bytes 327680 | tf_op jit(solution)/shard_map/all_to_all | solution.py:613
  67.8 1.6 %first_weights.1 = (bf16[1024,1024]{1,0:T(8,128)(2,1)S(1)}, bf16[1024,1024]{1,0:T(8,128)(2,1)S(1)}, f32[8,128]{1,0:T(8,128)S(1)}, f32[8,128]{1,0:T(8,128)S(1)}) custom-call(f32[8,384]{1,0:T(8,128)S(1)} %get-tuple-element.125.own_ref, f32[8,8,640]{2,1,0:T(8,128)S(1)} %all_to_all.10.all_ref, f32[256,1024]{1,0:T(8,128)S(1)} %get-tuple-element.127.refs_0_, ...), custom_call_target="tpu_custom_call" | custom-call | bytes 8388608 | tf_op jit(solution)/shard_map/first_weights/pallas_call | solution.py:382
  69.5 6.2 %update.2 = (f32[2048,512]{1,0:T(8,128)S(1)}, f32[2048,512]{1,0:T(8,128)S(1)}, bf16[2048,512]{1,0:T(8,128)(2,1)S(1)}) custom-call(bf16[2048,1024]{1,0:T(8,128)(2,1)S(1)} %get-tuple-element.113.refs_5_.refs_8_.turned_ref, bf16[2048,1024]{1,0:T(8,128)(2,1)S(1)} %get-tuple-element.114.squares_ref, ...), custom_call_target="tpu_custom_call", output_to_operand_aliasing={{0}: (2, {})} | custom-call | flops 4294967296 | tf_op jit(solution)/shard_map/update/pallas_call | solution.py:418
  75.7 2.3 %next_logits.3.refs_0_ = f32[1024,512]{1,0:T(8,128)S(1)} custom-call(bf16[1024,2048]{1,0:T(8,128)(2,1)S(1)} %get-tuple-element.111.plain_ref, bf16[2048,512]{1,0:T(8,128)(2,1)S(1)} %get-tuple-element.135.low_ref), custom_call_target="tpu_custom_call" | custom-call | flops 2147483648 | tf_op jit(solution)/shard_map/next_logits/pallas_call | solution.py:445
  78.1 6.4 %update.3 = (f32[2048,512]{1,0:T(8,128)S(1)}, f32[2048,512]{1,0:T(8,128)S(1)}, bf16[2048,512]{1,0:T(8,128)(2,1)S(1)}) custom-call(bf16[2048,1024]{1,0:T(8,128)(2,1)S(1)} %get-tuple-element.113.refs_5_.refs_8_.turned_ref, bf16[2048,1024]{1,0:T(8,128)(2,1)S(1)} %get-tuple-element.114.squares_ref, ...), custom_call_target="tpu_custom_call", output_to_operand_aliasing={{0}: (2, {})} | custom-call | flops 4294967296 | tf_op jit(solution)/shard_map/update/pallas_call | solution.py:418
  84.5 1.2 %next_logits.5.refs_1_ = f32[512,512]{1,0:T(8,128)S(1)} custom-call(bf16[1024,2048]{1,0:T(8,128)(2,1)S(1)} %get-tuple-element.111.plain_ref, bf16[2048,512]{1,0:T(8,128)(2,1)S(1)} %get-tuple-element.137.low_ref), custom_call_target="tpu_custom_call" | custom-call | flops 1073741824 | tf_op jit(solution)/shard_map/next_logits/pallas_call | solution.py:445
  85.8 0.6 collective-permute-start.25
  86.3 1.2 %next_logits.4.refs_1_ = f32[512,512]{1,0:T(8,128)S(1)} custom-call(bf16[1024,2048]{1,0:T(8,128)(2,1)S(1)} %get-tuple-element.111.plain_ref, bf16[2048,512]{1,0:T(8,128)(2,1)S(1)} %get-tuple-element.137.low_ref), custom_call_target="tpu_custom_call" | custom-call | flops 1073741824 | tf_op jit(solution)/shard_map/next_logits/pallas_call | solution.py:445
  87.7 1.0 collective-permute-done.25.refs_3_
  88.6 1.7 %last_stats.2 = (f32[512,1024]{1,0:T(8,128)S(1)}, f32[8,384]{1,0:T(8,128)S(1)}) custom-call(f32[1024,512]{1,0:T(8,128)S(1)} %next_logits.3.refs_0_, f32[512,512]{1,0:T(8,128)S(1)} %next_logits.5.refs_1_, f32[1024,512]{1,0:T(8,128)S(1)} %collective-permute-done.23.refs_2_, f32[512,512]{1,0:T(8,128)S(1)} %collective-permute-done.25.refs_3_, ...), custom_call_target="tpu_custom_call" | custom-call | bytes 12582912 | tf_op jit(solution)/shard_map/last_stats/pallas_call | solution.py:512
  90.3 1.7 %last_stats.3 = (f32[512,1024]{1,0:T(8,128)S(1)}, f32[8,384]{1,0:T(8,128)S(1)}, f32[8,8,384]{2,1,0:T(8,128)S(1)}) custom-call(f32[1024,512]{1,0:T(8,128)S(1)} %next_logits.3.refs_0_, f32[512,512]{1,0:T(8,128)S(1)} %next_logits.4.refs_1_, f32[1024,512]{1,0:T(8,128)S(1)} %collective-permute-done.23.refs_2_, f32[512,512]{1,0:T(8,128)S(1)} %collective-permute-done.24.refs_3_, ...), custom_call_target="tpu_custom_call" | custom-call | bytes 12582912 | tf_op jit(solution)/shard_map/last_stats/pallas_call | solution.py:512
  92.0 9.9 %all_to_all.11.all_ref = f32[8,8,384]{2,1,0:T(8,128)S(1)} all-to-all(f32[8,8,384]{2,1,0:T(8,128)S(1)} %get-tuple-element.141), channel_id=1, replica_groups=mesh['groups'=2,'example'=8,'cls'=2] {'example'}, dimensions={0} | all-to-all | bytes 196608 | tf_op jit(solution)/shard_map/all_to_all | solution.py:613
  101.9 6.9 %finish.1 = (f32[2048,1024]{1,0:T(8,128)}, f32[1,128]{1,0:T(1,128)}) custom-call(f32[8,384]{1,0:T(8,128)S(1)} %get-tuple-element.140.own_ref, f32[8,8,384]{2,1,0:T(8,128)S(1)} %all_to_all.11.all_ref, f32[8,128]{1,0:T(8,128)S(1)} %get-tuple-element.138.refs_4_.target_ref, bf16[2048,1024]{1,0:T(8,128)(2,1)S(1)} %get-tuple-element.113.refs_5_.refs_8_.turned_ref, ...), custom_call_target="tpu_custom_call" | custom-call | flops 4294967296 | tf_op jit(solution)/shard_map/finish/pallas_call | solution.py:591
  (37 shorter events, 2.7 us)
Async XLA Ops:
  1.7 12.7 %collective-permute-start = (bf16[64,2048]{1,0:T(8,128)(2,1)S(1)}, bf16[64,2048]{1,0:T(8,128)(2,1)S(1)}, u32[]{:S(2)}, u32[]{:S(2)}) collective-permute-start(bf16[64,2048]{1,0:T(8,128)(2,1)S(1)} %get-tuple-element.151.refs_0_), channel_id=1, source_target_pairs={{0,4},{2,6},{4,12},{6,14},{12,8},{14,10},{8,0},{10,2},{1,5},{3,7},... | collective-permute-start | bytes 786440 | tf_op jit(solution)/shard_map/ppermute | solution.py:100
  4.8 9.7 %collective-permute-start.4 = (bf16[64,2048]{1,0:T(8,128)(2,1)S(1)}, bf16[64,2048]{1,0:T(8,128)(2,1)S(1)}, u32[]{:S(2)}, u32[]{:S(2)}) collective-permute-start(bf16[64,2048]{1,0:T(8,128)(2,1)S(1)} %get-tuple-element.151.refs_0_), channel_id=1, source_target_pairs={{0,2},{2,0},{4,6},{6,4},{8,10},{10,8},{12,14},{14,12},{1,3},{3,1},... | collective-permute-start | bytes 786440 | tf_op jit(solution)/shard_map/ppermute | solution.py:35
  6.3 11.8 %collective-permute-start.2 = (bf16[64,2048]{1,0:T(8,128)(2,1)S(1)}, bf16[64,2048]{1,0:T(8,128)(2,1)S(1)}, u32[]{:S(2)}, u32[]{:S(2)}) collective-permute-start(bf16[64,2048]{1,0:T(8,128)(2,1)S(1)} %get-tuple-element.150.refs_1_), channel_id=1, source_target_pairs={{0,4},{2,6},{4,12},{6,14},{12,8},{14,10},{8,0},{10,2},{1,5},{3,7},... | collective-permute-start | bytes 786440 | tf_op jit(solution)/shard_map/ppermute | solution.py:100
  8.9 10.8 %collective-permute-start.5 = (bf16[64,2048]{1,0:T(8,128)(2,1)S(1)}, bf16[64,2048]{1,0:T(8,128)(2,1)S(1)}, u32[]{:S(2)}, u32[]{:S(2)}) collective-permute-start(bf16[64,2048]{1,0:T(8,128)(2,1)S(1)} %get-tuple-element.150.refs_1_), channel_id=1, source_target_pairs={{0,2},{2,0},{4,6},{6,4},{8,10},{10,8},{12,14},{14,12},{1,3},{3,1},... | collective-permute-start | bytes 786440 | tf_op jit(solution)/shard_map/ppermute | solution.py:35
  14.4 10.8 %collective-permute-start.6 = (bf16[64,2048]{1,0:T(8,128)(2,1)S(1)}, bf16[64,2048]{1,0:T(8,128)(2,1)S(1)}, u32[]{:S(2)}, u32[]{:S(2)}) collective-permute-start(bf16[64,2048]{1,0:T(8,128)(2,1)S(1)} %collective-permute-done.refs_5_.refs_0_), channel_id=1, source_target_pairs={{0,2},{2,0},{4,6},{6,4},{8,10},{10,8},{12,14},{14,12},{1,3},{3,1},... | collective-permute-start | bytes 786440 | tf_op jit(solution)/shard_map/ppermute | solution.py:35
  16.0 10.1 %collective-permute-start.1 = (bf16[64,2048]{1,0:T(8,128)(2,1)S(1)}, bf16[64,2048]{1,0:T(8,128)(2,1)S(1)}, u32[]{:S(2)}, u32[]{:S(2)}) collective-permute-start(bf16[64,2048]{1,0:T(8,128)(2,1)S(1)} %collective-permute-done.refs_5_.refs_0_), channel_id=1, source_target_pairs={{0,4},{2,6},{4,12},{6,14},{12,8},{14,10},{8,0},{10,2},{1,5},{3,7},... | collective-permute-start | bytes 786440 | tf_op jit(solution)/shard_map/ppermute | solution.py:100
  18.1 13.0 %collective-permute-start.3 = (bf16[64,2048]{1,0:T(8,128)(2,1)S(1)}, bf16[64,2048]{1,0:T(8,128)(2,1)S(1)}, u32[]{:S(2)}, u32[]{:S(2)}) collective-permute-start(bf16[64,2048]{1,0:T(8,128)(2,1)S(1)} %collective-permute-done.2.refs_6_.refs_1_), channel_id=1, source_target_pairs={{0,4},{2,6},{4,12},{6,14},{12,8},{14,10},{8,0},{10,2},{1,5},{3,7},... | collective-permute-start | bytes 786440 | tf_op jit(solution)/shard_map/ppermute | solution.py:100
  19.7 11.7 %collective-permute-start.8 = (bf16[64,2048]{1,0:T(8,128)(2,1)S(1)}, bf16[64,2048]{1,0:T(8,128)(2,1)S(1)}, u32[]{:S(2)}, u32[]{:S(2)}) collective-permute-start(bf16[64,2048]{1,0:T(8,128)(2,1)S(1)} %collective-permute-done.2.refs_6_.refs_1_), channel_id=1, source_target_pairs={{0,2},{2,0},{4,6},{6,4},{8,10},{10,8},{12,14},{14,12},{1,3},{3,1},... | collective-permute-start | bytes 786440 | tf_op jit(solution)/shard_map/ppermute | solution.py:35
  26.2 10.3 %collective-permute-start.7 = (bf16[64,2048]{1,0:T(8,128)(2,1)S(1)}, bf16[64,2048]{1,0:T(8,128)(2,1)S(1)}, u32[]{:S(2)}, u32[]{:S(2)}) collective-permute-start(bf16[64,2048]{1,0:T(8,128)(2,1)S(1)} %collective-permute-done.1.refs_8_.refs_0_), channel_id=1, source_target_pairs={{0,2},{2,0},{4,6},{6,4},{8,10},{10,8},{12,14},{14,12},{1,3},{3,1},... | collective-permute-start | bytes 786440 | tf_op jit(solution)/shard_map/ppermute | solution.py:35
  26.8 10.1 %collective-permute-start.14 = (bf16[64,2048]{1,0:T(8,128)(2,1)S(1)}, bf16[64,2048]{1,0:T(8,128)(2,1)S(1)}, u32[]{:S(2)}, u32[]{:S(2)}) collective-permute-start(bf16[64,2048]{1,0:T(8,128)(2,1)S(1)} %collective-permute-done.1.refs_8_.refs_0_), channel_id=1, source_target_pairs={{0,4},{2,6},{4,12},{6,14},{12,8},{14,10},{8,0},{10,2},{1,5},{3,7},... | collective-permute-start | bytes 786440 | tf_op jit(solution)/shard_map/ppermute | solution.py:100
  31.2 9.3 %collective-permute-start.15 = (bf16[64,2048]{1,0:T(8,128)(2,1)S(1)}, bf16[64,2048]{1,0:T(8,128)(2,1)S(1)}, u32[]{:S(2)}, u32[]{:S(2)}) collective-permute-start(bf16[64,2048]{1,0:T(8,128)(2,1)S(1)} %collective-permute-done.3.refs_9_.refs_1_), channel_id=1, source_target_pairs={{0,4},{2,6},{4,12},{6,14},{12,8},{14,10},{8,0},{10,2},{1,5},{3,7},... | collective-permute-start | bytes 786440 | tf_op jit(solution)/shard_map/ppermute | solution.py:100
  31.4 9.3 %collective-permute-start.9 = (bf16[64,2048]{1,0:T(8,128)(2,1)S(1)}, bf16[64,2048]{1,0:T(8,128)(2,1)S(1)}, u32[]{:S(2)}, u32[]{:S(2)}) collective-permute-start(bf16[64,2048]{1,0:T(8,128)(2,1)S(1)} %collective-permute-done.3.refs_9_.refs_1_), channel_id=1, source_target_pairs={{0,2},{2,0},{4,6},{6,4},{8,10},{10,8},{12,14},{14,12},{1,3},{3,1},... | collective-permute-start | bytes 786440 | tf_op jit(solution)/shard_map/ppermute | solution.py:35
  33.0 10.3 %collective-permute-start.10 = (f32[64,1024]{1,0:T(8,128)S(1)}, f32[64,1024]{1,0:T(8,128)S(1)}, u32[]{:S(2)}, u32[]{:S(2)}) collective-permute-start(f32[64,1024]{1,0:T(8,128)S(1)} %get-tuple-element.93.refs_0_), channel_id=1, source_target_pairs={{0,1},{1,0},{2,3},{3,2},{4,5},{5,4},{6,7},{7,6},{8,9},{9,8},{10,11... | collective-permute-start | bytes 786440 | tf_op jit(solution)/shard_map/ppermute | solution.py:35
  36.5 8.8 %collective-permute-start.11 = (f32[64,1024]{1,0:T(8,128)S(1)}, f32[64,1024]{1,0:T(8,128)S(1)}, u32[]{:S(2)}, u32[]{:S(2)}) collective-permute-start(f32[64,1024]{1,0:T(8,128)S(1)} %get-tuple-element.94.refs_1_), channel_id=1, source_target_pairs={{0,1},{1,0},{2,3},{3,2},{4,5},{5,4},{6,7},{7,6},{8,9},{9,8},{10,11... | collective-permute-start | bytes 786440 | tf_op jit(solution)/shard_map/ppermute | solution.py:35
  36.9 8.5 %collective-permute-start.12 = (f32[64,1024]{1,0:T(8,128)S(1)}, f32[64,1024]{1,0:T(8,128)S(1)}, u32[]{:S(2)}, u32[]{:S(2)}) collective-permute-start(f32[64,1024]{1,0:T(8,128)S(1)} %get-tuple-element.95.refs_2_), channel_id=1, source_target_pairs={{0,1},{1,0},{2,3},{3,2},{4,5},{5,4},{6,7},{7,6},{8,9},{9,8},{10,11... | collective-permute-start | bytes 786440 | tf_op jit(solution)/shard_map/ppermute | solution.py:35
  40.4 4.9 %collective-permute-start.13 = (f32[64,1024]{1,0:T(8,128)S(1)}, f32[64,1024]{1,0:T(8,128)S(1)}, u32[]{:S(2)}, u32[]{:S(2)}) collective-permute-start(f32[64,1024]{1,0:T(8,128)S(1)} %get-tuple-element.96.refs_3_), channel_id=1, source_target_pairs={{0,1},{1,0},{2,3},{3,2},{4,5},{5,4},{6,7},{7,6},{8,9},{9,8},{10,11... | collective-permute-start | bytes 786440 | tf_op jit(solution)/shard_map/ppermute | solution.py:35
  40.7 9.9 %collective-permute-start.18 = (bf16[64,2048]{1,0:T(8,128)(2,1)S(1)}, bf16[64,2048]{1,0:T(8,128)(2,1)S(1)}, u32[]{:S(2)}, u32[]{:S(2)}) collective-permute-start(bf16[64,2048]{1,0:T(8,128)(2,1)S(1)} %relay.3), channel_id=1, source_target_pairs={{0,4},{2,6},{4,12},{6,14},{12,8},{14,10},{8,0},{10,2},{1,5},{3,7},... | collective-permute-start | bytes 786440 | tf_op jit(solution)/shard_map/ppermute | solution.py:114
  43.3 7.2 %collective-permute-start.17 = (bf16[64,2048]{1,0:T(8,128)(2,1)S(1)}, bf16[64,2048]{1,0:T(8,128)(2,1)S(1)}, u32[]{:S(2)}, u32[]{:S(2)}) collective-permute-start(bf16[64,2048]{1,0:T(8,128)(2,1)S(1)} %relay.2), channel_id=1, source_target_pairs={{0,2},{2,0},{4,6},{6,4},{8,10},{10,8},{12,14},{14,12},{1,3},{3,1},... | collective-permute-start | bytes 786440 | tf_op jit(solution)/shard_map/ppermute | solution.py:35
  45.3 2.8 %collective-permute-start.16 = (f32[1,128]{1,0:T(1,128)S(1)}, f32[1,128]{1,0:T(1,128)S(1)}, u32[]{:S(2)}, u32[]{:S(2)}) collective-permute-start(f32[1,128]{1,0:T(1,128)S(1)} %get-tuple-element.102.refs_4_), channel_id=1, source_target_pairs={{0,1},{1,0},{2,3},{3,2},{4,5},{5,4},{6,7},{7,6},{8,9},{9,8},{10,11... | collective-permute-start | bytes 1544 | tf_op jit(solution)/shard_map/ppermute | solution.py:35
  47.2 5.2 %collective-permute-start.22 = (f32[256,1024]{1,0:T(8,128)S(1)}, f32[256,1024]{1,0:T(8,128)S(1)}, u32[]{:S(2)}, u32[]{:S(2)}) collective-permute-start(f32[256,1024]{1,0:T(8,128)S(1)} %get-tuple-element.121.refs_0_), channel_id=1, source_target_pairs={{0,1},{1,0},{2,3},{3,2},{4,5},{5,4},{6,7},{7,6},{8,9},{9,8},{10,11... | collective-permute-start | bytes 3145736 | tf_op jit(solution)/shard_map/ppermute | solution.py:35
  50.5 2.7 %collective-permute-start.21 = (f32[256,1024]{1,0:T(8,128)S(1)}, f32[256,1024]{1,0:T(8,128)S(1)}, u32[]{:S(2)}, u32[]{:S(2)}) collective-permute-start(f32[256,1024]{1,0:T(8,128)S(1)} %get-tuple-element.119.refs_0_), channel_id=1, source_target_pairs={{0,1},{1,0},{2,3},{3,2},{4,5},{5,4},{6,7},{7,6},{8,9},{9,8},{10,11... | collective-permute-start | bytes 3145736 | tf_op jit(solution)/shard_map/ppermute | solution.py:35
  50.6 3.4 %collective-permute-start.20 = (f32[128,1024]{1,0:T(8,128)S(1)}, f32[128,1024]{1,0:T(8,128)S(1)}, u32[]{:S(2)}, u32[]{:S(2)}) collective-permute-start(f32[128,1024]{1,0:T(8,128)S(1)} %get-tuple-element.118.refs_0_), channel_id=1, source_target_pairs={{0,1},{1,0},{2,3},{3,2},{4,5},{5,4},{6,7},{7,6},{8,9},{9,8},{10,11... | collective-permute-start | bytes 1572872 | tf_op jit(solution)/shard_map/ppermute | solution.py:35
  51.9 2.9 %collective-permute-start.19 = (f32[128,1024]{1,0:T(8,128)S(1)}, f32[128,1024]{1,0:T(8,128)S(1)}, u32[]{:S(2)}, u32[]{:S(2)}) collective-permute-start(f32[128,1024]{1,0:T(8,128)S(1)} %get-tuple-element.116.refs_4_.refs_0_.refs_7_), channel_id=1, source_target_pairs={{0,1},{1,0},{2,3},{3,2},{4,5},{5,4},{6,7},{7,6},{8,9},{9,8},{10,11... | collective-permute-start | bytes 1572872 | tf_op jit(solution)/shard_map/ppermute | solution.py:35
  78.0 10.6 %collective-permute-start.23 = (f32[1024,512]{1,0:T(8,128)S(1)}, f32[1024,512]{1,0:T(8,128)S(1)}, u32[]{:S(2)}, u32[]{:S(2)}) collective-permute-start(f32[1024,512]{1,0:T(8,128)S(1)} %next_logits.3.refs_0_), channel_id=1, source_target_pairs={{0,1},{1,0},{2,3},{3,2},{4,5},{5,4},{6,7},{7,6},{8,9},{9,8},{10,11... | collective-permute-start | bytes 6291464 | tf_op jit(solution)/shard_map/ppermute | solution.py:35
  85.8 2.8 %collective-permute-start.25 = (f32[512,512]{1,0:T(8,128)S(1)}, f32[512,512]{1,0:T(8,128)S(1)}, u32[]{:S(2)}, u32[]{:S(2)}) collective-permute-start(f32[512,512]{1,0:T(8,128)S(1)} %next_logits.5.refs_1_), channel_id=1, source_target_pairs={{0,1},{1,0},{2,3},{3,2},{4,5},{5,4},{6,7},{7,6},{8,9},{9,8},{10,11... | collective-permute-start | bytes 3145736 | tf_op jit(solution)/shard_map/ppermute | solution.py:35
  87.6 2.7 %collective-permute-start.24 = (f32[512,512]{1,0:T(8,128)S(1)}, f32[512,512]{1,0:T(8,128)S(1)}, u32[]{:S(2)}, u32[]{:S(2)}) collective-permute-start(f32[512,512]{1,0:T(8,128)S(1)} %next_logits.4.refs_1_), channel_id=1, source_target_pairs={{0,1},{1,0},{2,3},{3,2},{4,5},{5,4},{6,7},{7,6},{8,9},{9,8},{10,11... | collective-permute-start | bytes 3145736 | tf_op jit(solution)/shard_map/ppermute | solution.py:35
